TPU v7x, 32 devices: a whole 2x2x4 slice. The times are simulated.
32 devices in a mesh: dp: 8 (over z, y), head: 4 (over x, core).
Axes of the slice: x: 2, y: 2, z: 4, core: 2. Of those that a mesh axis runs over, the one named last changes fastest.
Arguments:
- inputs: bfloat16 [8192, 768], P('dp'), may hold values from -6 to 6
- seg_lengths: int32 [8, 4], P('dp'), may hold values from 1 to 512, 1024 in all within a row
- cotangent: bfloat16 [8192, 768], P('dp'), may hold values from -6 to 6
- qkv_weight: float32 [3, 768, 768], P(None, 'dp', 'head'), may hold values from -0.21875 to 0.21875
- qkv_moment: float32 [3, 768, 768], P(None, 'dp', 'head'), may hold values from -256 to 256
- qkv_average: float32 [3, 768, 768], P(None, 'dp', 'head'), may hold values from -0.21875 to 0.21875
- out_weight: float32 [768, 768], P('head', 'dp'), may hold values from -2 to 2
- out_moment: float32 [768, 768], P('head', 'dp'), may hold values from -32 to 32
- out_average: float32 [768, 768], P('head', 'dp'), may hold values from -2 to 2
- up_weight: float32 [768, 3072], P('dp', 'head'), may hold values from -0.21875 to 0.21875
- up_moment: float32 [768, 3072], P('dp', 'head'), may hold values from -192 to 192
- up_average: float32 [768, 3072], P('dp', 'head'), may hold values from -0.21875 to 0.21875
- down_weight: float32 [3072, 768], P('head', 'dp'), may hold values from -0.109375 to 0.109375
- down_moment: float32 [3072, 768], P('head', 'dp'), may hold values from -224 to 224
- down_average: float32 [3072, 768], P('head', 'dp'), may hold values from -0.109375 to 0.109375
- rel_table: float32 [512, 768], P(('dp', 'head')), may hold values from -6 to 6
- table_moment: float32 [512, 768], P(('dp', 'head')), may hold values from -16 to 16
- table_average: float32 [512, 768], P(('dp', 'head')), may hold values from -6 to 6
- vectors: float32 [11520], P(('dp', 'head')), may hold values from -1.5 to 1.75, as said below
- vector_moment: float32 [11520], P(('dp', 'head')), may hold values from -256 to 256
- vector_average: float32 [11520], P(('dp', 'head')), may hold values from -1.5 to 1.75
Outputs:
- output: bfloat16 [8192, 768], P(('dp', 'head'))
- input_grad: float32 [8192, 768], P(('dp', 'head'))
- qkv_new: float32 [3, 768, 768], P(None, 'dp', 'head')
- qkv_moment_new: float32 [3, 768, 768], P(None, 'dp', 'head')
- qkv_average_new: float32 [3, 768, 768], P(None, 'dp', 'head')
- out_new: float32 [768, 768], P('head', 'dp')
- out_moment_new: float32 [768, 768], P('head', 'dp')
- out_average_new: float32 [768, 768], P('head', 'dp')
- up_new: float32 [768, 3072], P('dp', 'head')
- up_moment_new: float32 [768, 3072], P('dp', 'head')
- up_average_new: float32 [768, 3072], P('dp', 'head')
- down_new: float32 [3072, 768], P('head', 'dp')
- down_moment_new: float32 [3072, 768], P('head', 'dp')
- down_average_new: float32 [3072, 768], P('head', 'dp')
- table_new: float32 [512, 768], P(('dp', 'head'))
- table_moment_new: float32 [512, 768], P(('dp', 'head'))
- table_average_new: float32 [512, 768], P(('dp', 'head'))
- vector_new: float32 [11520], P(('dp', 'head'))
- vector_moment_new: float32 [11520], P(('dp', 'head'))
- vector_average_new: float32 [11520], P(('dp', 'head'))
Inputs may be any that keep to these rules, and one draw needn't show every extreme that they name: `seg_lengths`: each row sums to 1024; each row holds one sequence of exactly 512 tokens. `vectors`: the three gains lie in [0.25, 1.75].
All inputs are finite; a program needn't handle non-finite values.
Results may differ from a plain program's by a relative error of at most 0.02.
Values may be sent and summed in bfloat16 or wider, within the bound.
No kernel may reach another device: no remote copies, remote signals or barrier semaphores. Data moves between devices by JAX's collectives and lax.ppermute only.
A program may use at most 448 MiB of HBM per device.

v0:
```python
import functools
import math

import jax
import jax.numpy as jnp
import numpy as np
from jax import lax
from jax.experimental import pallas as pl
from jax.experimental.pallas import tpu as pltpu
from jax.sharding import PartitionSpec as P

D = 768
HEADS = 12
HD = 64
FF = 3072
BUCKETS = 256
MAXLEN = 512

EPSILON = 1e-07
MOMENTUM = 0.9
DECAY = 0.01
AVERAGE = 0.7
MASKED = -1e30

TILE = 128
NARROW = 5
SCALE = (3.0 * HD) ** -0.5
LOG2E = math.log2(math.e)
HALF = jnp.bfloat16
FULL = jnp.float32
NN = (((1,), (0,)), ((), ()))
NT = (((1,), (1,)), ((), ()))
TN = (((0,), (0,)), ((), ()))


def dot(left, right, dims=NN):
    return lax.dot_general(left, right, dims, preferred_element_type=FULL)


def shear(values, count, low):
    rolled = [
        pltpu.roll(values[:, m * TILE : (m + 1) * TILE], 0, 1, stride=1, stride_axis=0)
        for m in range(count + 1)
    ]
    return jnp.concatenate(
        [jnp.where(low, rolled[m], rolled[m + 1]) for m in range(count)], axis=1
    )


def unshear(values, count, after, shift):
    rolled = [
        pltpu.roll(values[:, m * TILE : (m + 1) * TILE], shift, 1, stride=1, stride_axis=0)
        for m in range(count)
    ]
    zero = jnp.zeros((TILE, TILE), values.dtype)
    return jnp.concatenate(
        [
            jnp.where(
                after, rolled[m] if m < count else zero, rolled[m - 1] if m > 0 else zero
            ).astype(HALF)
            for m in range(count + 1)
        ],
        axis=1,
    )


def flip_matrix():
    across = lax.broadcasted_iota(jnp.int32, (TILE, TILE), 1)
    down = lax.broadcasted_iota(jnp.int32, (TILE, TILE), 0)
    return (across + down == TILE - 1).astype(FULL).astype(HALF)


def tiles_of(block, count=1):
    return pl.ds(pl.multiple_of(block * TILE, TILE), count * TILE)


def sequence_bounds(ends, first, last):
    start, stop = jnp.int32(0), jnp.int32(0)
    begin = jnp.int32(0)
    for end in ends:
        start = jnp.where((begin <= first) & (first < end), begin, start)
        stop = jnp.where((begin <= last) & (last < end), end, stop)
        begin = end
    return start, stop


def by_window(ends, block, tiles, body):
    start, stop = sequence_bounds(ends, block * TILE, block * TILE + TILE - 1)
    first = start // TILE
    narrow = min(NARROW, tiles)
    fits = (stop + TILE - 1) // TILE - first <= narrow

    @pl.when(fits)
    def _():
        body(narrow, jnp.minimum(first, tiles - narrow))

    @pl.when(jnp.logical_not(fits))
    def _():
        body(tiles, jnp.int32(0))


def sequence_ends(info, count):
    ends, total = [], jnp.int32(0)
    for s in range(count):
        total = total + info[s]
        ends.append(total)
    return ends


def sequence_of(places, ends):
    return sum((places >= end).astype(jnp.int32) for end in ends[:-1])


def turned(block, rank, per_owner):
    return ((block // per_owner) ^ rank) * per_owner + block % per_owner


def probs_copy(source, target, sems, block):
    rows = tiles_of(block)
    return pltpu.make_async_copy(source.at[:, rows], target.at[:, rows], sems.at[block])


def forward_kernel(info, qkv_ref, tab_ref, *refs, owners):
    ctx_ref, p_far, q_ref, k_ref, v_ref, qb_ref, kb_ref, p2c_ref, p_ref, sems = refs[-10:]
    heads, tiles = q_ref.shape[0], q_ref.shape[1] // TILE
    segments = info.shape[0] - 1
    rank, per_owner = info[segments], tiles // owners
    ends = sequence_ends(info, segments)
    across = lax.broadcasted_iota(jnp.int32, (TILE, TILE), 1)
    down = lax.broadcasted_iota(jnp.int32, (TILE, TILE), 0)
    low = across < down
    flip = flip_matrix()
    for h in range(heads):
        for i, ref in enumerate((q_ref, k_ref, v_ref)):
            ref[h] = qkv_ref[:, (i * heads + h) * HD : (i * heads + h + 1) * HD]
        for i, ref in enumerate((qb_ref, kb_ref)):
            ref[h] = tab_ref[:, (i * heads + h) * HD : (i * heads + h + 1) * HD]

    def p2c_block(block, carried):
        rows = tiles_of(block)

        def body(count, first):
            offsets = tiles_of(first - block + tiles - 1, count + 1)
            for h in range(heads):
                sheared = shear(dot(k_ref[h, rows, :], qb_ref[h, offsets, :], NT), count, low)
                for m in range(count):
                    p2c_ref[h, tiles_of(first + m), rows] = sheared[
                        :, m * TILE : (m + 1) * TILE
                    ].T

        by_window(ends, block, tiles, body)
        return carried

    lax.fori_loop(0, tiles, p2c_block, 0)

    def score_block(block, carried):
        rows = tiles_of(block)
        row_sequence = sequence_of(down + block * TILE, ends)

        def body(count, first):
            cols = tiles_of(first, count)
            offsets = tiles_of(first - block + tiles - 1, count + 1)
            same = [
                row_sequence == sequence_of(across + (first + m) * TILE, ends) for m in range(count)
            ]
            same = jnp.concatenate(same, axis=1)
            contexts = []
            for h in range(heads):
                query = q_ref[h, rows, :]
                c2p = shear(dot(query, kb_ref[h, offsets, :], NT), count, low)
                raw = dot(query, k_ref[h, cols, :], NT) + c2p + p2c_ref[h, rows, cols]
                scores = jnp.where(same, (SCALE * LOG2E) * raw, MASKED)
                powers = jnp.exp2(scores - jnp.max(scores, axis=1, keepdims=True))
                probs = (powers * (1.0 / jnp.sum(powers, axis=1, keepdims=True))).astype(HALF)
                for m in range(count):
                    p_ref[h, rows, tiles_of(tiles - 1 - first - m)] = dot(
                        probs[:, m * TILE : (m + 1) * TILE], flip
                    ).astype(HALF)
                contexts.append(dot(probs, v_ref[h, cols, :]).astype(HALF))
            ctx_ref[tiles_of(turned(block, rank, per_owner)), :] = jnp.concatenate(contexts, axis=1)

        by_window(ends, block, tiles, body)
        probs_copy(p_ref, p_far, sems, block).start()
        return carried

    lax.fori_loop(0, tiles, score_block, 0)

    def finish(block, carried):
        probs_copy(p_ref, p_far, sems, block).wait()
        return carried

    lax.fori_loop(0, tiles, finish, 0)


def backward_kernel(
    info,
    qkv_ref,
    tab_ref,
    p_far,
    g_ref,
    *refs,
    owners,
):
    dqkv_ref, gtab_ref, q_ref, k_ref, krev_ref, vrev_ref, qbs_ref, kbs_ref = refs[-14:-6]
    grad_ref, dst_ref, dvt_ref, gsum_ref, p_ref, sems = refs[-6:]
    heads, tiles = q_ref.shape[0], q_ref.shape[1] // TILE
    width = heads * HD
    segments = info.shape[0] - 1
    rank, per_owner = info[segments], tiles // owners
    ends = sequence_ends(info, segments)
    across = lax.broadcasted_iota(jnp.int32, (TILE, TILE), 1)
    down = lax.broadcasted_iota(jnp.int32, (TILE, TILE), 0)
    flip = flip_matrix()

    def begin(block, carried):
        probs_copy(p_far, p_ref, sems, block).start()
        return carried

    lax.fori_loop(0, tiles, begin, 0)
    dst_ref[...] = jnp.zeros_like(dst_ref)
    dvt_ref[...] = jnp.zeros_like(dvt_ref)
    gsum_ref[...] = jnp.zeros_like(gsum_ref)
    for h in range(heads):
        q_ref[h] = qkv_ref[:, h * HD : (h + 1) * HD]
        k_ref[h] = qkv_ref[:, width + h * HD : width + (h + 1) * HD]
        qbs_ref[h] = tab_ref[:, h * HD : (h + 1) * HD]
        grad_ref[h] = g_ref[:, h * HD : (h + 1) * HD]
    for m in range(tiles):
        here, there = slice(m * TILE, (m + 1) * TILE), slice((tiles - 1 - m) * TILE, (tiles - m) * TILE)
        turned_rows = dot(flip, qkv_ref[here, width:]).astype(HALF)
        for h in range(heads):
            krev_ref[h, there, :] = turned_rows[:, h * HD : (h + 1) * HD]
            vrev_ref[h, there, :] = turned_rows[:, width + h * HD : width + (h + 1) * HD]
    for m in range(2 * tiles):
        here = slice(m * TILE, (m + 1) * TILE)
        there = slice((2 * tiles - 1 - m) * TILE, (2 * tiles - m) * TILE)
        turned_rows = dot(flip, tab_ref[here, width:]).astype(HALF)
        for h in range(heads):
            kbs_ref[h, there, :] = turned_rows[:, h * HD : (h + 1) * HD]

    def query_block(block, carried):
        rows = tiles_of(block)
        probs_copy(p_far, p_ref, sems, block).wait()

        def body(count, first):
            start = tiles - first - count
            cols = tiles_of(start, count)
            offsets = tiles_of(block + start, count + 1)
            grads = []
            for h in range(heads):
                grad = grad_ref[h, tiles_of(turned(block, rank, per_owner)), :]
                probs_low = p_ref[h, rows, cols]
                probs = probs_low.astype(FULL)
                grad_probs = dot(grad, vrev_ref[h, cols, :], NT)
                inner = jnp.sum(probs * grad_probs, axis=1, keepdims=True)
                grad_raw = (probs * (grad_probs - inner)) * SCALE
                by_offset = unshear(grad_raw, count, across >= down, 0)
                grads.append(
                    (
                        dot(grad_raw.astype(HALF), krev_ref[h, cols, :])
                        + dot(by_offset, kbs_ref[h, offsets, :])
                    ).astype(HALF)
                )
                gsum_ref[heads + h, :, offsets] += dot(
                    q_ref[h, rows, :].astype(FULL).T.astype(HALF), by_offset
                )
                dvt_ref[h, :, cols] += dot(grad.astype(FULL).T.astype(HALF), probs_low)
                for m in range(count):
                    dst_ref[h, tiles_of(start + m), rows] = grad_raw[
                        :, m * TILE : (m + 1) * TILE
                    ].T
            dqkv_ref[rows, :width] = jnp.concatenate(grads, axis=1)

        by_window(ends, block, tiles, body)
        return carried

    lax.fori_loop(0, tiles, query_block, 0)

    def key_block(block, carried):
        rows, back = tiles_of(block), tiles_of(tiles - 1 - block)

        def body(count, first):
            cols = tiles_of(first, count)
            offsets = tiles_of(tiles - 1 - block + first, count + 1)
            grads = []
            for h in range(heads):
                grad_raw = dst_ref[h, back, cols]
                by_offset = unshear(grad_raw, count, across > down, 1)
                grads.append(
                    (
                        dot(grad_raw.astype(HALF), q_ref[h, cols, :])
                        + dot(by_offset, qbs_ref[h, offsets, :])
                    ).astype(HALF)
                )
                gsum_ref[h, :, offsets] += dot(
                    krev_ref[h, back, :].astype(FULL).T.astype(HALF), by_offset
                )
            grads += [dvt_ref[h, :, back].T.astype(HALF) for h in range(heads)]
            dqkv_ref[rows, width:] = dot(flip, jnp.concatenate(grads, axis=1)).astype(HALF)

        by_window(ends, block, tiles, body)
        return carried

    lax.fori_loop(0, tiles, key_block, 0)
    for i in range(heads):
        gtab_ref[i * HD : (i + 1) * HD, :] = gsum_ref[i].astype(HALF)
        for m in range(2 * tiles):
            there = slice((2 * tiles - 1 - m) * TILE, (2 * tiles - m) * TILE)
            gtab_ref[width + i * HD : width + (i + 1) * HD, there] = dot(
                gsum_ref[heads + i, :, m * TILE : (m + 1) * TILE].astype(HALF), flip
            ).astype(HALF)


SMEM_SPEC = pl.BlockSpec(memory_space=pltpu.SMEM)
VMEM_SPEC = pl.BlockSpec(memory_space=pltpu.VMEM)
ANY_SPEC = pl.BlockSpec(memory_space=pl.ANY)


def kernel_cost(microseconds):
    return pl.CostEstimate(
        flops=int(microseconds * 1e9), bytes_accessed=int(microseconds * 1e6), transcendentals=0
    )


def attention_forward(info, qkv, tables, owners, before):
    rows, heads = qkv.shape[0], qkv.shape[1] // (3 * HD)
    small, wide = pltpu.VMEM((heads, rows, HD), HALF), pltpu.VMEM((heads, 2 * rows, HD), HALF)
    return pl.pallas_call(
        functools.partial(forward_kernel, owners=owners),
        out_shape=(
            jax.ShapeDtypeStruct((rows, heads * HD), HALF),
            jax.ShapeDtypeStruct((heads, rows, rows), HALF),
        ),
        in_specs=[SMEM_SPEC] + [VMEM_SPEC] * 2 + [ANY_SPEC] * len(before),
        out_specs=(VMEM_SPEC, ANY_SPEC),
        scratch_shapes=[small] * 3
        + [wide] * 2
        + [
            pltpu.VMEM((heads, rows, rows), FULL),
            pltpu.VMEM((heads, rows, rows), HALF),
            pltpu.SemaphoreType.DMA((rows // TILE,)),
        ],
        compiler_params=pltpu.CompilerParams(vmem_limit_bytes=48 * 2**20),
        cost_estimate=kernel_cost(30),
    )(info, qkv, tables, *before)


def attention_backward(info, qkv, tables, probs, grad, owners, before):
    rows, heads = qkv.shape[0], qkv.shape[1] // (3 * HD)
    shape = jax.ShapeDtypeStruct
    small, wide = pltpu.VMEM((heads, rows, HD), HALF), pltpu.VMEM((heads, 2 * rows, HD), HALF)
    return pl.pallas_call(
        functools.partial(backward_kernel, owners=owners),
        out_shape=(shape(qkv.shape, HALF), shape((2 * heads * HD, 2 * rows), HALF)),
        in_specs=[SMEM_SPEC] + [VMEM_SPEC] * 2
        + [ANY_SPEC, VMEM_SPEC]
        + [ANY_SPEC] * len(before),
        out_specs=(VMEM_SPEC,) * 2,
        scratch_shapes=[small] * 4
        + [wide] * 2
        + [
            small,
            pltpu.VMEM((heads, rows, rows), FULL),
            pltpu.VMEM((heads, HD, rows), FULL),
            pltpu.VMEM((2 * heads, HD, 2 * rows), FULL),
            pltpu.VMEM((heads, rows, rows), HALF),
            pltpu.SemaphoreType.DMA((rows // TILE,)),
        ],
        compiler_params=pltpu.CompilerParams(vmem_limit_bytes=52 * 2**20),
        cost_estimate=kernel_cost(34),
    )(info, qkv, tables, probs, grad, *before)


def standardise(values):
    center = values - jnp.mean(values, axis=-1, keepdims=True)
    spread = jnp.mean(center * center, axis=-1, keepdims=True)
    inverse = lax.rsqrt(spread + EPSILON)
    return center * inverse, inverse


def standardise_back(grad, unit, inverse):
    return inverse * (
        grad
        - jnp.mean(grad, axis=-1, keepdims=True)
        - unit * jnp.mean(grad * unit, axis=-1, keepdims=True)
    )


def exact_dot(values, order, dims):
    high = values.astype(HALF)
    rest = values - high.astype(FULL)
    middle = rest.astype(HALF)
    last = (rest - middle.astype(FULL)).astype(HALF)
    return dot(high, order, dims) + dot(middle, order, dims) + dot(last, order, dims)


def turn(values):
    return values.astype(FULL).T.astype(HALF)


def middle_kernel(info, x_ref, cot_ref, order_ref, vec_ref, bias_ref, *refs):
    heads = bias_ref.shape[0]
    ctx, up_far, down_far = refs[:heads], refs[heads : heads + 8], refs[heads + 8 : heads + 12]
    half, chunk = up_far[0].shape[0], down_far[0].shape[1]
    refs = refs[len(refs) - heads - 16 :]
    out_ref, pre_ref, sums_ref, grad_bias_ref = refs[:4]
    grad_ctx = refs[4 : heads + 4]
    up_keep, up_send, down_keep, down_send = refs[heads + 4 : heads + 8]
    slope_ref, hidden_ref, up, down, grad_up, grad_down, sems_in, sems_out = refs[heads + 8 :]
    wide = bias_ref.shape[1]
    arrivals = [
        [
            pltpu.make_async_copy(
                up_far[4 * (o % 2) + 2 * (o // 2) + i].at[:, lanes],
                up.at[o, i * half : (i + 1) * half, lanes],
                sems_in.at[2 * j + i, o],
            )
            for o in range(heads)
        ]
        for j, lanes in enumerate((slice(wide, up.shape[2]), slice(0, wide)))
        for i in range(2)
    ]
    arrivals += [
        [
            pltpu.make_async_copy(
                down_far[2 * (o % 2) + i % 2].at[2 * (o // 2) + i // 2],
                down.at[o, i * chunk : (i + 1) * chunk],
                sems_in.at[4 + i, o],
            )
            for o in range(heads)
        ]
        for i in range(4)
    ]
    for copies in arrivals[:2]:
        for copy in copies:
            copy.start()
    for o in range(heads):
        for copies in arrivals[2:]:
            copies[o].start()
    departures = []

    def depart(i, o):
        near, keep, send = ((grad_up, up_keep, up_send), (grad_down, down_keep, down_send))[i > 1]
        lanes = (slice(0, wide), slice(wide, grad_up.shape[2]), slice(0, wide))[i]
        copy = pltpu.make_async_copy(
            near.at[o, :, lanes],
            (send if o % 2 else keep).at[o // 2, :, lanes],
            sems_out.at[i, o],
        )
        copy.start()
        departures.append(copy)

    rank = info[info.shape[0] - 1]
    wide = bias_ref.shape[1]
    span = ctx[0].shape[1]
    order = order_ref[...]
    vec = exact_dot(vec_ref[...], order, NT)
    gain1, bias1, gain2, bias2, bias_out, bias_down = (vec[i : i + 1] for i in range(6))

    pre_first = dot(x_ref[...], order, NT) + bias_out
    for o in range(heads):
        arrivals[0][o].wait()
        arrivals[1][o].wait()
        pre_first = pre_first + dot(ctx[o][...], up[o, :, wide : wide + span], NT)
    unit_first, inverse_first = standardise(pre_first)
    first = unit_first * gain1 + bias1
    first_low = first.astype(HALF)
    total = first + bias_down
    for o in range(heads):
        arrivals[2][o].wait()
        arrivals[3][o].wait()
        values = dot(first_low, up[o, :, :wide]) + bias_ref[pl.ds(rank ^ o, 1), :]
        below = 0.5 + 0.5 * lax.erf(values * math.sqrt(0.5))
        hidden = (values * below).astype(HALF)
        hidden_ref[o] = hidden
        slope_ref[o] = below + values * (
            jnp.exp2(values * values * (-0.5 * LOG2E)) * (1.0 / math.sqrt(2.0 * math.pi))
        )
        for copies in arrivals[4:]:
            copies[o].wait()
        total = total + dot(hidden, down[o], NT)
    unit_second, inverse_second = standardise(total)
    out_ref[...] = dot((unit_second * gain2 + bias2).astype(HALF), order).astype(HALF)

    grad_out = dot(cot_ref[...], order, NT)
    grad_second = standardise_back(grad_out * gain2, unit_second, inverse_second)
    grad_down_low = grad_second.astype(HALF)
    grad_down_turned, first_turned = turn(grad_down_low), turn(first_low)
    grad_first = grad_second
    for o in range(heads):
        grad_down[o] = dot(grad_down_turned, hidden_ref[o]).astype(HALF)
        depart(2, o)
        grad_values = (slope_ref[o] * dot(grad_down_low, down[o])).astype(HALF)
        grad_bias_ref[pl.ds(rank ^ o, 1), :] = jnp.sum(
            grad_values.astype(FULL), axis=0, keepdims=True
        )
        grad_up[o, :, :wide] = dot(first_turned, grad_values).astype(HALF)
        depart(0, o)
        grad_first = grad_first + dot(grad_values, up[o, :, :wide], NT)
    grad_pre = standardise_back(grad_first * gain1, unit_first, inverse_first)
    grad_low = grad_pre.astype(HALF)
    grad_turned = turn(grad_low)
    for o in range(heads):
        grad_ctx[o][...] = dot(grad_low, up[o, :, wide : wide + span]).astype(HALF)
        grad_up[o, :, wide : wide + span] = dot(grad_turned, ctx[o][...]).astype(HALF)
        if wide + span < up.shape[2]:
            grad_up[o, :, wide + span :] = jnp.zeros((up.shape[1], up.shape[2] - wide - span), HALF)
        depart(1, o)
    pre_ref[...] = exact_dot(grad_pre, order, NN)
    sums = [
        jnp.sum(part, axis=0, keepdims=True)
        for part in (
            grad_first * unit_first,
            grad_first,
            grad_out * unit_second,
            grad_out,
            grad_pre,
            grad_second,
        )
    ]
    sums_ref[...] = exact_dot(jnp.concatenate(sums + [jnp.zeros_like(sums[0])] * 2, axis=0), order, NN)
    for copy in departures:
        copy.wait()


def middle(info, x, cot, order, vec, bias, ctx, up, down, before):
    heads, (rows, width), wide = len(ctx), x.shape, bias.shape[1]
    up_shape, down_shape = (width, up[0].shape[1]), (width, wide)
    shape = jax.ShapeDtypeStruct
    results = pl.pallas_call(
        middle_kernel,
        out_shape=(
            shape((rows, width), HALF),
            shape((rows, width), FULL),
            shape(vec.shape, FULL),
            shape(bias.shape, FULL),
        )
        + tuple(shape(c.shape, HALF) for c in ctx)
        + tuple(shape((heads // 2,) + w, HALF) for w in (up_shape, up_shape, down_shape, down_shape)),
        in_specs=[SMEM_SPEC] + [VMEM_SPEC] * (5 + heads) + [ANY_SPEC] * (12 + len(before)),
        out_specs=(VMEM_SPEC,) * (4 + heads) + (ANY_SPEC,) * 4,
        scratch_shapes=[pltpu.VMEM((heads, rows, wide), FULL), pltpu.VMEM((heads, rows, wide), HALF)]
        + [pltpu.VMEM((heads,) + w, HALF) for w in (up_shape, down_shape, up_shape, down_shape)]
        + [pltpu.SemaphoreType.DMA((8, heads))] * 2,
        compiler_params=pltpu.CompilerParams(vmem_limit_bytes=48 * 2**20),
        cost_estimate=kernel_cost(20),
    )(info, x, cot, order, vec, bias, *ctx, *up, *down, *before)
    return results[:4] + (results[4 : 4 + heads],) + results[4 + heads :]


def by_row(parts, count):
    row = lax.broadcasted_iota(jnp.int32, (count, parts[0].shape[1]), 0)
    total = jnp.zeros(row.shape, FULL)
    for i, part in enumerate(parts):
        total = jnp.where(row == i, part, total)
    return total


def tail_kernel(
    info,
    dqkv_ref,
    offsets_ref,
    w_ref,
    inputs_ref,
    normed_ref,
    unit_ref,
    selector_ref,
    order_ref,
    norm_sums_ref,
    bias_up_ref,
    *refs,
):
    qkv_keep, qkv_send, parts_ref, normed_grad_ref, vector_ref = refs[-5:]
    rank = info[info.shape[0] - 1]
    width = dqkv_ref.shape[1] // 3
    owners, quarter = parts_ref.shape[:2]
    tables = dot(selector_ref[...], offsets_ref[...], NT).astype(HALF)
    turned_tables = dot(order_ref[...], tables).astype(HALF)
    weights = w_ref[...]
    grad_normed = dot(turned_tables, weights[:, : 2 * width], NT)
    normed_grad_ref[...] = grad_normed.astype(HALF)
    grads = dqkv_ref[...]
    grad_qkv = dot(inputs_ref[...], grads)
    grad_qkv = jnp.concatenate(
        [
            grad_qkv[:, : 2 * width] + dot(normed_ref[...], turned_tables),
            grad_qkv[:, 2 * width :],
        ],
        axis=1,
    ).astype(HALF)
    half = qkv_keep.shape[0]
    for i, ref in enumerate((qkv_keep, qkv_send)):
        ref[:, : 3 * width] = grad_qkv[i * half : (i + 1) * half]
        if 3 * width < ref.shape[1]:
            ref[:, 3 * width :] = jnp.zeros((half, ref.shape[1] - 3 * width), HALF)
    for o in range(owners):
        apart = rank ^ o
        parts_ref[(apart % 2) * (owners // 2) + apart // 2] = dot(
            dqkv_ref[o * quarter : (o + 1) * quarter, :], weights, NT
        ).astype(HALF)
    sums = jnp.sum(grads.astype(FULL), axis=0, keepdims=True)
    table_sums = jnp.sum(turned_tables.astype(FULL), axis=0, keepdims=True)
    sums = jnp.concatenate([sums[:, : 2 * width] + table_sums, sums[:, 2 * width :]], axis=1)
    sums = by_row([sums[:, i * width : (i + 1) * width] for i in range(3)], 8)
    places = (
        lax.broadcasted_iota(jnp.int32, (width, D), 1)
        == lax.broadcasted_iota(jnp.int32, (width, D), 0) + rank * width
    ).astype(FULL).astype(HALF)
    placed = exact_dot(sums, places, NN)
    norm_sums, bias_up = norm_sums_ref[...], bias_up_ref[...]
    parts = [norm_sums[i : i + 1] for i in range(4)]
    parts.append(jnp.sum(grad_normed * unit_ref[...].astype(FULL), axis=0, keepdims=True))
    parts.append(jnp.sum(grad_normed, axis=0, keepdims=True))
    parts += [norm_sums[i : i + 1] for i in range(4, 6)]
    parts += [placed[i : i + 1] for i in range(3)]
    parts += [bias_up[i : i + 1] for i in range(bias_up.shape[0])]
    vector_ref[...] = by_row(parts, vector_ref.shape[0])


def tail(
    info, dqkv, offsets, weights, inputs, normed, unit, selector, order, norm_sums, bias_up,
    owners, lanes, before,
):
    rows, shape = dqkv.shape[0], jax.ShapeDtypeStruct
    return pl.pallas_call(
        tail_kernel,
        out_shape=(
            shape((D // 2, lanes), HALF),
            shape((D // 2, lanes), HALF),
            shape((owners, rows // owners, D), HALF),
            shape(normed.shape[::-1], HALF),
            shape((-(-(11 + bias_up.shape[0]) // 8) * 8, D), FULL),
        ),
        in_specs=[SMEM_SPEC] + [VMEM_SPEC] * 10 + [ANY_SPEC] * len(before),
        out_specs=(VMEM_SPEC,) * 5,
        compiler_params=pltpu.CompilerParams(vmem_limit_bytes=40 * 2**20),
        cost_estimate=kernel_cost(0.1),
    )(info, dqkv, offsets, weights, inputs, normed, unit, selector, order, norm_sums, bias_up, *before)


def index_steps(axis):
    size = lax.axis_size(axis)
    steps, bit = [], size // 2
    while bit >= 1:
        steps.append((axis, bit))
        bit //= 2
    return steps


def swap(values, step):
    axis, bit = step
    return lax.ppermute(values, axis, [(i, i ^ bit) for i in range(lax.axis_size(axis))])


def after(values, *others):
    return lax.optimization_barrier((values,) + others)[0]


def swap_both(values, one, other):
    (axis, bit), (along, place) = one, other
    width = lax.axis_size(along)
    count = lax.axis_size(axis) * width
    return lax.ppermute(
        values, (axis, along), [(i, i ^ (bit * width) ^ place) for i in range(count)]
    )


def gather_blocks(values, steps, layout):
    taken = []
    for step in steps:
        place = sum(1 for other in taken if layout.index(other) < layout.index(step))
        taken.append(step)
        other = swap(values, step)
        values = jnp.concatenate(
            [jnp.expand_dims(values, place), jnp.expand_dims(other, place)], axis=place
        )
    return values


def gather_rows(values, steps):
    for step in steps:
        values = jnp.concatenate([values, swap(values, step)], axis=0)
    return values


def scatter_rows(values, steps):
    kind = values.dtype
    for i, step in enumerate(steps):
        half = values.shape[0] // 2
        values = values[:half].astype(FULL) + swap(values[half:], step).astype(FULL)
        if i < len(steps) - 1:
            values = values.astype(kind)
    return values


def add(*parts):
    return sum(part.astype(FULL) for part in parts).astype(HALF)


def block_owner(rank, steps, axis):
    places = np.arange(2 ** len(steps))
    offsets = sum(
        ((places >> i) & 1) * bit for i, (along, bit) in enumerate(steps) if along == axis
    )
    return jnp.asarray(offsets, jnp.int32) ^ rank


def one_hot(owners, per_block):
    own = (owners[:, None] * per_block + jnp.arange(per_block, dtype=jnp.int32)[None, :]).reshape(-1)
    return (own[:, None] == jnp.arange(own.shape[0], dtype=jnp.int32)[None, :]).astype(HALF)


def bucket_of(offset, buckets, longest):
    middle = buckets // 2
    distance = middle - 1 if abs(offset) < middle else abs(offset)
    sign_of = 1 if offset > 0 else -1 if offset < 0 else 0
    far_bucket = (
        math.ceil(math.log(distance / middle) / math.log((longest - 1) / middle) * (middle - 1))
        + middle
    )
    bucket = offset if distance <= middle else sign_of * far_bucket
    return min(max(bucket + buckets, 0), 2 * buckets - 1)


def offset_selector():
    selector = np.zeros((4 * MAXLEN, 2 * BUCKETS), dtype=np.float32)
    for offset in range(1 - MAXLEN, MAXLEN):
        selector[offset + 2 * MAXLEN - 1, bucket_of(offset, BUCKETS, MAXLEN)] = 1.0
    return selector


def nesterov(weight, moment, average, gradient, step_rate):
    decayed = gradient + DECAY * weight
    moment_new = MOMENTUM * moment + decayed
    weight_new = weight - step_rate * (decayed + MOMENTUM * moment_new)
    average_new = AVERAGE * average + (1.0 - AVERAGE) * weight_new
    return (weight_new, moment_new, average_new)


def column_sums(matrix):
    return jnp.sum(matrix, axis=0, dtype=FULL)


def per_device(
    inputs,
    seg_lengths,
    cotangent,
    qkv_weight,
    qkv_moment,
    qkv_average,
    out_weight,
    out_moment,
    out_average,
    up_weight,
    up_moment,
    up_average,
    down_weight,
    down_moment,
    down_average,
    rel_table,
    table_moment,
    table_average,
    vectors,
    vector_moment,
    vector_average,
):
    tok_rows = inputs.shape[0]
    head_count = lax.axis_size("head")
    dp_count = lax.axis_size("dp")
    head_rank = lax.axis_index("head")
    dp_rank = lax.axis_index("dp")
    local_heads = HEADS // head_count
    local_width = local_heads * HD
    quarter = tok_rows // head_count
    total_tokens = tok_rows * dp_count
    up_local = up_weight.shape[1]
    dp_steps, head_steps = index_steps("dp"), index_steps("head")
    device_count = dp_count * head_count

    width_order = one_hot(block_owner(dp_rank, dp_steps, "dp"), D // dp_count)
    inputs_across = dot(width_order, inputs, NT).astype(HALF)
    qkv_span = 3 * local_width
    qkv_lanes = -(-qkv_span // 128) * 128
    w_qkv_own = jnp.pad(
        jnp.concatenate([qkv_weight[i].astype(HALF) for i in range(3)], axis=1),
        ((0, 0), (0, qkv_lanes - qkv_span)),
    )
    unit_own, inverse_own = standardise(rel_table)
    vec_rows = vectors.shape[0]
    table_part = rel_table.shape[0]
    vec_high = vectors.astype(HALF)
    vec_low = (vectors - vec_high.astype(FULL)).astype(HALF)
    vec_lanes = -(-2 * vec_rows // table_part // 128) * 128
    vec_pack = jnp.pad(
        jnp.concatenate([vec_high, vec_low]), (0, table_part * vec_lanes - 2 * vec_rows)
    ).reshape(table_part, vec_lanes)
    small = jnp.concatenate([unit_own.astype(HALF), vec_pack], axis=1)
    small_steps = dp_steps + head_steps
    both_first = gather_rows(w_qkv_own, dp_steps[:1])
    small = gather_rows(small, small_steps)
    inputs_own, cotangent_own = (
        lax.dynamic_slice_in_dim(values, head_rank * quarter, quarter, 0)
        for values in (inputs, cotangent)
    )
    both_first = after(both_first, inputs_across, inputs_own, cotangent_own)
    both_more = gather_rows(both_first, dp_steps[1:-1])
    both_last = swap(both_more, dp_steps[-1])
    w_qkv_turned = jnp.concatenate([both_more, both_last])[:, :qkv_span]
    owner = block_owner(dp_rank, small_steps, "dp") * head_count + block_owner(
        head_rank, small_steps, "head"
    )
    unit_table = small[:, :D]
    vec_used = -(-2 * vec_rows // vec_lanes)
    vec_all = (
        small[:, D:]
        .reshape(device_count, table_part, vec_lanes)[:, :vec_used]
        .reshape(device_count, vec_used * vec_lanes)
    )
    vec_all = dot(one_hot(owner, 1), vec_all, TN)
    vector_full = (vec_all[:, :vec_rows] + vec_all[:, vec_rows : 2 * vec_rows]).reshape(-1)
    vector_rows = vector_full[: 11 * D].reshape(11, D)

    far, core, low, mid = head_steps[0], head_steps[1], dp_steps[-1], dp_steps[-2]
    half = D // 2
    wide_lanes = -(-(up_local + local_width) // 256) * 256
    up_out_own = jnp.pad(
        jnp.concatenate([up_weight, out_weight.T], axis=1).astype(HALF),
        ((0, 0), (0, wide_lanes - up_local - local_width)),
    )
    up_near = gather_rows(up_out_own, dp_steps[:-1])
    up_blocks = [up_near, swap(up_near, low), swap(up_near, far), swap_both(up_near, low, far)]
    up_near_core = swap(up_near, core)
    down_one = gather_rows(after(down_weight.T.astype(HALF), both_first), dp_steps[:-2])
    down_near = jnp.stack(
        [down_one, swap(down_one, low), swap(down_one, far), swap_both(down_one, low, far)]
    )
    down_far = swap(down_near, mid)
    down_near_core = swap(down_near, core)
    differences = list(range(head_count))

    table_order = one_hot(owner, table_part)
    w_qkv = dot(width_order, w_qkv_turned, TN).astype(HALF)

    def head_part(row_values):
        return lax.dynamic_slice_in_dim(row_values, head_rank * local_width, local_width)

    bias_qkv = jnp.concatenate([head_part(vector_rows[8 + i]) for i in range(3)])
    normed = (unit_table.astype(FULL) * vector_rows[4] + vector_rows[5]).astype(HALF)
    normed_across = dot(width_order, normed, NT).astype(HALF)
    tables = (dot(normed, w_qkv[:, : 2 * local_width]) + bias_qkv[: 2 * local_width]).astype(HALF)
    tables = dot(table_order, tables, TN).astype(HALF)
    selector = offset_selector()[::-1]
    by_offset = dot(jnp.asarray(selector, dtype=HALF), tables).astype(HALF)
    qkv = (dot(inputs, w_qkv) + bias_qkv).astype(HALF)
    info = jnp.concatenate([seg_lengths[0], head_rank[None].astype(jnp.int32)])
    context, probs = attention_forward(info, qkv, by_offset, head_count, (up_near, down_near, unit_table))
    context, up_near_core, down_near_core = lax.optimization_barrier(
        (context, up_near_core, down_near_core)
    )
    def exchange(blocks):
        return {
            o: swap(block, ("head", o)) if o else block for o, block in blocks.items()
        }

    context_low = exchange({o: context[o * quarter : (o + 1) * quarter] for o in differences})
    *up_rest, down_far, _ = lax.optimization_barrier((*up_blocks[1:], down_far, tuple(context_low.values())))
    up_blocks = [up_near] + up_rest + [up_near_core] + [swap(block, core) for block in up_rest]
    down_blocks = [down_near, down_far, down_near_core, swap(down_far, core)]

    vec = jnp.concatenate([vector_rows[:4], vector_rows[6:8], vector_rows[:2]], axis=0)
    bias_up = vector_full[11 * D :].reshape(head_count, up_local)
    output, grad_pre_first, norm_sums, grad_bias_up, grad_context, *weight_grads = middle(
        info,
        inputs_own,
        cotangent_own,
        width_order,
        vec,
        bias_up,
        [context_low[o] for o in differences],
        up_blocks,
        down_blocks,
        (normed_across, table_order),
    )

    def fold(blocks, step):
        bit = step[1]
        return {
            o: (block.astype(FULL) + swap(blocks[o ^ bit], step).astype(FULL)).astype(HALF)
            for o, block in blocks.items()
            if not o & bit
        }

    up_keep, up_send, down_keep, down_send = weight_grads
    grad_context = exchange(dict(zip(differences, grad_context)))
    grad_context = jnp.concatenate([grad_context[o] for o in differences], axis=0)
    up_got, down_got, _ = lax.optimization_barrier(
        (swap(up_send, core), swap(down_send, core), grad_context)
    )
    lower, upper = slice(0, half), slice(half, D)
    up_stays, up_low, up_far, up_both = (
        (up_keep[i, rows], up_got[i, rows])
        for i, rows in ((0, lower), (0, upper), (1, lower), (1, upper))
    )
    up_low, up_far, up_both = add(*up_low), add(*up_far), add(*up_both)
    down_keep, down_got = (
        values.reshape(2, 2, 2, D // 4, up_local) for values in (down_keep, down_got)
    )
    down_leaves = add(down_keep[:, :, 1], down_got[:, :, 1])
    grad_qkv_low, grad_offsets = attention_backward(
        info,
        qkv,
        by_offset,
        probs,
        grad_context,
        head_count,
        (up_low, up_far, up_both, down_leaves),
    )
    *up_got, down_got_mid, _ = lax.optimization_barrier(
        (
            swap(up_low, low),
            swap(up_far, far),
            swap_both(up_both, low, far),
            swap(down_leaves, mid),
            grad_qkv_low,
        )
    )
    up_next = add(*up_stays, *up_got)
    down_stays, down_low, down_far, down_both = (
        add(down_keep[i, j, 0], down_got[i, j, 0], down_got_mid[i, j])
        for i, j in ((0, 0), (0, 1), (1, 0), (1, 1))
    )
    qkv_keep, qkv_send, input_parts, grad_normed, grad_vector = tail(
        info,
        grad_qkv_low,
        grad_offsets,
        w_qkv,
        inputs_across,
        normed_across,
        unit_table,
        jnp.asarray(selector.T, dtype=HALF),
        table_order,
        norm_sums,
        grad_bias_up,
        head_count,
        qkv_lanes,
        (up_next, down_low, down_far, down_both),
    )
    up_next = scatter_rows(up_next, dp_steps[1:-1][::-1]).astype(HALF)
    down_next = add(
        down_stays, swap(down_low, low), swap(down_far, far), swap_both(down_both, low, far)
    )
    down_next = scatter_rows(down_next, dp_steps[1:-2][::-1]).astype(HALF)
    qkv_first = add(qkv_keep, swap(qkv_send, low))
    qkv_shard = scatter_rows(qkv_first, dp_steps[:-1][::-1])
    input_both = scatter_rows(input_parts, head_steps[-1:]).astype(HALF)
    input_grad = grad_pre_first + scatter_rows(input_both, head_steps[:-1][::-1])[0]

    vec_lanes = -(-vec_rows // 128) * 128
    grad_vector = jnp.pad(
        grad_vector.reshape(-1)[: device_count * vec_rows].reshape(device_count, vec_rows),
        ((0, 0), (0, vec_lanes - vec_rows)),
    )
    grad_vector = dot(one_hot(owner, 1), grad_vector.astype(HALF)).astype(HALF)
    spare = -(-vec_lanes // table_part // 128) * 128 * table_part
    grad_vector = jnp.pad(grad_vector, ((0, 0), (0, spare - vec_lanes)))
    grad_vector = grad_vector.reshape(device_count * table_part, -1)
    small = jnp.concatenate([grad_normed, grad_vector], axis=1)
    small = scatter_rows(small, small_steps[:2:-1]).astype(HALF)
    small_shard = scatter_rows(small, small_steps[2::-1])
    part = up_next.shape[0] // 2
    up_got, down_got, _, _ = lax.optimization_barrier(
        (
            swap(up_next[part:], dp_steps[0]),
            swap(down_next[D // dp_count :], dp_steps[0]),
            small,
            qkv_first,
        )
    )
    up_out_shard = up_next[:part].astype(FULL) + up_got.astype(FULL)
    down_shard = (down_next[: D // dp_count].astype(FULL) + down_got.astype(FULL)).T
    up_shard = up_out_shard[:, :up_local]
    out_shard = up_out_shard[:, up_local : up_local + local_width].T
    table_shard = standardise_back(small_shard[:, :D] * vector_rows[4], unit_own, inverse_own)
    vector_shard = small_shard[:, D:].reshape(-1)[:vec_rows]

    qkv_grad_shard = jnp.stack(
        [qkv_shard[:, i * local_width : (i + 1) * local_width] for i in range(3)]
    )
    new_qkv = nesterov(
        qkv_weight, qkv_moment, qkv_average, qkv_grad_shard, 0.75 / math.sqrt(D * total_tokens)
    )
    new_out = nesterov(
        out_weight,
        out_moment,
        out_average,
        out_shard,
        0.125 * MAXLEN / math.sqrt(D * total_tokens),
    )
    new_up = nesterov(up_weight, up_moment, up_average, up_shard, 1.1 / math.sqrt(D * total_tokens))
    new_down = nesterov(
        down_weight, down_moment, down_average, down_shard, 1.0 / math.sqrt(FF * total_tokens)
    )
    new_table = nesterov(
        rel_table,
        table_moment,
        table_average,
        table_shard,
        0.55 * math.sqrt(MAXLEN / total_tokens),
    )
    new_vector = nesterov(
        vectors, vector_moment, vector_average, vector_shard, 0.3 / math.sqrt(total_tokens)
    )
    return (output, input_grad) + new_qkv + new_out + new_up + new_down + new_table + new_vector


def solution(mesh):
    rows = P("dp", None)
    owned = P(("dp", "head"), None)
    qkv = P(None, "dp", "head")
    out = P("head", "dp")
    up = P("dp", "head")
    vector = P(("dp", "head"))
    return jax.shard_map(
        per_device,
        mesh=mesh,
        in_specs=(rows,) * 3 + (qkv,) * 3 + (out,) * 3 + (up,) * 3 + (out,) * 3 + (owned,) * 3 + (vector,) * 3,
        out_specs=(owned,) * 2 + (qkv,) * 3 + (out,) * 3 + (up,) * 3 + (out,) * 3 + (owned,) * 3 + (vector,) * 3,
        check_vma=False,
    )
```

profile of v0, /device:TPU:0, one launch (start us, length us, event | category | flops | bytes accessed | tf_op | source)
XLA Modules:
  0.0 283.9 jit_solution(17710728164125113134)
XLA Ops:
  0.7 1.0 convert.22
  1.9 4.1 %collective-permute-start.5 = (bf16[96,640]{1,0:T(8,128)(2,1)S(1)}, bf16[96,640]{1,0:T(8,128)(2,1)S(1)}, u32[]{:S(2)}, u32[]{:S(2)}) collective-permute-start(bf16[96,640]{1,0:T(8,128)(2,1)S(1)} %fusion.36), channel_id=1, source_target_pairs={{0,16},{4,20},{8,24},{12,28},{16,0},{20,4},{24,8},{28,12},{1,17},{... | collective-permute-start | bytes 368648 | tf_op jit(solution)/shard_map/ppermute | solution.py:652
  11.3 3.0 %collective-permute-start.8 = (bf16[96,1024]{1,0:T(8,128)(2,1)S(1)}, bf16[96,1024]{1,0:T(8,128)(2,1)S(1)}, u32[]{:S(2)}, u32[]{:S(2)}) collective-permute-start(bf16[96,1024]{1,0:T(8,128)(2,1)S(1)} %fusion.34), channel_id=1, source_target_pairs={{0,16},{4,20},{8,24},{12,28},{16,0},{20,4},{24,8},{28,12},{1,17},{... | collective-permute-start | bytes 589832 | tf_op jit(solution)/shard_map/ppermute | solution.py:652
  14.6 4.1 %fusion.5.inputs_ref = bf16[768,1024]{1,0:T(8,128)(2,1)} fusion(bf16[1024,768]{1,0:T(8,128)(2,1)} %param.26, s32[768]{0:T(1024)S(1)} %add.292), kind=kOutput, calls=%fused_computation.9 | convolution fusion | flops 1209335808 | bytes 3148800 | tf_op jit(solution)/shard_map/dot_general | solution.py:37
  18.7 1.9 constant_dynamic-slice_fusion
  20.8 1.6 collective-permute-start.1
  23.0 2.0 collective-permute-done.1
  25.0 1.6 collective-permute-start.2
  27.3 1.6 collective-permute-start.6
  28.9 1.6 collective-permute-start.10
  30.7 1.6 collective-permute-start.3
  32.3 6.1 %collective-permute-done.10 = bf16[96,768]{1,0:T(8,128)(2,1)S(1)} collective-permute-done((bf16[96,768]{1,0:T(8,128)(2,1)S(1)}, bf16[96,768]{1,0:T(8,128)(2,1)S(1)}, u32[]{:S(2)}, u32[]{:S(2)}) %collective-permute-start.10) | collective-permute-done | bytes 147488 | tf_op jit(solution)/shard_map/ppermute | solution.py:652
  38.9 1.5 collective-permute-start.12
  40.4 1.5 collective-permute-start.13
  42.7 10.7 %collective-permute-done.11 = bf16[192,768]{1,0:T(8,128)(2,1)S(1)} collective-permute-done((bf16[192,768]{1,0:T(8,128)(2,1)S(1)}, bf16[192,768]{1,0:T(8,128)(2,1)S(1)}, u32[]{:S(2)}, u32[]{:S(2)}) %collective-permute-start.11) | collective-permute-done | bytes 294944 | tf_op jit(solution)/shard_map/ppermute | solution.py:652
  54.2 3.4 %collective-permute-start.22 = (bf16[4,192,768]{2,1,0:T(8,128)(2,1)S(1)}, bf16[4,192,768]{2,1,0:T(8,128)(2,1)}, u32[]{:S(2)}, u32[]{:S(2)}) collective-permute-start(bf16[4,192,768]{2,1,0:T(8,128)(2,1)S(1)} %pad_maximum_fusion.refs_1_.refs_12_), channel_id=1, source_target_pairs={{0,8},{4,12},{8,0},{12,4},{16,24},{20,28},{24,16},{28,20},{1,9},{5... | collective-permute-start | bytes 3538952 | tf_op jit(solution)/shard_map/ppermute | solution.py:652
  59.7 1.4 fusion.9.w_ref
  61.1 1.5 collective-permute-start.20
  65.9 2.5 fusion.12
  68.4 4.5 %fusion.tab_ref = bf16[2048,384]{1,0:T(8,128)(2,1)} fusion(bf16[2048,512]{1,0:T(8,128)(2,1)} %constant.27.clone, bf16[512,384]{1,0:T(8,128)(2,1)} %fusion.12, s32[512]{0:T(512)S(1)} %add.302), kind=kOutput, calls=%fused_computation.2 | convolution fusion | flops 1007878144 | bytes 4065280 | tf_op jit(solution)/shard_map/dot_general | solution.py:37
  72.9 2.9 %fusion.10.qkv_ref = bf16[1024,576]{1,0:T(8,128)(2,1)S(1)} fusion(bf16[1024,768]{1,0:T(8,128)(2,1)} %param.26, bf16[768,576]{1,0:T(8,128)(2,1)S(1)} %fusion.9.w_ref, f32[576]{0:T(1024)S(1)} %pad_maximum_fusion.14), kind=kOutput, calls=%fused_computation.20 | convolution fusion | flops 907149312 | bytes 3639552 | tf_op jit(solution)/shard_map/dot_general | solution.py:37
  75.9 1.6 collective-permute-start.21
  77.4 37.9 %shard_map.401 = (bf16[1024,192]{1,0:T(8,128)(2,1)S(1)}, bf16[3,1024,1024]{2,1,0:T(8,128)(2,1)}) custom-call(s32[5]{0:T(128)S(1)} %pad_add_fusion.info, bf16[1024,576]{1,0:T(8,128)(2,1)S(1)} %fusion.10.qkv_ref, bf16[2048,384]{1,0:T(8,128)(2,1)S(1)} %copy-done.17, bf16[384,1024]{1,0:T(8,128)(2,1)} %pad_maximum_fusion.5.refs_0_.refs_4_, ...), custom_call_target="tpu_custom_call" | custom-call | flops 30000001024 | bytes 30000000 | tf_op jit(solution)/shard_map/pallas_call | solution.py:328
  115.5 1.6 collective-permute-start.17
  117.4 4.5 %collective-permute-done.17.refs_2_ = bf16[256,192]{1,0:T(8,128)(2,1)S(1)} collective-permute-done((bf16[256,192]{1,0:T(8,128)(2,1)S(1)}, bf16[256,192]{1,0:T(8,128)(2,1)S(1)}, u32[]{:S(2)}, u32[]{:S(2)}) %collective-permute-start.17) | collective-permute-done | bytes 98336 | tf_op jit(solution)/shard_map/ppermute | solution.py:652
  121.9 1.9 collective-permute-done.18.refs_3_
  124.2 1.3 fusion.4.order_ref
  126.5 2.9 %fusion.11.refs_16_.normed_ref = bf16[768,512]{1,0:T(8,128)(2,1)} fusion(s32[768]{0:T(1024)S(1)} %add.292, f32[768]{0:T(1024)S(1)} %get-tuple-element.203, f32[768]{0:T(1024)S(1)} %get-tuple-element.202, bf16[512,896]{1,0:T(8,128)(2,1)} %copy-done.31), kind=kOutput, calls=%fused_computation.21 | convolution fusion | flops 606535680 | bytes 1582080 | tf_op jit(solution)/shard_map/dot_general | solution.py:37
  129.4 1.0 collective-permute-done.25.refs_11_
  131.3 20.6 %shard_map.402 = (bf16[256,768]{1,0:T(8,128)(2,1)}, f32[256,768]{1,0:T(8,128)S(1)}, f32[8,768]{1,0:T(8,128)S(1)}, f32[4,768]{1,0:T(4,128)S(1)}, bf16[256,192]{1,...) custom-call(s32[5]{0:T(128)S(1)} %pad_add_fusion.info, ...), custom_call_target="tpu_custom_call" | custom-call | flops 20000000000 | bytes 20000000 | tf_op jit(solution)/shard_map/pallas_call | solution.py:530
  155.0 1.5 collective-permute-start.28
  156.6 2.2 collective-permute-done.27
  158.8 2.5 collective-permute-done.28
  161.3 1.5 collective-permute-done.29
  162.9 2.1 fusion.13.refs_3_
  164.9 6.2 %collective-permute-start.35 = (bf16[2,2,192,768]{3,2,1,0:T(8,128)(2,1)S(1)}, bf16[2,2,192,768]{3,2,1,0:T(8,128)(2,1)S(1)}, u32[]{:S(2)}, u32[]{:S(2)}) collective-permute-start(bf16[2,2,192,768]{3,2,1,0:T(8,128)(2,1)S(1)} %fusion.13.refs_3_), channel_id=1, source_target_pairs={{0,8},{4,12},{8,0},{12,4},{16,24},{20,28},{24,16},{28,20},{1,9},{5... | collective-permute-start | bytes 3538952 | tf_op jit(solution)/shard_map/ppermute | solution.py:652
  171.1 3.6 %fusion.21 = (bf16[384,1024]{1,0:T(8,128)(2,1)S(1)}, bf16[384,1024]{1,0:T(8,128)(2,1)}, bf16[384,1024]{1,0:T(8,128)(2,1)S(1)}) fusion(bf16[2,768,1024]{2,1,0:T(8,128)(2,1)} %collective-permute-done.30, bf16[2,768,1024]{2,1,0:T(8,128)(2,1)S(1)} %copy-done.20), kind=kLoop, calls=%fused_computation.40 | loop fusion | flops 4718592 | bytes 7077888 | tf_op jit(solution)/shard_map/convert_element_type | solution.py:697
  175.2 1.5 collective-permute-start.33
  176.7 1.5 collective-permute-start.34
  178.2 31.3 %shard_map.403 = (bf16[1024,576]{1,0:T(8,128)(2,1)}, bf16[384,2048]{1,0:T(8,128)(2,1)}) custom-call(s32[5]{0:T(128)S(1)} %pad_add_fusion.info, bf16[1024,576]{1,0:T(8,128)(2,1)} %copy-done.18, bf16[2048,384]{1,0:T(8,128)(2,1)} %fusion.tab_ref, bf16[3,1024,1024]{2,1,0:T(8,128)(2,1)} %get-tuple-element.70.p_far, ...), custom_call_target="tpu_custom_call" | custom-call | flops 33999998976 | bytes 34000000 | tf_op jit(solution)/shard_map/pallas_call | solution.py:352
  209.6 3.0 %collective-permute-done.34 = bf16[384,1024]{1,0:T(8,128)(2,1)S(1)} collective-permute-done((bf16[384,1024]{1,0:T(8,128)(2,1)S(1)}, bf16[384,1024]{1,0:T(8,128)(2,1)S(1)}, u32[]{:S(2)}, u32[]{:S(2)}) %collective-permute-start.34) | collective-permute-done | bytes 786464 | tf_op jit(solution)/shard_map/ppermute | solution.py:663
  213.5 2.2 fusion.24
  216.3 1.5 collective-permute-start.44
  217.8 1.5 collective-permute-start.45
  219.3 2.2 fusion.8.refs_0_
  221.6 6.7 %shard_map.404 = (bf16[384,640]{1,0:T(8,128)(2,1)S(1)}, bf16[384,640]{1,0:T(8,128)(2,1)S(1)}, bf16[4,256,768]{2,1,0:T(8,128)(2,1)S(1)}, bf16[512,768]{1,0:T(8,128)(2,1)S(1)}, f32[16,768]{1,0:T(8,128)S(1)}) custom-call(s32[5]{0:T(128)S(1)} %pad_add_fusion.info, bf16[1024,576]{1,0:T(8,128)(2,1)S(1)} %copy-done.4, bf16[384,2048]{1,0:T(8,128)(2,1)S(1)} %copy-done.3, ...), custom_call_target="tpu_custom_call" | custom-call | flops 100000000 | bytes 100000 | tf_op jit(solution)/shard_map/pallas_call | solution.py:625
  228.2 1.1 copy-done
  233.7 2.2 constant_dynamic-update-slice_fusion.18
  236.6 1.7 constant_dynamic-update-slice_fusion.17
  238.3 1.1 slice.391
  241.4 1.6 add_convert_fusion.12
  243.4 1.1 add_convert_fusion.9
  244.6 2.7 collective-permute-start.42
  247.4 1.3 collective-permute-start.48
  248.7 5.3 %collective-permute-done.38 = bf16[384,640]{1,0:T(8,128)(2,1)S(1)} collective-permute-done((bf16[384,640]{1,0:T(8,128)(2,1)S(1)}, bf16[384,640]{1,0:T(8,128)(2,1)S(1)}, u32[]{:S(2)}, u32[]{:S(2)}) %collective-permute-start.38) | collective-permute-done | bytes 491552 | tf_op jit(solution)/shard_map/ppermute | solution.py:652
  254.9 1.3 collective-permute-start.39
  258.2 3.6 %collective-permute-done.42 = bf16[96,1024]{1,0:T(8,128)(2,1)S(1)} collective-permute-done((bf16[96,1024]{1,0:T(8,128)(2,1)S(1)}, bf16[96,1024]{1,0:T(8,128)(2,1)S(1)}, u32[]{:S(2)}, u32[]{:S(2)}) %collective-permute-start.42) | collective-permute-done | bytes 196640 | tf_op jit(solution)/shard_map/ppermute | solution.py:652
  265.2 2.2 multiply_add_fusion
  267.4 1.0 add_convert_fusion.13
  269.5 1.6 collective-permute-start.50
  271.1 1.3 add_convert_fusion.2
  272.5 1.3 collective-permute-start.37
  273.8 2.5 collective-permute-done.50
  277.9 3.2 %collective-permute-done.51 = bf16[16,896]{1,0:T(8,128)(2,1)S(1)} collective-permute-done((bf16[16,896]{1,0:T(8,128)(2,1)S(1)}, bf16[16,896]{1,0:T(8,128)(2,1)S(1)}, u32[]{:S(2)}, u32[]{:S(2)}) %collective-permute-start.51) | collective-permute-done | bytes 28704 | tf_op jit(solution)/shard_map/ppermute | solution.py:652
  (282 shorter events, 41.7 us)
Async XLA Ops:
  0.7 13.6 %copy-start.58 = (s32[8]{0:T(128)S(1)}, s32[8]{0:T(128)}, u32[]{:S(2)}) copy-start(s32[8]{0:T(128)} %constant.24.clone) | copy-start | bytes 100
  0.7 13.8 %copy-start.51 = (s32[32]{0:T(128)S(1)}, s32[32]{0:T(128)}, u32[]{:S(2)}) copy-start(s32[32]{0:T(128)} %constant.25.clone) | copy-start | bytes 388
  0.7 13.8 %copy-start.52 = (s32[32]{0:T(128)S(1)}, s32[32]{0:T(128)}, u32[]{:S(2)}) copy-start(s32[32]{0:T(128)} %constant.26.clone) | copy-start | bytes 388
  0.7 13.8 %copy-start.26 = (f32[768,96]{0,1:T(8,128)S(1)}, f32[768,96]{0,1:T(8,128)}, u32[]{:S(2)}) copy-start(f32[768,96]{0,1:T(8,128)} %param.38) | copy-start | bytes 884740
  1.9 25.4 %collective-permute-start.5 = (bf16[96,640]{1,0:T(8,128)(2,1)S(1)}, bf16[96,640]{1,0:T(8,128)(2,1)S(1)}, u32[]{:S(2)}, u32[]{:S(2)}) collective-permute-start(bf16[96,640]{1,0:T(8,128)(2,1)S(1)} %fusion.36), channel_id=1, source_target_pairs={{0,16},{4,20},{8,24},{12,28},{16,0},{20,4},{24,8},{28,12},{1,17},{... | collective-permute-start | bytes 368648 | tf_op jit(solution)/shard_map/ppermute | solution.py:652
  10.2 10.5 %collective-permute-start = (bf16[16,896]{1,0:T(8,128)(2,1)S(1)}, bf16[16,896]{1,0:T(8,128)(2,1)S(1)}, u32[]{:S(2)}, u32[]{:S(2)}) collective-permute-start(bf16[16,896]{1,0:T(8,128)(2,1)S(1)} %get-tuple-element.215), channel_id=1, source_target_pairs={{0,16},{4,20},{8,24},{12,28},{16,0},{20,4},{24,8},{28,12},{1,17},{... | collective-permute-start | bytes 86024 | tf_op jit(solution)/shard_map/ppermute | solution.py:652
  11.3 19.2 %collective-permute-start.8 = (bf16[96,1024]{1,0:T(8,128)(2,1)S(1)}, bf16[96,1024]{1,0:T(8,128)(2,1)S(1)}, u32[]{:S(2)}, u32[]{:S(2)}) collective-permute-start(bf16[96,1024]{1,0:T(8,128)(2,1)S(1)} %fusion.34), channel_id=1, source_target_pairs={{0,16},{4,20},{8,24},{12,28},{16,0},{20,4},{24,8},{28,12},{1,17},{... | collective-permute-start | bytes 589832 | tf_op jit(solution)/shard_map/ppermute | solution.py:652
  20.8 4.2 %collective-permute-start.1 = (bf16[32,896]{1,0:T(8,128)(2,1)S(1)}, bf16[32,896]{1,0:T(8,128)(2,1)S(1)}, u32[]{:S(2)}, u32[]{:S(2)}) collective-permute-start(bf16[32,896]{1,0:T(8,128)(2,1)S(1)} %pad_maximum_fusion.11), channel_id=1, source_target_pairs={{0,8},{4,12},{8,0},{12,4},{16,24},{20,28},{24,16},{28,20},{1,9},{5... | collective-permute-start | bytes 172040 | tf_op jit(solution)/shard_map/ppermute | solution.py:652
  25.0 5.7 %collective-permute-start.2 = (bf16[64,896]{1,0:T(8,128)(2,1)S(1)}, bf16[64,896]{1,0:T(8,128)(2,1)S(1)}, u32[]{:S(2)}, u32[]{:S(2)}) collective-permute-start(bf16[64,896]{1,0:T(8,128)(2,1)S(1)} %pad_maximum_fusion.10), channel_id=1, source_target_pairs={{0,4},{4,0},{8,12},{12,8},{16,20},{20,16},{24,28},{28,24},{1,5},{5... | collective-permute-start | bytes 344072 | tf_op jit(solution)/shard_map/ppermute | solution.py:652
  27.3 15.3 %copy-start.50 = (bf16[256,896]{1,0:T(8,128)(2,1)S(1)}, bf16[256,896]{1,0:T(8,128)(2,1)}, u32[]{:S(2)}) copy-start(bf16[256,896]{1,0:T(8,128)(2,1)} %get-tuple-element.200) | copy-start | bytes 1376260
  27.3 13.2 %collective-permute-start.6 = (bf16[192,640]{1,0:T(8,128)(2,1)S(1)}, bf16[192,640]{1,0:T(8,128)(2,1)S(1)}, u32[]{:S(2)}, u32[]{:S(2)}) collective-permute-start(bf16[192,640]{1,0:T(8,128)(2,1)S(1)} %pad_maximum_fusion.8), channel_id=1, source_target_pairs={{0,8},{4,12},{8,0},{12,4},{16,24},{20,28},{24,16},{28,20},{1,9},{5... | collective-permute-start | bytes 737288 | tf_op jit(solution)/shard_map/ppermute | solution.py:652
  28.9 9.4 %collective-permute-start.10 = (bf16[96,768]{1,0:T(8,128)(2,1)S(1)}, bf16[96,768]{1,0:T(8,128)(2,1)S(1)}, u32[]{:S(2)}, u32[]{:S(2)}) collective-permute-start(bf16[96,768]{1,0:T(8,128)(2,1)S(1)} %convert_bitcast_fusion), channel_id=1, source_target_pairs={{0,16},{4,20},{8,24},{12,28},{16,0},{20,4},{24,8},{28,12},{1,17},{... | collective-permute-start | bytes 442376 | tf_op jit(solution)/shard_map/ppermute | solution.py:652
  30.6 27.0 %collective-permute-start.9 = (bf16[192,1024]{1,0:T(8,128)(2,1)S(1)}, bf16[192,1024]{1,0:T(8,128)(2,1)S(1)}, u32[]{:S(2)}, u32[]{:S(2)}) collective-permute-start(bf16[192,1024]{1,0:T(8,128)(2,1)S(1)} %pad_maximum_fusion.7), channel_id=1, source_target_pairs={{0,8},{4,12},{8,0},{12,4},{16,24},{20,28},{24,16},{28,20},{1,9},{5... | collective-permute-start | bytes 1179656 | tf_op jit(solution)/shard_map/ppermute | solution.py:652
  30.7 11.2 %collective-permute-start.3 = (bf16[128,896]{1,0:T(8,128)(2,1)S(1)}, bf16[128,896]{1,0:T(8,128)(2,1)S(1)}, u32[]{:S(2)}, u32[]{:S(2)}) collective-permute-start(bf16[128,896]{1,0:T(8,128)(2,1)S(1)} %pad_maximum_fusion.9), channel_id=1, source_target_pairs={{0,2},{1,3},{2,0},{3,1},{4,6},{5,7},{6,4},{7,5},{8,10},{9,11},{10,... | collective-permute-start | bytes 688136 | tf_op jit(solution)/shard_map/ppermute | solution.py:652
  38.4 15.0 %collective-permute-start.11 = (bf16[192,768]{1,0:T(8,128)(2,1)S(1)}, bf16[192,768]{1,0:T(8,128)(2,1)S(1)}, u32[]{:S(2)}, u32[]{:S(2)}) collective-permute-start(bf16[192,768]{1,0:T(8,128)(2,1)S(1)} %constant_dynamic-update-slice_fusion.11), channel_id=1, source_target_pairs={{0,4},{4,0},{8,12},{12,8},{16,20},{20,16},{24,28},{28,24},{1,5},{5... | collective-permute-start | bytes 884744 | tf_op jit(solution)/shard_map/ppermute | solution.py:652
  38.9 14.5 %collective-permute-start.12 = (bf16[192,768]{1,0:T(8,128)(2,1)S(1)}, bf16[192,768]{1,0:T(8,128)(2,1)S(1)}, u32[]{:S(2)}, u32[]{:S(2)}) collective-permute-start(bf16[192,768]{1,0:T(8,128)(2,1)S(1)} %constant_dynamic-update-slice_fusion.11), channel_id=1, source_target_pairs={{0,2},{1,3},{2,0},{3,1},{4,6},{5,7},{6,4},{7,5},{8,10},{9,11},{10,... | collective-permute-start | bytes 884744 | tf_op jit(solution)/shard_map/ppermute | solution.py:652
  40.4 13.0 %collective-permute-start.13 = (bf16[192,768]{1,0:T(8,128)(2,1)S(1)}, bf16[192,768]{1,0:T(8,128)(2,1)S(1)}, u32[]{:S(2)}, u32[]{:S(2)}) collective-permute-start(bf16[192,768]{1,0:T(8,128)(2,1)S(1)} %constant_dynamic-update-slice_fusion.11), channel_id=1, source_target_pairs={{0,6},{1,7},{2,4},{3,5},{4,2},{5,3},{6,0},{7,1},{8,14},{9,15},{10,... | collective-permute-start | bytes 884744 | tf_op jit(solution)/shard_map/ppermute | solution.py:663
  42.0 17.2 %collective-permute-start.7 = (bf16[384,640]{1,0:T(8,128)(2,1)S(1)}, bf16[384,640]{1,0:T(8,128)(2,1)S(1)}, u32[]{:S(2)}, u32[]{:S(2)}) collective-permute-start(bf16[384,640]{1,0:T(8,128)(2,1)S(1)} %pad_maximum_fusion.6), channel_id=1, source_target_pairs={{0,4},{4,0},{8,12},{12,8},{16,20},{20,16},{24,28},{28,24},{1,5},{5... | collective-permute-start | bytes 1474568 | tf_op jit(solution)/shard_map/ppermute | solution.py:652
  42.6 10.8 %copy-start.29 = (bf16[512,896]{1,0:T(8,128)(2,1)}, bf16[512,896]{1,0:T(8,128)(2,1)S(1)}, u32[]{:S(2)}) copy-start(bf16[512,896]{1,0:T(8,128)(2,1)S(1)} %get-tuple-element.194) | copy-start | bytes 2752516
  53.4 7.7 %collective-permute-start.4 = (bf16[256,896]{1,0:T(8,128)(2,1)S(1)}, bf16[256,896]{1,0:T(8,128)(2,1)S(1)}, u32[]{:S(2)}, u32[]{:S(2)}) collective-permute-start(bf16[256,896]{1,0:T(8,128)(2,1)S(1)} %get-tuple-element.193), channel_id=1, source_target_pairs={{0,1},{1,0},{2,3},{3,2},{4,5},{5,4},{6,7},{7,6},{8,9},{9,8},{10,11... | collective-permute-start | bytes 1376264 | tf_op jit(solution)/shard_map/ppermute | solution.py:652
  53.6 23.8 %copy-start.5 = (bf16[4,192,768]{2,1,0:T(8,128)(2,1)}, bf16[4,192,768]{2,1,0:T(8,128)(2,1)S(1)}, u32[]{:S(2)}) copy-start(bf16[4,192,768]{2,1,0:T(8,128)(2,1)S(1)} %pad_maximum_fusion.refs_1_.refs_12_) | copy-start | bytes 3538948
  53.6 61.8 %collective-permute-start.15 = (bf16[4,192,768]{2,1,0:T(8,128)(2,1)S(1)}, bf16[4,192,768]{2,1,0:T(8,128)(2,1)}, u32[]{:S(2)}, u32[]{:S(2)}) collective-permute-start(bf16[4,192,768]{2,1,0:T(8,128)(2,1)S(1)} %pad_maximum_fusion.refs_1_.refs_12_), channel_id=1, source_target_pairs={{0,1},{1,0},{2,3},{3,2},{4,5},{5,4},{6,7},{7,6},{8,9},{9,8},{10,11... | collective-permute-start | bytes 3538952 | tf_op jit(solution)/shard_map/ppermute | solution.py:652
  54.2 63.2 %collective-permute-start.22 = (bf16[4,192,768]{2,1,0:T(8,128)(2,1)S(1)}, bf16[4,192,768]{2,1,0:T(8,128)(2,1)}, u32[]{:S(2)}, u32[]{:S(2)}) collective-permute-start(bf16[4,192,768]{2,1,0:T(8,128)(2,1)S(1)} %pad_maximum_fusion.refs_1_.refs_12_), channel_id=1, source_target_pairs={{0,8},{4,12},{8,0},{12,4},{16,24},{20,28},{24,16},{28,20},{1,9},{5... | collective-permute-start | bytes 3538952 | tf_op jit(solution)/shard_map/ppermute | solution.py:652
  58.5 17.4 %collective-permute-start.14 = (bf16[384,1024]{1,0:T(8,128)(2,1)}, bf16[384,1024]{1,0:T(8,128)(2,1)}, u32[]{:S(2)}, u32[]{:S(2)}) collective-permute-start(bf16[384,1024]{1,0:T(8,128)(2,1)} %pad_maximum_fusion.5.refs_0_.refs_4_), channel_id=1, source_target_pairs={{0,1},{1,0},{2,3},{3,2},{4,5},{5,4},{6,7},{7,6},{8,9},{9,8},{10,11... | collective-permute-start | bytes 2359304 | tf_op jit(solution)/shard_map/ppermute | solution.py:652
  59.2 56.3 %collective-permute-start.19 = (bf16[384,1024]{1,0:T(8,128)(2,1)}, bf16[384,1024]{1,0:T(8,128)(2,1)}, u32[]{:S(2)}, u32[]{:S(2)}) collective-permute-start(bf16[384,1024]{1,0:T(8,128)(2,1)} %pad_maximum_fusion.5.refs_0_.refs_4_), channel_id=1, source_target_pairs={{0,4},{4,0},{8,12},{12,8},{16,20},{20,16},{24,28},{28,24},{1,5},{5... | collective-permute-start | bytes 2359304 | tf_op jit(solution)/shard_map/ppermute | solution.py:652
  61.1 11.8 %copy-start.6 = (bf16[768,576]{1,0:T(8,128)(2,1)}, bf16[768,576]{1,0:T(8,128)(2,1)S(1)}, u32[]{:S(2)}) copy-start(bf16[768,576]{1,0:T(8,128)(2,1)S(1)} %fusion.9.w_ref) | copy-start | bytes 2654212
  61.1 56.0 %collective-permute-start.20 = (bf16[384,1024]{1,0:T(8,128)(2,1)}, bf16[384,1024]{1,0:T(8,128)(2,1)}, u32[]{:S(2)}, u32[]{:S(2)}) collective-permute-start(bf16[384,1024]{1,0:T(8,128)(2,1)} %pad_maximum_fusion.5.refs_0_.refs_4_), channel_id=1, source_target_pairs={{0,2},{1,3},{2,0},{3,1},{4,6},{5,7},{6,4},{7,5},{8,10},{9,11},{10,... | collective-permute-start | bytes 2359304 | tf_op jit(solution)/shard_map/ppermute | solution.py:652
  75.8 39.5 %copy-start.18 = (bf16[1024,576]{1,0:T(8,128)(2,1)}, bf16[1024,576]{1,0:T(8,128)(2,1)S(1)}, u32[]{:S(2)}) copy-start(bf16[1024,576]{1,0:T(8,128)(2,1)S(1)} %fusion.10.qkv_ref) | copy-start | bytes 3538948
  75.9 41.5 %collective-permute-start.21 = (bf16[384,1024]{1,0:T(8,128)(2,1)}, bf16[384,1024]{1,0:T(8,128)(2,1)S(1)}, u32[]{:S(2)}, u32[]{:S(2)}) collective-permute-start(bf16[384,1024]{1,0:T(8,128)(2,1)} %pad_maximum_fusion.5.refs_0_.refs_4_), channel_id=1, source_target_pairs={{0,6},{1,7},{2,4},{3,5},{4,2},{5,3},{6,0},{7,1},{8,14},{9,15},{10,... | collective-permute-start | bytes 2359304 | tf_op jit(solution)/shard_map/ppermute | solution.py:663
  115.4 2.0 collective-permute-start.16
  115.5 6.4 %collective-permute-start.17 = (bf16[256,192]{1,0:T(8,128)(2,1)S(1)}, bf16[256,192]{1,0:T(8,128)(2,1)S(1)}, u32[]{:S(2)}, u32[]{:S(2)}) collective-permute-start(bf16[256,192]{1,0:T(8,128)(2,1)S(1)} %get-tuple-element.187), channel_id=1, source_target_pairs={{0,2},{1,3},{2,0},{3,1},{4,6},{5,7},{6,4},{7,5},{8,10},{9,11},{10,... | collective-permute-start | bytes 294920 | tf_op jit(solution)/shard_map/ppermute | solution.py:652
  117.1 6.7 %collective-permute-start.18 = (bf16[256,192]{1,0:T(8,128)(2,1)S(1)}, bf16[256,192]{1,0:T(8,128)(2,1)S(1)}, u32[]{:S(2)}, u32[]{:S(2)}) collective-permute-start(bf16[256,192]{1,0:T(8,128)(2,1)S(1)} %get-tuple-element.186), channel_id=1, source_target_pairs={{0,3},{1,2},{2,1},{3,0},{4,7},{5,6},{6,5},{7,4},{8,11},{9,10},{10,... | collective-permute-start | bytes 294920 | tf_op jit(solution)/shard_map/ppermute | solution.py:652
  123.8 6.7 %collective-permute-start.26 = (bf16[4,192,768]{2,1,0:T(8,128)(2,1)}, bf16[4,192,768]{2,1,0:T(8,128)(2,1)}, u32[]{:S(2)}, u32[]{:S(2)}) collective-permute-start(bf16[4,192,768]{2,1,0:T(8,128)(2,1)} %collective-permute-done.22.refs_13_), channel_id=1, source_target_pairs={{0,1},{1,0},{2,3},{3,2},{4,5},{5,4},{6,7},{7,6},{8,9},{9,8},{10,11... | collective-permute-start | bytes 3538952 | tf_op jit(solution)/shard_map/ppermute | solution.py:652
  125.6 3.8 %collective-permute-start.23 = (bf16[384,1024]{1,0:T(8,128)(2,1)}, bf16[384,1024]{1,0:T(8,128)(2,1)S(1)}, u32[]{:S(2)}, u32[]{:S(2)}) collective-permute-start(bf16[384,1024]{1,0:T(8,128)(2,1)} %collective-permute-done.19.refs_5_), channel_id=1, source_target_pairs={{0,1},{1,0},{2,3},{3,2},{4,5},{5,4},{6,7},{7,6},{8,9},{9,8},{10,11... | collective-permute-start | bytes 2359304 | tf_op jit(solution)/shard_map/ppermute | solution.py:652
  125.9 3.5 %collective-permute-start.24 = (bf16[384,1024]{1,0:T(8,128)(2,1)}, bf16[384,1024]{1,0:T(8,128)(2,1)S(1)}, u32[]{:S(2)}, u32[]{:S(2)}) collective-permute-start(bf16[384,1024]{1,0:T(8,128)(2,1)} %collective-permute-done.20.refs_6_), channel_id=1, source_target_pairs={{0,1},{1,0},{2,3},{3,2},{4,5},{5,4},{6,7},{7,6},{8,9},{9,8},{10,11... | collective-permute-start | bytes 2359304 | tf_op jit(solution)/shard_map/ppermute | solution.py:652
  126.2 4.2 %collective-permute-start.25 = (bf16[384,1024]{1,0:T(8,128)(2,1)}, bf16[384,1024]{1,0:T(8,128)(2,1)S(1)}, u32[]{:S(2)}, u32[]{:S(2)}) collective-permute-start(bf16[384,1024]{1,0:T(8,128)(2,1)} %copy-done.53), channel_id=1, source_target_pairs={{0,1},{1,0},{2,3},{3,2},{4,5},{5,4},{6,7},{7,6},{8,9},{9,8},{10,11... | collective-permute-start | bytes 2359304 | tf_op jit(solution)/shard_map/ppermute | solution.py:652
  131.3 22.0 %copy-start.43 = (f32[192,96]{1,0:T(8,128)S(1)}, f32[192,96]{1,0:T(8,128)}, u32[]{:S(2)}) copy-start(f32[192,96]{1,0:T(8,128)} %param.33) | copy-start | bytes 221188
  131.3 22.7 %copy-start.44 = (f32[192,96]{1,0:T(8,128)S(1)}, f32[192,96]{1,0:T(8,128)}, u32[]{:S(2)}) copy-start(f32[192,96]{1,0:T(8,128)} %param.34) | copy-start | bytes 221188
  152.8 10.1 %collective-permute-start.30 = (bf16[2,768,1024]{2,1,0:T(8,128)(2,1)}, bf16[2,768,1024]{2,1,0:T(8,128)(2,1)}, u32[]{:S(2)}, u32[]{:S(2)}) collective-permute-start(bf16[2,768,1024]{2,1,0:T(8,128)(2,1)} %get-tuple-element.76), channel_id=1, source_target_pairs={{0,1},{1,0},{2,3},{3,2},{4,5},{5,4},{6,7},{7,6},{8,9},{9,8},{10,11... | collective-permute-start | bytes 9437192 | tf_op jit(solution)/shard_map/ppermute | solution.py:652
  153.0 9.9 %collective-permute-start.31 = (bf16[2,768,768]{2,1,0:T(8,128)(2,1)}, bf16[2,768,768]{2,1,0:T(8,128)(2,1)}, u32[]{:S(2)}, u32[]{:S(2)}) collective-permute-start(bf16[2,768,768]{2,1,0:T(8,128)(2,1)} %get-tuple-element.77), channel_id=1, source_target_pairs={{0,1},{1,0},{2,3},{3,2},{4,5},{5,4},{6,7},{7,6},{8,9},{9,8},{10,11... | collective-permute-start | bytes 7077896 | tf_op jit(solution)/shard_map/ppermute | solution.py:652
  154.7 4.1 %collective-permute-start.27 = (bf16[256,192]{1,0:T(8,128)(2,1)S(1)}, bf16[256,192]{1,0:T(8,128)(2,1)S(1)}, u32[]{:S(2)}, u32[]{:S(2)}) collective-permute-start(bf16[256,192]{1,0:T(8,128)(2,1)S(1)} %get-tuple-element.72), channel_id=1, source_target_pairs={{0,1},{1,0},{2,3},{3,2},{4,5},{5,4},{6,7},{7,6},{8,9},{9,8},{10,11... | collective-permute-start | bytes 294920 | tf_op jit(solution)/shard_map/ppermute | solution.py:652
  155.0 6.3 %collective-permute-start.28 = (bf16[256,192]{1,0:T(8,128)(2,1)S(1)}, bf16[256,192]{1,0:T(8,128)(2,1)S(1)}, u32[]{:S(2)}, u32[]{:S(2)}) collective-permute-start(bf16[256,192]{1,0:T(8,128)(2,1)S(1)} %get-tuple-element.73), channel_id=1, source_target_pairs={{0,2},{1,3},{2,0},{3,1},{4,6},{5,7},{6,4},{7,5},{8,10},{9,11},{10,... | collective-permute-start | bytes 294920 | tf_op jit(solution)/shard_map/ppermute | solution.py:652
  156.5 6.4 %collective-permute-start.29 = (bf16[256,192]{1,0:T(8,128)(2,1)S(1)}, bf16[256,192]{1,0:T(8,128)(2,1)S(1)}, u32[]{:S(2)}, u32[]{:S(2)}) collective-permute-start(bf16[256,192]{1,0:T(8,128)(2,1)S(1)} %get-tuple-element.74), channel_id=1, source_target_pairs={{0,3},{1,2},{2,1},{3,0},{4,7},{5,6},{6,5},{7,4},{8,11},{9,10},{10,... | collective-permute-start | bytes 294920 | tf_op jit(solution)/shard_map/ppermute | solution.py:652
  164.9 47.7 %collective-permute-start.35 = (bf16[2,2,192,768]{3,2,1,0:T(8,128)(2,1)S(1)}, bf16[2,2,192,768]{3,2,1,0:T(8,128)(2,1)S(1)}, u32[]{:S(2)}, u32[]{:S(2)}) collective-permute-start(bf16[2,2,192,768]{3,2,1,0:T(8,128)(2,1)S(1)} %fusion.13.refs_3_), channel_id=1, source_target_pairs={{0,8},{4,12},{8,0},{12,4},{16,24},{20,28},{24,16},{28,20},{1,9},{5... | collective-permute-start | bytes 3538952 | tf_op jit(solution)/shard_map/ppermute | solution.py:652
  174.7 34.8 %collective-permute-start.32 = (bf16[384,1024]{1,0:T(8,128)(2,1)S(1)}, bf16[384,1024]{1,0:T(8,128)(2,1)S(1)}, u32[]{:S(2)}, u32[]{:S(2)}) collective-permute-start(bf16[384,1024]{1,0:T(8,128)(2,1)S(1)} %get-tuple-element.182.refs_0_), channel_id=1, source_target_pairs={{0,4},{4,0},{8,12},{12,8},{16,20},{20,16},{24,28},{28,24},{1,5},{5... | collective-permute-start | bytes 2359304 | tf_op jit(solution)/shard_map/ppermute | solution.py:652
  175.2 34.3 %collective-permute-start.33 = (bf16[384,1024]{1,0:T(8,128)(2,1)}, bf16[384,1024]{1,0:T(8,128)(2,1)S(1)}, u32[]{:S(2)}, u32[]{:S(2)}) collective-permute-start(bf16[384,1024]{1,0:T(8,128)(2,1)} %get-tuple-element.181.refs_1_), channel_id=1, source_target_pairs={{0,2},{1,3},{2,0},{3,1},{4,6},{5,7},{6,4},{7,5},{8,10},{9,11},{10,... | collective-permute-start | bytes 2359304 | tf_op jit(solution)/shard_map/ppermute | solution.py:652
  176.7 35.9 %collective-permute-start.34 = (bf16[384,1024]{1,0:T(8,128)(2,1)S(1)}, bf16[384,1024]{1,0:T(8,128)(2,1)S(1)}, u32[]{:S(2)}, u32[]{:S(2)}) collective-permute-start(bf16[384,1024]{1,0:T(8,128)(2,1)S(1)} %get-tuple-element.180.refs_2_), channel_id=1, source_target_pairs={{0,6},{1,7},{2,4},{3,5},{4,2},{5,3},{6,0},{7,1},{8,14},{9,15},{10,... | collective-permute-start | bytes 2359304 | tf_op jit(solution)/shard_map/ppermute | solution.py:663
  215.7 24.7 %collective-permute-start.43 = (bf16[192,768]{1,0:T(8,128)(2,1)S(1)}, bf16[192,768]{1,0:T(8,128)(2,1)}, u32[]{:S(2)}, u32[]{:S(2)}) collective-permute-start(bf16[192,768]{1,0:T(8,128)(2,1)S(1)} %get-tuple-element.185.refs_1_), channel_id=1, source_target_pairs={{0,4},{4,0},{8,12},{12,8},{16,20},{20,16},{24,28},{28,24},{1,5},{5... | collective-permute-start | bytes 884744 | tf_op jit(solution)/shard_map/ppermute | solution.py:652
  216.3 24.9 %collective-permute-start.44 = (bf16[192,768]{1,0:T(8,128)(2,1)S(1)}, bf16[192,768]{1,0:T(8,128)(2,1)}, u32[]{:S(2)}, u32[]{:S(2)}) collective-permute-start(bf16[192,768]{1,0:T(8,128)(2,1)S(1)} %get-tuple-element.184.refs_2_), channel_id=1, source_target_pairs={{0,2},{1,3},{2,0},{3,1},{4,6},{5,7},{6,4},{7,5},{8,10},{9,11},{10,... | collective-permute-start | bytes 884744 | tf_op jit(solution)/shard_map/ppermute | solution.py:652
  217.8 23.6 %collective-permute-start.45 = (bf16[192,768]{1,0:T(8,128)(2,1)S(1)}, bf16[192,768]{1,0:T(8,128)(2,1)}, u32[]{:S(2)}, u32[]{:S(2)}) collective-permute-start(bf16[192,768]{1,0:T(8,128)(2,1)S(1)} %get-tuple-element.183.refs_3_), channel_id=1, source_target_pairs={{0,6},{1,7},{2,4},{3,5},{4,2},{5,3},{6,0},{7,1},{8,14},{9,15},{10,... | collective-permute-start | bytes 884744 | tf_op jit(solution)/shard_map/ppermute | solution.py:663
  232.9 10.5 %collective-permute-start.41 = (bf16[192,1024]{1,0:T(8,128)(2,1)}, bf16[192,1024]{1,0:T(8,128)(2,1)}, u32[]{:S(2)}, u32[]{:S(2)}) collective-permute-start(bf16[192,1024]{1,0:T(8,128)(2,1)} %slice.383), channel_id=1, source_target_pairs={{0,8},{4,12},{8,0},{12,4},{16,24},{20,28},{24,16},{28,20},{1,9},{5... | collective-permute-start | bytes 1179656 | tf_op jit(solution)/shard_map/ppermute | solution.py:652
  239.4 7.9 %collective-permute-start.47 = (bf16[256,896]{1,0:T(8,128)(2,1)S(1)}, bf16[256,896]{1,0:T(8,128)(2,1)S(1)}, u32[]{:S(2)}, u32[]{:S(2)}) collective-permute-start(bf16[256,896]{1,0:T(8,128)(2,1)S(1)} %slice.391), channel_id=1, source_target_pairs={{0,1},{1,0},{2,3},{3,2},{4,5},{5,4},{6,7},{7,6},{8,9},{9,8},{10,11... | collective-permute-start | bytes 1376264 | tf_op jit(solution)/shard_map/ppermute | solution.py:652
  240.4 13.7 %collective-permute-start.38 = (bf16[384,640]{1,0:T(8,128)(2,1)S(1)}, bf16[384,640]{1,0:T(8,128)(2,1)S(1)}, u32[]{:S(2)}, u32[]{:S(2)}) collective-permute-start(bf16[384,640]{1,0:T(8,128)(2,1)S(1)} %copy-done.16), channel_id=1, source_target_pairs={{0,4},{4,0},{8,12},{12,8},{16,20},{20,16},{24,28},{28,24},{1,5},{5... | collective-permute-start | bytes 1474568 | tf_op jit(solution)/shard_map/ppermute | solution.py:652
  241.2 29.8 %collective-permute-start.36 = (bf16[2,256,768]{2,1,0:T(8,128)(2,1)}, bf16[2,256,768]{2,1,0:T(8,128)(2,1)}, u32[]{:S(2)}, u32[]{:S(2)}) collective-permute-start(bf16[2,256,768]{2,1,0:T(8,128)(2,1)} %slice.312), channel_id=1, source_target_pairs={{0,1},{1,0},{2,3},{3,2},{4,5},{5,4},{6,7},{7,6},{8,9},{9,8},{10,11... | collective-permute-start | bytes 2359304 | tf_op jit(solution)/shard_map/ppermute | solution.py:652
  243.1 11.0 %copy-start.13 = (bf16[384,640]{1,0:T(8,128)(2,1)S(1)}, bf16[384,640]{1,0:T(8,128)(2,1)}, u32[]{:S(2)}) copy-start(bf16[384,640]{1,0:T(8,128)(2,1)} %copy-done.12) | copy-start | bytes 1474564
  243.1 15.1 %collective-permute-start.46 = (bf16[96,768]{1,0:T(8,128)(2,1)S(1)}, bf16[96,768]{1,0:T(8,128)(2,1)S(1)}, u32[]{:S(2)}, u32[]{:S(2)}) collective-permute-start(bf16[96,768]{1,0:T(8,128)(2,1)S(1)} %slice.388), channel_id=1, source_target_pairs={{0,16},{4,20},{8,24},{12,28},{16,0},{20,4},{24,8},{28,12},{1,17},{... | collective-permute-start | bytes 442376 | tf_op jit(solution)/shard_map/ppermute | solution.py:652
  244.6 17.3 %collective-permute-start.42 = (bf16[96,1024]{1,0:T(8,128)(2,1)S(1)}, bf16[96,1024]{1,0:T(8,128)(2,1)S(1)}, u32[]{:S(2)}, u32[]{:S(2)}) collective-permute-start(bf16[96,1024]{1,0:T(8,128)(2,1)S(1)} %slice.385), channel_id=1, source_target_pairs={{0,16},{4,20},{8,24},{12,28},{16,0},{20,4},{24,8},{28,12},{1,17},{... | collective-permute-start | bytes 589832 | tf_op jit(solution)/shard_map/ppermute | solution.py:652
  247.4 8.8 %collective-permute-start.48 = (bf16[128,896]{1,0:T(8,128)(2,1)S(1)}, bf16[128,896]{1,0:T(8,128)(2,1)S(1)}, u32[]{:S(2)}, u32[]{:S(2)}) collective-permute-start(bf16[128,896]{1,0:T(8,128)(2,1)S(1)} %slice.393), channel_id=1, source_target_pairs={{0,2},{1,3},{2,0},{3,1},{4,6},{5,7},{6,4},{7,5},{8,10},{9,11},{10,... | collective-permute-start | bytes 688136 | tf_op jit(solution)/shard_map/ppermute | solution.py:652
  254.9 12.4 %collective-permute-start.39 = (bf16[192,640]{1,0:T(8,128)(2,1)}, bf16[192,640]{1,0:T(8,128)(2,1)}, u32[]{:S(2)}, u32[]{:S(2)}) collective-permute-start(bf16[192,640]{1,0:T(8,128)(2,1)} %slice.376), channel_id=1, source_target_pairs={{0,8},{4,12},{8,0},{12,4},{16,24},{20,28},{24,16},{28,20},{1,9},{5... | collective-permute-start | bytes 737288 | tf_op jit(solution)/shard_map/ppermute | solution.py:652
  257.0 11.5 %collective-permute-start.49 = (bf16[64,896]{1,0:T(8,128)(2,1)}, bf16[64,896]{1,0:T(8,128)(2,1)}, u32[]{:S(2)}, u32[]{:S(2)}) collective-permute-start(bf16[64,896]{1,0:T(8,128)(2,1)} %slice.398), channel_id=1, source_target_pairs={{0,4},{4,0},{8,12},{12,8},{16,20},{20,16},{24,28},{28,24},{1,5},{5... | collective-permute-start | bytes 344072 | tf_op jit(solution)/shard_map/ppermute | solution.py:652
  268.4 8.3 %collective-permute-start.40 = (bf16[96,640]{1,0:T(8,128)(2,1)S(1)}, bf16[96,640]{1,0:T(8,128)(2,1)S(1)}, u32[]{:S(2)}, u32[]{:S(2)}) collective-permute-start(bf16[96,640]{1,0:T(8,128)(2,1)S(1)} %slice.378), channel_id=1, source_target_pairs={{0,16},{4,20},{8,24},{12,28},{16,0},{20,4},{24,8},{28,12},{1,17},{... | collective-permute-start | bytes 368648 | tf_op jit(solution)/shard_map/ppermute | solution.py:652
  269.5 6.8 %collective-permute-start.50 = (bf16[32,896]{1,0:T(8,128)(2,1)S(1)}, bf16[32,896]{1,0:T(8,128)(2,1)S(1)}, u32[]{:S(2)}, u32[]{:S(2)}) collective-permute-start(bf16[32,896]{1,0:T(8,128)(2,1)S(1)} %slice.400), channel_id=1, source_target_pairs={{0,8},{4,12},{8,0},{12,4},{16,24},{20,28},{24,16},{28,20},{1,9},{5... | collective-permute-start | bytes 172040 | tf_op jit(solution)/shard_map/ppermute | solution.py:652
  272.5 10.3 %collective-permute-start.37 = (bf16[1,256,768]{2,1,0:T(8,128)(2,1)S(1)}, bf16[1,256,768]{2,1,0:T(8,128)(2,1)S(1)}, u32[]{:S(2)}, u32[]{:S(2)}) collective-permute-start(bf16[1,256,768]{2,1,0:T(8,128)(2,1)S(1)} %slice.374), channel_id=1, source_target_pairs={{0,2},{1,3},{2,0},{3,1},{4,6},{5,7},{6,4},{7,5},{8,10},{9,11},{10,... | collective-permute-start | bytes 1179656 | tf_op jit(solution)/shard_map/ppermute | solution.py:652
  276.3 4.8 %collective-permute-start.51 = (bf16[16,896]{1,0:T(8,128)(2,1)S(1)}, bf16[16,896]{1,0:T(8,128)(2,1)S(1)}, u32[]{:S(2)}, u32[]{:S(2)}) collective-permute-start(bf16[16,896]{1,0:T(8,128)(2,1)S(1)} %slice.402), channel_id=1, source_target_pairs={{0,16},{4,20},{8,24},{12,28},{16,0},{20,4},{24,8},{28,12},{1,17},{... | collective-permute-start | bytes 86024 | tf_op jit(solution)/shard_map/ppermute | solution.py:652
  (47 other events, 216.4 us)
where the time goes:
time: 286 us; the launch traced here: 284 us
  Pallas kernels  96.5 us (34%)
  starting transfers between devices  57.2 us (20%)
  waiting for transfers between devices  51.3 us (18%)
  other arithmetic  31.8 us (11%)
  local copies, waits for them, and re-layouts  26.6 us (9%)
  matrix products  18.7 us (7%)
    ppermute x48, starting transfers between devices, swap(): lax.ppermute(values, axis, [(i, i ^ bit) for i in range(lax.axis_size(axi...  51.2 us
    ppermute x48, waiting for transfers between devices, swap(): lax.ppermute(values, axis, [(i, i ^ bit) for i in range(lax.axis_size(axi...  48.2 us
    pallas_call x1, Pallas kernels, attention_forward(): pl.pallas_call(functools.partial(forward_kernel, owners=owners), out_shap...  37.9 us
    pallas_call x1, Pallas kernels, attention_backward(): pl.pallas_call(functools.partial(backward_kernel, owners=owners), out_sha...  31.3 us
    pallas_call x1, Pallas kernels, middle(): pl.pallas_call(middle_kernel, out_shape=(shape((rows, width), HALF), shap...  20.6 us
    dot_general x8, matrix products, dot(): return lax.dot_general(left, right, dims, preferred_element_type=FULL)  18.7 us
    unnamed x132, local copies, waits for them, and re-layouts  15.6 us
    convert_element_type x6, other arithmetic, add(): return sum((part.astype(FULL) for part in parts)).astype(HALF)  11.8 us
  transfers between devices with their start and end apart: 52, of which 16 were waited for; matrix products, arithmetic and copies ran while one was open for 22% of the time, Pallas kernels for 27%

commit v1 on v0

--- a/solution.py
+++ b/solution.py
@@ -341,7 +341,7 @@
             pltpu.SemaphoreType.DMA((rows // TILE,)),
         ],
         compiler_params=pltpu.CompilerParams(vmem_limit_bytes=48 * 2**20),
-        cost_estimate=kernel_cost(30),
+        cost_estimate=kernel_cost(60),
     )(info, qkv, tables, *before)
 
 
@@ -367,7 +367,7 @@
             pltpu.SemaphoreType.DMA((rows // TILE,)),
         ],
         compiler_params=pltpu.CompilerParams(vmem_limit_bytes=52 * 2**20),
-        cost_estimate=kernel_cost(34),
+        cost_estimate=kernel_cost(60),
     )(info, qkv, tables, probs, grad, *before)
 
 
@@ -802,7 +802,6 @@
         lax.dynamic_slice_in_dim(values, head_rank * quarter, quarter, 0)
         for values in (inputs, cotangent)
     )
-    both_first = after(both_first, inputs_across, inputs_own, cotangent_own)
     both_more = gather_rows(both_first, dp_steps[1:-1])
     both_last = swap(both_more, dp_steps[-1])
     w_qkv_turned = jnp.concatenate([both_more, both_last])[:, :qkv_span]
@@ -830,10 +829,10 @@
     up_near = gather_rows(up_out_own, dp_steps[:-1])
     up_blocks = [up_near, swap(up_near, low), swap(up_near, far), swap_both(up_near, low, far)]
     up_near_core = swap(up_near, core)
-    down_one = gather_rows(after(down_weight.T.astype(HALF), both_first), dp_steps[:-2])
-    down_near = jnp.stack(
-        [down_one, swap(down_one, low), swap(down_one, far), swap_both(down_one, low, far)]
-    )
+    down_one = gather_rows(after(down_weight.T.astype(HALF), both_more), dp_steps[:-2])
+    down_rest = (swap(down_one, low), swap(down_one, far), swap_both(down_one, low, far))
+    down_rest, *_ = lax.optimization_barrier((down_rest, both_last, up_near, inputs_across, inputs_own, cotangent_own))
+    down_near = jnp.stack([down_one, *down_rest])
     down_far = swap(down_near, mid)
     down_near_core = swap(down_near, core)
     differences = list(range(head_count))

time: 286 us -> 282 us (0.986)
  starting transfers between devices: 57.2 us -> 49.1 us
  waiting for transfers between devices: 51.3 us -> 56.7 us
    ppermute x48, starting transfers between devices: 51.2 us -> 42.5 us  [swap(): lax.ppermute(values, axis, [(i, i ^ bit) for i in range(lax.axis_size(axi...]
    ppermute x48, waiting for transfers between devices: 48.2 us -> 54.4 us  [swap(): lax.ppermute(values, axis, [(i, i ^ bit) for i in range(lax.axis_size(axi...]
    unnamed x132 -> x146, local copies, waits for them, and re-layouts: 15.6 us -> 16.8 us
  transfers between devices with their start and end apart: 52 -> 52, of which waited for: 16 -> 18; matrix products, arithmetic and copies ran while one was open for 22% -> 21% of each run, Pallas kernels for 27% -> 28%
where the time goes in v1:
time: 282 us; the launch traced here: 280 us
  Pallas kernels  99 us (35%)
  waiting for transfers between devices  56.7 us (20%)
  starting transfers between devices  49.1 us (17%)
  other arithmetic  29.6 us (10%)
  local copies, waits for them, and re-layouts  24.8 us (9%)
  matrix products  18.7 us (7%)
    ppermute x48, waiting for transfers between devices, swap(): lax.ppermute(values, axis, [(i, i ^ bit) for i in range(lax.axis_size(axi...  54.4 us
    ppermute x48, starting transfers between devices, swap(): lax.ppermute(values, axis, [(i, i ^ bit) for i in range(lax.axis_size(axi...  42.5 us
    pallas_call x1, Pallas kernels, attention_forward(): pl.pallas_call(functools.partial(forward_kernel, owners=owners), out_shap...  39.4 us
    pallas_call x1, Pallas kernels, attention_backward(): pl.pallas_call(functools.partial(backward_kernel, owners=owners), out_sha...  32.3 us
    pallas_call x1, Pallas kernels, middle(): pl.pallas_call(middle_kernel, out_shape=(shape((rows, width), HALF), shap...  20.6 us
    dot_general x8, matrix products, dot(): return lax.dot_general(left, right, dims, preferred_element_type=FULL)  18.7 us
    unnamed x146, local copies, waits for them, and re-layouts  16.8 us
    convert_element_type x6, other arithmetic, add(): return sum((part.astype(FULL) for part in parts)).astype(HALF)  11.9 us
  transfers between devices with their start and end apart: 52, of which 18 were waited for; matrix products, arithmetic and copies ran while one was open for 21% of the time, Pallas kernels for 28%

profile of v1, /device:TPU:0, one launch (start us, length us, event | category | flops | bytes accessed | tf_op | source)
XLA Modules:
  0.0 279.9 jit_solution(10197560996245184034)
XLA Ops:
  0.7 1.0 convert.22
  1.9 4.1 %collective-permute-start.5 = (bf16[96,640]{1,0:T(8,128)(2,1)S(1)}, bf16[96,640]{1,0:T(8,128)(2,1)S(1)}, u32[]{:S(2)}, u32[]{:S(2)}) collective-permute-start(bf16[96,640]{1,0:T(8,128)(2,1)S(1)} %fusion.36), channel_id=1, source_target_pairs={{0,16},{4,20},{8,24},{12,28},{16,0},{20,4},{24,8},{28,12},{1,17},{... | collective-permute-start | bytes 368648 | tf_op jit(solution)/shard_map/ppermute | solution.py:652
  6.0 1.0 copy.72
  7.6 1.0 convert.23
  9.8 2.9 %collective-permute-start = (bf16[16,896]{1,0:T(8,128)(2,1)S(1)}, bf16[16,896]{1,0:T(8,128)(2,1)S(1)}, u32[]{:S(2)}, u32[]{:S(2)}) collective-permute-start(bf16[16,896]{1,0:T(8,128)(2,1)S(1)} %get-tuple-element.219), channel_id=1, source_target_pairs={{0,16},{4,20},{8,24},{12,28},{16,0},{20,4},{24,8},{28,12},{1,17},{... | collective-permute-start | bytes 86024 | tf_op jit(solution)/shard_map/ppermute | solution.py:652
  13.1 4.1 %fusion.5.inputs_ref = bf16[768,1024]{1,0:T(8,128)(2,1)} fusion(bf16[1024,768]{1,0:T(8,128)(2,1)} %param.26, s32[768]{0:T(1024)S(1)} %add.292), kind=kOutput, calls=%fused_computation.9 | convolution fusion | flops 1209335808 | bytes 3148800 | tf_op jit(solution)/shard_map/dot_general | solution.py:37
  17.1 1.9 constant_dynamic-slice_fusion
  19.2 2.4 collective-permute-done
  23.0 1.4 collective-permute-start.6
  24.3 1.9 collective-permute-done.1
  26.2 1.7 collective-permute-start.2
  29.4 2.5 collective-permute-done.6
  31.9 3.4 %collective-permute-start.10 = (bf16[96,768]{1,0:T(8,128)(2,1)S(1)}, bf16[96,768]{1,0:T(8,128)(2,1)S(1)}, u32[]{:S(2)}, u32[]{:S(2)}) collective-permute-start(bf16[96,768]{1,0:T(8,128)(2,1)S(1)} %convert_bitcast_fusion), channel_id=1, source_target_pairs={{0,16},{4,20},{8,24},{12,28},{16,0},{20,4},{24,8},{28,12},{1,17},{... | collective-permute-start | bytes 442376 | tf_op jit(solution)/shard_map/ppermute | solution.py:652
  35.4 1.6 collective-permute-start.3
  37.0 1.5 collective-permute-start.7
  38.5 2.3 collective-permute-done.10
  40.8 1.7 collective-permute-start.11
  42.5 1.5 collective-permute-start.12
  44.5 1.1 pad_maximum_fusion.7.refs_0_.refs_4_
  45.6 14.2 %collective-permute-done.11 = bf16[192,768]{1,0:T(8,128)(2,1)S(1)} collective-permute-done((bf16[192,768]{1,0:T(8,128)(2,1)S(1)}, bf16[192,768]{1,0:T(8,128)(2,1)S(1)}, u32[]{:S(2)}, u32[]{:S(2)}) %collective-permute-start.11) | collective-permute-done | bytes 294944 | tf_op jit(solution)/shard_map/ppermute | solution.py:652
  59.8 1.5 collective-permute-start.19
  61.8 1.4 collective-permute-start.21
  63.4 1.4 fusion.9.w_ref
  66.9 2.5 fusion.12
  69.5 4.5 %fusion.tab_ref = bf16[2048,384]{1,0:T(8,128)(2,1)} fusion(bf16[2048,512]{1,0:T(8,128)(2,1)} %constant.27.clone, bf16[512,384]{1,0:T(8,128)(2,1)} %fusion.12, s32[512]{0:T(512)S(1)} %add.302), kind=kOutput, calls=%fused_computation.2 | convolution fusion | flops 1007878144 | bytes 4065280 | tf_op jit(solution)/shard_map/dot_general | solution.py:37
  74.0 2.9 %fusion.10.qkv_ref = bf16[1024,576]{1,0:T(8,128)(2,1)S(1)} fusion(bf16[1024,768]{1,0:T(8,128)(2,1)} %param.26, bf16[768,576]{1,0:T(8,128)(2,1)S(1)} %fusion.9.w_ref, f32[576]{0:T(1024)S(1)} %pad_maximum_fusion.16), kind=kOutput, calls=%fused_computation.20 | convolution fusion | flops 907149312 | bytes 3639552 | tf_op jit(solution)/shard_map/dot_general | solution.py:37
  76.9 1.4 collective-permute-start.22
  78.3 39.4 %shard_map.401 = (bf16[1024,192]{1,0:T(8,128)(2,1)S(1)}, bf16[3,1024,1024]{2,1,0:T(8,128)(2,1)}) custom-call(s32[5]{0:T(128)S(1)} %pad_add_fusion.info, bf16[1024,576]{1,0:T(8,128)(2,1)S(1)} %fusion.10.qkv_ref, bf16[2048,384]{1,0:T(8,128)(2,1)S(1)} %copy-done.17, bf16[384,1024]{1,0:T(8,128)(2,1)} %pad_maximum_fusion.7.refs_0_.refs_4_, ...), custom_call_target="tpu_custom_call" | custom-call | flops 60000002048 | bytes 60000000 | tf_op jit(solution)/shard_map/pallas_call | solution.py:328
  119.8 4.5 %collective-permute-done.17.refs_2_ = bf16[256,192]{1,0:T(8,128)(2,1)S(1)} collective-permute-done((bf16[256,192]{1,0:T(8,128)(2,1)S(1)}, bf16[256,192]{1,0:T(8,128)(2,1)S(1)}, u32[]{:S(2)}, u32[]{:S(2)}) %collective-permute-start.17) | collective-permute-done | bytes 98336 | tf_op jit(solution)/shard_map/ppermute | solution.py:652
  124.3 1.9 collective-permute-done.18.refs_3_
  126.6 1.3 fusion.4.order_ref
  128.9 2.9 %fusion.11.refs_16_.normed_ref = bf16[768,512]{1,0:T(8,128)(2,1)} fusion(s32[768]{0:T(1024)S(1)} %add.292, f32[768]{0:T(1024)S(1)} %get-tuple-element.207, f32[768]{0:T(1024)S(1)} %get-tuple-element.206, bf16[512,896]{1,0:T(8,128)(2,1)} %copy-done.31), kind=kOutput, calls=%fused_computation.21 | convolution fusion | flops 606535680 | bytes 1582080 | tf_op jit(solution)/shard_map/dot_general | solution.py:37
  131.8 1.1 collective-permute-done.25.refs_11_
  133.7 20.6 %shard_map.402 = (bf16[256,768]{1,0:T(8,128)(2,1)}, f32[256,768]{1,0:T(8,128)S(1)}, f32[8,768]{1,0:T(8,128)S(1)}, f32[4,768]{1,0:T(4,128)S(1)}, bf16[256,192]{1,...) custom-call(s32[5]{0:T(128)S(1)} %pad_add_fusion.info, ...), custom_call_target="tpu_custom_call" | custom-call | flops 20000000000 | bytes 20000000 | tf_op jit(solution)/shard_map/pallas_call | solution.py:530
  159.0 2.2 collective-permute-done.27
  161.2 2.5 collective-permute-done.28
  163.7 1.5 collective-permute-done.29
  165.3 2.1 fusion.13.refs_3_
  167.9 3.6 %fusion.21 = (bf16[384,1024]{1,0:T(8,128)(2,1)S(1)}, bf16[384,1024]{1,0:T(8,128)(2,1)}, bf16[384,1024]{1,0:T(8,128)(2,1)S(1)}) fusion(bf16[2,768,1024]{2,1,0:T(8,128)(2,1)} %collective-permute-done.30, bf16[2,768,1024]{2,1,0:T(8,128)(2,1)S(1)} %copy-done.20), kind=kLoop, calls=%fused_computation.41 | loop fusion | flops 4718592 | bytes 7077888 | tf_op jit(solution)/shard_map/convert_element_type | solution.py:697
  172.5 2.5 collective-permute-start.34
  175.0 32.3 %shard_map.403 = (bf16[1024,576]{1,0:T(8,128)(2,1)}, bf16[384,2048]{1,0:T(8,128)(2,1)}) custom-call(s32[5]{0:T(128)S(1)} %pad_add_fusion.info, bf16[1024,576]{1,0:T(8,128)(2,1)} %copy-done.18, bf16[2048,384]{1,0:T(8,128)(2,1)} %fusion.tab_ref, bf16[3,1024,1024]{2,1,0:T(8,128)(2,1)} %get-tuple-element.74.p_far, ...), custom_call_target="tpu_custom_call" | custom-call | flops 60000002048 | bytes 60000000 | tf_op jit(solution)/shard_map/pallas_call | solution.py:352
  207.4 2.3 collective-permute-done.34
  210.6 2.2 fusion.24
  214.1 2.2 collective-permute-start.45
  216.4 2.2 fusion.8.refs_0_
  218.6 6.7 %shard_map.404 = (bf16[384,640]{1,0:T(8,128)(2,1)S(1)}, bf16[384,640]{1,0:T(8,128)(2,1)S(1)}, bf16[4,256,768]{2,1,0:T(8,128)(2,1)S(1)}, bf16[512,768]{1,0:T(8,128)(2,1)S(1)}, f32[16,768]{1,0:T(8,128)S(1)}) custom-call(s32[5]{0:T(128)S(1)} %pad_add_fusion.info, bf16[1024,576]{1,0:T(8,128)(2,1)S(1)} %copy-done.4, bf16[384,2048]{1,0:T(8,128)(2,1)S(1)} %copy-done.3, ...), custom_call_target="tpu_custom_call" | custom-call | flops 100000000 | bytes 100000 | tf_op jit(solution)/shard_map/pallas_call | solution.py:625
  225.3 1.2 copy-done
  230.0 1.3 collective-permute-start.41
  231.3 2.2 constant_dynamic-update-slice_fusion.18
  234.3 1.1 slice.391
  237.5 1.6 add_convert_fusion.12
  239.9 1.1 add_convert_fusion.9
  241.0 2.3 collective-permute-start.42
  244.4 5.7 %collective-permute-done.38 = bf16[384,640]{1,0:T(8,128)(2,1)S(1)} collective-permute-done((bf16[384,640]{1,0:T(8,128)(2,1)S(1)}, bf16[384,640]{1,0:T(8,128)(2,1)S(1)}, u32[]{:S(2)}, u32[]{:S(2)}) %collective-permute-start.38) | collective-permute-done | bytes 491552 | tf_op jit(solution)/shard_map/ppermute | solution.py:652
  253.8 4.0 %collective-permute-done.42 = bf16[96,1024]{1,0:T(8,128)(2,1)S(1)} collective-permute-done((bf16[96,1024]{1,0:T(8,128)(2,1)S(1)}, bf16[96,1024]{1,0:T(8,128)(2,1)S(1)}, u32[]{:S(2)}, u32[]{:S(2)}) %collective-permute-start.42) | collective-permute-done | bytes 196640 | tf_op jit(solution)/shard_map/ppermute | solution.py:652
  257.9 1.0 multiply_add_fusion.2
  261.2 2.1 multiply_add_fusion
  263.3 1.0 add_convert_fusion.13
  265.4 1.2 collective-permute-start.50
  266.6 1.3 add_convert_fusion.2
  268.8 3.4 %collective-permute-done.50 = bf16[32,896]{1,0:T(8,128)(2,1)S(1)} collective-permute-done((bf16[32,896]{1,0:T(8,128)(2,1)S(1)}, bf16[32,896]{1,0:T(8,128)(2,1)S(1)}, u32[]{:S(2)}, u32[]{:S(2)}) %collective-permute-start.50) | collective-permute-done | bytes 57376 | tf_op jit(solution)/shard_map/ppermute | solution.py:652
  272.9 1.0 multiply_add_fusion.4
  273.9 3.2 %collective-permute-done.51 = bf16[16,896]{1,0:T(8,128)(2,1)S(1)} collective-permute-done((bf16[16,896]{1,0:T(8,128)(2,1)S(1)}, bf16[16,896]{1,0:T(8,128)(2,1)S(1)}, u32[]{:S(2)}, u32[]{:S(2)}) %collective-permute-start.51) | collective-permute-done | bytes 28704 | tf_op jit(solution)/shard_map/ppermute | solution.py:652
  278.8 1.0 bitcast_add_fusion.1
  (296 shorter events, 39.9 us)
Async XLA Ops:
  0.7 12.1 %copy-start.65 = (s32[8]{0:T(128)S(1)}, s32[8]{0:T(128)}, u32[]{:S(2)}) copy-start(s32[8]{0:T(128)} %constant.24.clone) | copy-start | bytes 100
  0.7 12.3 %copy-start.59 = (s32[32]{0:T(128)S(1)}, s32[32]{0:T(128)}, u32[]{:S(2)}) copy-start(s32[32]{0:T(128)} %constant.25.clone) | copy-start | bytes 388
  0.7 12.3 %copy-start.60 = (s32[32]{0:T(128)S(1)}, s32[32]{0:T(128)}, u32[]{:S(2)}) copy-start(s32[32]{0:T(128)} %constant.26.clone) | copy-start | bytes 388
  0.7 12.0 %copy-start.26 = (f32[768,96]{0,1:T(8,128)S(1)}, f32[768,96]{0,1:T(8,128)}, u32[]{:S(2)}) copy-start(f32[768,96]{0,1:T(8,128)} %param.38) | copy-start | bytes 884740
  1.9 21.1 %collective-permute-start.5 = (bf16[96,640]{1,0:T(8,128)(2,1)S(1)}, bf16[96,640]{1,0:T(8,128)(2,1)S(1)}, u32[]{:S(2)}, u32[]{:S(2)}) collective-permute-start(bf16[96,640]{1,0:T(8,128)(2,1)S(1)} %fusion.36), channel_id=1, source_target_pairs={{0,16},{4,20},{8,24},{12,28},{16,0},{20,4},{24,8},{28,12},{1,17},{... | collective-permute-start | bytes 368648 | tf_op jit(solution)/shard_map/ppermute | solution.py:652
  8.6 19.9 %collective-permute-start.8 = (bf16[96,1024]{1,0:T(8,128)(2,1)S(1)}, bf16[96,1024]{1,0:T(8,128)(2,1)S(1)}, u32[]{:S(2)}, u32[]{:S(2)}) collective-permute-start(bf16[96,1024]{1,0:T(8,128)(2,1)S(1)} %fusion.34), channel_id=1, source_target_pairs={{0,16},{4,20},{8,24},{12,28},{16,0},{20,4},{24,8},{28,12},{1,17},{... | collective-permute-start | bytes 589832 | tf_op jit(solution)/shard_map/ppermute | solution.py:652
  9.8 11.7 %collective-permute-start = (bf16[16,896]{1,0:T(8,128)(2,1)S(1)}, bf16[16,896]{1,0:T(8,128)(2,1)S(1)}, u32[]{:S(2)}, u32[]{:S(2)}) collective-permute-start(bf16[16,896]{1,0:T(8,128)(2,1)S(1)} %get-tuple-element.219), channel_id=1, source_target_pairs={{0,16},{4,20},{8,24},{12,28},{16,0},{20,4},{24,8},{28,12},{1,17},{... | collective-permute-start | bytes 86024 | tf_op jit(solution)/shard_map/ppermute | solution.py:652
  13.0 53.2 %copy-start.54 = (s32[32]{0:T(128)}, s32[32]{0:T(128)S(1)}, u32[]{:S(2)}) copy-start(s32[32]{0:T(128)S(1)} %get-tuple-element.181) | copy-start | bytes 388
  21.6 4.6 %collective-permute-start.1 = (bf16[32,896]{1,0:T(8,128)(2,1)S(1)}, bf16[32,896]{1,0:T(8,128)(2,1)S(1)}, u32[]{:S(2)}, u32[]{:S(2)}) collective-permute-start(bf16[32,896]{1,0:T(8,128)(2,1)S(1)} %pad_maximum_fusion.13), channel_id=1, source_target_pairs={{0,8},{4,12},{8,0},{12,4},{16,24},{20,28},{24,16},{28,20},{1,9},{5... | collective-permute-start | bytes 172040 | tf_op jit(solution)/shard_map/ppermute | solution.py:652
  23.0 8.9 %collective-permute-start.6 = (bf16[192,640]{1,0:T(8,128)(2,1)S(1)}, bf16[192,640]{1,0:T(8,128)(2,1)S(1)}, u32[]{:S(2)}, u32[]{:S(2)}) collective-permute-start(bf16[192,640]{1,0:T(8,128)(2,1)S(1)} %pad_maximum_fusion.10), channel_id=1, source_target_pairs={{0,8},{4,12},{8,0},{12,4},{16,24},{20,28},{24,16},{28,20},{1,9},{5... | collective-permute-start | bytes 737288 | tf_op jit(solution)/shard_map/ppermute | solution.py:652
  26.2 9.2 %collective-permute-start.2 = (bf16[64,896]{1,0:T(8,128)(2,1)S(1)}, bf16[64,896]{1,0:T(8,128)(2,1)S(1)}, u32[]{:S(2)}, u32[]{:S(2)}) collective-permute-start(bf16[64,896]{1,0:T(8,128)(2,1)S(1)} %pad_maximum_fusion.12), channel_id=1, source_target_pairs={{0,4},{4,0},{8,12},{12,8},{16,20},{20,16},{24,28},{28,24},{1,5},{5... | collective-permute-start | bytes 344072 | tf_op jit(solution)/shard_map/ppermute | solution.py:652
  28.5 15.8 %copy-start.58 = (bf16[256,896]{1,0:T(8,128)(2,1)S(1)}, bf16[256,896]{1,0:T(8,128)(2,1)}, u32[]{:S(2)}) copy-start(bf16[256,896]{1,0:T(8,128)(2,1)} %get-tuple-element.204) | copy-start | bytes 1376260
  28.5 15.9 %collective-permute-start.9 = (bf16[192,1024]{1,0:T(8,128)(2,1)S(1)}, bf16[192,1024]{1,0:T(8,128)(2,1)S(1)}, u32[]{:S(2)}, u32[]{:S(2)}) collective-permute-start(bf16[192,1024]{1,0:T(8,128)(2,1)S(1)} %pad_maximum_fusion.9), channel_id=1, source_target_pairs={{0,8},{4,12},{8,0},{12,4},{16,24},{20,28},{24,16},{28,20},{1,9},{5... | collective-permute-start | bytes 1179656 | tf_op jit(solution)/shard_map/ppermute | solution.py:652
  31.9 8.8 %collective-permute-start.10 = (bf16[96,768]{1,0:T(8,128)(2,1)S(1)}, bf16[96,768]{1,0:T(8,128)(2,1)S(1)}, u32[]{:S(2)}, u32[]{:S(2)}) collective-permute-start(bf16[96,768]{1,0:T(8,128)(2,1)S(1)} %convert_bitcast_fusion), channel_id=1, source_target_pairs={{0,16},{4,20},{8,24},{12,28},{16,0},{20,4},{24,8},{28,12},{1,17},{... | collective-permute-start | bytes 442376 | tf_op jit(solution)/shard_map/ppermute | solution.py:652
  35.4 8.6 %collective-permute-start.3 = (bf16[128,896]{1,0:T(8,128)(2,1)S(1)}, bf16[128,896]{1,0:T(8,128)(2,1)S(1)}, u32[]{:S(2)}, u32[]{:S(2)}) collective-permute-start(bf16[128,896]{1,0:T(8,128)(2,1)S(1)} %pad_maximum_fusion.11), channel_id=1, source_target_pairs={{0,2},{1,3},{2,0},{3,1},{4,6},{5,7},{6,4},{7,5},{8,10},{9,11},{10,... | collective-permute-start | bytes 688136 | tf_op jit(solution)/shard_map/ppermute | solution.py:652
  37.0 24.9 %collective-permute-start.7 = (bf16[384,640]{1,0:T(8,128)(2,1)S(1)}, bf16[384,640]{1,0:T(8,128)(2,1)S(1)}, u32[]{:S(2)}, u32[]{:S(2)}) collective-permute-start(bf16[384,640]{1,0:T(8,128)(2,1)S(1)} %pad_maximum_fusion.8), channel_id=1, source_target_pairs={{0,4},{4,0},{8,12},{12,8},{16,20},{20,16},{24,28},{28,24},{1,5},{5... | collective-permute-start | bytes 1474568 | tf_op jit(solution)/shard_map/ppermute | solution.py:652
  40.8 19.0 %collective-permute-start.11 = (bf16[192,768]{1,0:T(8,128)(2,1)S(1)}, bf16[192,768]{1,0:T(8,128)(2,1)S(1)}, u32[]{:S(2)}, u32[]{:S(2)}) collective-permute-start(bf16[192,768]{1,0:T(8,128)(2,1)S(1)} %constant_dynamic-update-slice_fusion.11), channel_id=1, source_target_pairs={{0,4},{4,0},{8,12},{12,8},{16,20},{20,16},{24,28},{28,24},{1,5},{5... | collective-permute-start | bytes 884744 | tf_op jit(solution)/shard_map/ppermute | solution.py:652
  42.5 17.3 %collective-permute-start.12 = (bf16[192,768]{1,0:T(8,128)(2,1)S(1)}, bf16[192,768]{1,0:T(8,128)(2,1)S(1)}, u32[]{:S(2)}, u32[]{:S(2)}) collective-permute-start(bf16[192,768]{1,0:T(8,128)(2,1)S(1)} %constant_dynamic-update-slice_fusion.11), channel_id=1, source_target_pairs={{0,2},{1,3},{2,0},{3,1},{4,6},{5,7},{6,4},{7,5},{8,10},{9,11},{10,... | collective-permute-start | bytes 884744 | tf_op jit(solution)/shard_map/ppermute | solution.py:652
  44.0 17.3 %collective-permute-start.13 = (bf16[192,768]{1,0:T(8,128)(2,1)S(1)}, bf16[192,768]{1,0:T(8,128)(2,1)S(1)}, u32[]{:S(2)}, u32[]{:S(2)}) collective-permute-start(bf16[192,768]{1,0:T(8,128)(2,1)S(1)} %constant_dynamic-update-slice_fusion.11), channel_id=1, source_target_pairs={{0,6},{1,7},{2,4},{3,5},{4,2},{5,3},{6,0},{7,1},{8,14},{9,15},{10,... | collective-permute-start | bytes 884744 | tf_op jit(solution)/shard_map/ppermute | solution.py:663
  44.4 18.8 %copy-start.29 = (bf16[512,896]{1,0:T(8,128)(2,1)}, bf16[512,896]{1,0:T(8,128)(2,1)S(1)}, u32[]{:S(2)}) copy-start(bf16[512,896]{1,0:T(8,128)(2,1)S(1)} %get-tuple-element.198) | copy-start | bytes 2752516
  44.5 20.4 %collective-permute-start.4 = (bf16[256,896]{1,0:T(8,128)(2,1)S(1)}, bf16[256,896]{1,0:T(8,128)(2,1)S(1)}, u32[]{:S(2)}, u32[]{:S(2)}) collective-permute-start(bf16[256,896]{1,0:T(8,128)(2,1)S(1)} %get-tuple-element.197), channel_id=1, source_target_pairs={{0,1},{1,0},{2,3},{3,2},{4,5},{5,4},{6,7},{7,6},{8,9},{9,8},{10,11... | collective-permute-start | bytes 1376264 | tf_op jit(solution)/shard_map/ppermute | solution.py:652
  59.8 17.2 %collective-permute-start.14 = (bf16[384,1024]{1,0:T(8,128)(2,1)}, bf16[384,1024]{1,0:T(8,128)(2,1)}, u32[]{:S(2)}, u32[]{:S(2)}) collective-permute-start(bf16[384,1024]{1,0:T(8,128)(2,1)} %pad_maximum_fusion.7.refs_0_.refs_4_), channel_id=1, source_target_pairs={{0,1},{1,0},{2,3},{3,2},{4,5},{5,4},{6,7},{7,6},{8,9},{9,8},{10,11... | collective-permute-start | bytes 2359304 | tf_op jit(solution)/shard_map/ppermute | solution.py:652
  59.8 58.2 %collective-permute-start.19 = (bf16[384,1024]{1,0:T(8,128)(2,1)}, bf16[384,1024]{1,0:T(8,128)(2,1)}, u32[]{:S(2)}, u32[]{:S(2)}) collective-permute-start(bf16[384,1024]{1,0:T(8,128)(2,1)} %pad_maximum_fusion.7.refs_0_.refs_4_), channel_id=1, source_target_pairs={{0,4},{4,0},{8,12},{12,8},{16,20},{20,16},{24,28},{28,24},{1,5},{5... | collective-permute-start | bytes 2359304 | tf_op jit(solution)/shard_map/ppermute | solution.py:652
  61.3 57.6 %collective-permute-start.20 = (bf16[384,1024]{1,0:T(8,128)(2,1)}, bf16[384,1024]{1,0:T(8,128)(2,1)}, u32[]{:S(2)}, u32[]{:S(2)}) collective-permute-start(bf16[384,1024]{1,0:T(8,128)(2,1)} %pad_maximum_fusion.7.refs_0_.refs_4_), channel_id=1, source_target_pairs={{0,2},{1,3},{2,0},{3,1},{4,6},{5,7},{6,4},{7,5},{8,10},{9,11},{10,... | collective-permute-start | bytes 2359304 | tf_op jit(solution)/shard_map/ppermute | solution.py:652
  61.8 57.9 %collective-permute-start.21 = (bf16[384,1024]{1,0:T(8,128)(2,1)}, bf16[384,1024]{1,0:T(8,128)(2,1)}, u32[]{:S(2)}, u32[]{:S(2)}) collective-permute-start(bf16[384,1024]{1,0:T(8,128)(2,1)} %pad_maximum_fusion.7.refs_0_.refs_4_), channel_id=1, source_target_pairs={{0,6},{1,7},{2,4},{3,5},{4,2},{5,3},{6,0},{7,1},{8,14},{9,15},{10,... | collective-permute-start | bytes 2359304 | tf_op jit(solution)/shard_map/ppermute | solution.py:663
  63.4 14.9 %copy-start.5 = (bf16[4,192,768]{2,1,0:T(8,128)(2,1)}, bf16[4,192,768]{2,1,0:T(8,128)(2,1)S(1)}, u32[]{:S(2)}) copy-start(bf16[4,192,768]{2,1,0:T(8,128)(2,1)S(1)} %pad_maximum_fusion.refs_1_.refs_12_) | copy-start | bytes 3538948
  64.8 52.9 %collective-permute-start.15 = (bf16[4,192,768]{2,1,0:T(8,128)(2,1)S(1)}, bf16[4,192,768]{2,1,0:T(8,128)(2,1)}, u32[]{:S(2)}, u32[]{:S(2)}) collective-permute-start(bf16[4,192,768]{2,1,0:T(8,128)(2,1)S(1)} %pad_maximum_fusion.refs_1_.refs_12_), channel_id=1, source_target_pairs={{0,1},{1,0},{2,3},{3,2},{4,5},{5,4},{6,7},{7,6},{8,9},{9,8},{10,11... | collective-permute-start | bytes 3538952 | tf_op jit(solution)/shard_map/ppermute | solution.py:652
  76.9 40.8 %copy-start.18 = (bf16[1024,576]{1,0:T(8,128)(2,1)}, bf16[1024,576]{1,0:T(8,128)(2,1)S(1)}, u32[]{:S(2)}) copy-start(bf16[1024,576]{1,0:T(8,128)(2,1)S(1)} %fusion.10.qkv_ref) | copy-start | bytes 3538948
  76.9 42.8 %collective-permute-start.22 = (bf16[4,192,768]{2,1,0:T(8,128)(2,1)S(1)}, bf16[4,192,768]{2,1,0:T(8,128)(2,1)}, u32[]{:S(2)}, u32[]{:S(2)}) collective-permute-start(bf16[4,192,768]{2,1,0:T(8,128)(2,1)S(1)} %pad_maximum_fusion.refs_1_.refs_12_), channel_id=1, source_target_pairs={{0,8},{4,12},{8,0},{12,4},{16,24},{20,28},{24,16},{28,20},{1,9},{5... | collective-permute-start | bytes 3538952 | tf_op jit(solution)/shard_map/ppermute | solution.py:652
  117.8 2.0 collective-permute-start.16
  118.0 6.3 %collective-permute-start.17 = (bf16[256,192]{1,0:T(8,128)(2,1)S(1)}, bf16[256,192]{1,0:T(8,128)(2,1)S(1)}, u32[]{:S(2)}, u32[]{:S(2)}) collective-permute-start(bf16[256,192]{1,0:T(8,128)(2,1)S(1)} %get-tuple-element.191), channel_id=1, source_target_pairs={{0,2},{1,3},{2,0},{3,1},{4,6},{5,7},{6,4},{7,5},{8,10},{9,11},{10,... | collective-permute-start | bytes 294920 | tf_op jit(solution)/shard_map/ppermute | solution.py:652
  118.9 7.2 %collective-permute-start.18 = (bf16[256,192]{1,0:T(8,128)(2,1)S(1)}, bf16[256,192]{1,0:T(8,128)(2,1)S(1)}, u32[]{:S(2)}, u32[]{:S(2)}) collective-permute-start(bf16[256,192]{1,0:T(8,128)(2,1)S(1)} %get-tuple-element.190), channel_id=1, source_target_pairs={{0,3},{1,2},{2,1},{3,0},{4,7},{5,6},{6,5},{7,4},{8,11},{9,10},{10,... | collective-permute-start | bytes 294920 | tf_op jit(solution)/shard_map/ppermute | solution.py:652
  126.2 6.7 %collective-permute-start.26 = (bf16[4,192,768]{2,1,0:T(8,128)(2,1)}, bf16[4,192,768]{2,1,0:T(8,128)(2,1)}, u32[]{:S(2)}, u32[]{:S(2)}) collective-permute-start(bf16[4,192,768]{2,1,0:T(8,128)(2,1)} %collective-permute-done.22.refs_13_), channel_id=1, source_target_pairs={{0,1},{1,0},{2,3},{3,2},{4,5},{5,4},{6,7},{7,6},{8,9},{9,8},{10,11... | collective-permute-start | bytes 3538952 | tf_op jit(solution)/shard_map/ppermute | solution.py:652
  128.0 3.7 %collective-permute-start.23 = (bf16[384,1024]{1,0:T(8,128)(2,1)}, bf16[384,1024]{1,0:T(8,128)(2,1)S(1)}, u32[]{:S(2)}, u32[]{:S(2)}) collective-permute-start(bf16[384,1024]{1,0:T(8,128)(2,1)} %collective-permute-done.19.refs_5_), channel_id=1, source_target_pairs={{0,1},{1,0},{2,3},{3,2},{4,5},{5,4},{6,7},{7,6},{8,9},{9,8},{10,11... | collective-permute-start | bytes 2359304 | tf_op jit(solution)/shard_map/ppermute | solution.py:652
  128.3 3.4 %collective-permute-start.24 = (bf16[384,1024]{1,0:T(8,128)(2,1)}, bf16[384,1024]{1,0:T(8,128)(2,1)S(1)}, u32[]{:S(2)}, u32[]{:S(2)}) collective-permute-start(bf16[384,1024]{1,0:T(8,128)(2,1)} %collective-permute-done.20.refs_6_), channel_id=1, source_target_pairs={{0,1},{1,0},{2,3},{3,2},{4,5},{5,4},{6,7},{7,6},{8,9},{9,8},{10,11... | collective-permute-start | bytes 2359304 | tf_op jit(solution)/shard_map/ppermute | solution.py:652
  128.6 4.2 %collective-permute-start.25 = (bf16[384,1024]{1,0:T(8,128)(2,1)}, bf16[384,1024]{1,0:T(8,128)(2,1)S(1)}, u32[]{:S(2)}, u32[]{:S(2)}) collective-permute-start(bf16[384,1024]{1,0:T(8,128)(2,1)} %collective-permute-done.21.refs_7_), channel_id=1, source_target_pairs={{0,1},{1,0},{2,3},{3,2},{4,5},{5,4},{6,7},{7,6},{8,9},{9,8},{10,11... | collective-permute-start | bytes 2359304 | tf_op jit(solution)/shard_map/ppermute | solution.py:652
  133.7 22.0 %copy-start.44 = (f32[192,96]{1,0:T(8,128)S(1)}, f32[192,96]{1,0:T(8,128)}, u32[]{:S(2)}) copy-start(f32[192,96]{1,0:T(8,128)} %param.33) | copy-start | bytes 221188
  133.7 22.7 %copy-start.45 = (f32[192,96]{1,0:T(8,128)S(1)}, f32[192,96]{1,0:T(8,128)}, u32[]{:S(2)}) copy-start(f32[192,96]{1,0:T(8,128)} %param.34) | copy-start | bytes 221188
  155.2 10.1 %collective-permute-start.30 = (bf16[2,768,1024]{2,1,0:T(8,128)(2,1)}, bf16[2,768,1024]{2,1,0:T(8,128)(2,1)}, u32[]{:S(2)}, u32[]{:S(2)}) collective-permute-start(bf16[2,768,1024]{2,1,0:T(8,128)(2,1)} %get-tuple-element.80), channel_id=1, source_target_pairs={{0,1},{1,0},{2,3},{3,2},{4,5},{5,4},{6,7},{7,6},{8,9},{9,8},{10,11... | collective-permute-start | bytes 9437192 | tf_op jit(solution)/shard_map/ppermute | solution.py:652
  155.4 9.9 %collective-permute-start.31 = (bf16[2,768,768]{2,1,0:T(8,128)(2,1)}, bf16[2,768,768]{2,1,0:T(8,128)(2,1)}, u32[]{:S(2)}, u32[]{:S(2)}) collective-permute-start(bf16[2,768,768]{2,1,0:T(8,128)(2,1)} %get-tuple-element.81), channel_id=1, source_target_pairs={{0,1},{1,0},{2,3},{3,2},{4,5},{5,4},{6,7},{7,6},{8,9},{9,8},{10,11... | collective-permute-start | bytes 7077896 | tf_op jit(solution)/shard_map/ppermute | solution.py:652
  157.2 4.1 %collective-permute-start.27 = (bf16[256,192]{1,0:T(8,128)(2,1)S(1)}, bf16[256,192]{1,0:T(8,128)(2,1)S(1)}, u32[]{:S(2)}, u32[]{:S(2)}) collective-permute-start(bf16[256,192]{1,0:T(8,128)(2,1)S(1)} %get-tuple-element.76), channel_id=1, source_target_pairs={{0,1},{1,0},{2,3},{3,2},{4,5},{5,4},{6,7},{7,6},{8,9},{9,8},{10,11... | collective-permute-start | bytes 294920 | tf_op jit(solution)/shard_map/ppermute | solution.py:652
  157.4 6.3 %collective-permute-start.28 = (bf16[256,192]{1,0:T(8,128)(2,1)S(1)}, bf16[256,192]{1,0:T(8,128)(2,1)S(1)}, u32[]{:S(2)}, u32[]{:S(2)}) collective-permute-start(bf16[256,192]{1,0:T(8,128)(2,1)S(1)} %get-tuple-element.77), channel_id=1, source_target_pairs={{0,2},{1,3},{2,0},{3,1},{4,6},{5,7},{6,4},{7,5},{8,10},{9,11},{10,... | collective-permute-start | bytes 294920 | tf_op jit(solution)/shard_map/ppermute | solution.py:652
  158.3 6.9 %collective-permute-start.29 = (bf16[256,192]{1,0:T(8,128)(2,1)S(1)}, bf16[256,192]{1,0:T(8,128)(2,1)S(1)}, u32[]{:S(2)}, u32[]{:S(2)}) collective-permute-start(bf16[256,192]{1,0:T(8,128)(2,1)S(1)} %get-tuple-element.78), channel_id=1, source_target_pairs={{0,3},{1,2},{2,1},{3,0},{4,7},{5,6},{6,5},{7,4},{8,11},{9,10},{10,... | collective-permute-start | bytes 294920 | tf_op jit(solution)/shard_map/ppermute | solution.py:652
  167.3 42.3 %collective-permute-start.35 = (bf16[2,2,192,768]{3,2,1,0:T(8,128)(2,1)S(1)}, bf16[2,2,192,768]{3,2,1,0:T(8,128)(2,1)S(1)}, u32[]{:S(2)}, u32[]{:S(2)}) collective-permute-start(bf16[2,2,192,768]{3,2,1,0:T(8,128)(2,1)S(1)} %fusion.13.refs_3_), channel_id=1, source_target_pairs={{0,8},{4,12},{8,0},{12,4},{16,24},{20,28},{24,16},{28,20},{1,9},{5... | collective-permute-start | bytes 3538952 | tf_op jit(solution)/shard_map/ppermute | solution.py:652
  171.5 35.8 %collective-permute-start.32 = (bf16[384,1024]{1,0:T(8,128)(2,1)S(1)}, bf16[384,1024]{1,0:T(8,128)(2,1)S(1)}, u32[]{:S(2)}, u32[]{:S(2)}) collective-permute-start(bf16[384,1024]{1,0:T(8,128)(2,1)S(1)} %get-tuple-element.186.refs_0_), channel_id=1, source_target_pairs={{0,4},{4,0},{8,12},{12,8},{16,20},{20,16},{24,28},{28,24},{1,5},{5... | collective-permute-start | bytes 2359304 | tf_op jit(solution)/shard_map/ppermute | solution.py:652
  171.8 35.5 %collective-permute-start.33 = (bf16[384,1024]{1,0:T(8,128)(2,1)}, bf16[384,1024]{1,0:T(8,128)(2,1)S(1)}, u32[]{:S(2)}, u32[]{:S(2)}) collective-permute-start(bf16[384,1024]{1,0:T(8,128)(2,1)} %get-tuple-element.185.refs_1_), channel_id=1, source_target_pairs={{0,2},{1,3},{2,0},{3,1},{4,6},{5,7},{6,4},{7,5},{8,10},{9,11},{10,... | collective-permute-start | bytes 2359304 | tf_op jit(solution)/shard_map/ppermute | solution.py:652
  172.5 37.1 %collective-permute-start.34 = (bf16[384,1024]{1,0:T(8,128)(2,1)S(1)}, bf16[384,1024]{1,0:T(8,128)(2,1)S(1)}, u32[]{:S(2)}, u32[]{:S(2)}) collective-permute-start(bf16[384,1024]{1,0:T(8,128)(2,1)S(1)} %get-tuple-element.184.refs_2_), channel_id=1, source_target_pairs={{0,6},{1,7},{2,4},{3,5},{4,2},{5,3},{6,0},{7,1},{8,14},{9,15},{10,... | collective-permute-start | bytes 2359304 | tf_op jit(solution)/shard_map/ppermute | solution.py:663
  212.8 23.6 %collective-permute-start.43 = (bf16[192,768]{1,0:T(8,128)(2,1)S(1)}, bf16[192,768]{1,0:T(8,128)(2,1)}, u32[]{:S(2)}, u32[]{:S(2)}) collective-permute-start(bf16[192,768]{1,0:T(8,128)(2,1)S(1)} %get-tuple-element.189.refs_1_), channel_id=1, source_target_pairs={{0,4},{4,0},{8,12},{12,8},{16,20},{20,16},{24,28},{28,24},{1,5},{5... | collective-permute-start | bytes 884744 | tf_op jit(solution)/shard_map/ppermute | solution.py:652
  213.2 24.1 %collective-permute-start.44 = (bf16[192,768]{1,0:T(8,128)(2,1)S(1)}, bf16[192,768]{1,0:T(8,128)(2,1)}, u32[]{:S(2)}, u32[]{:S(2)}) collective-permute-start(bf16[192,768]{1,0:T(8,128)(2,1)S(1)} %get-tuple-element.188.refs_2_), channel_id=1, source_target_pairs={{0,2},{1,3},{2,0},{3,1},{4,6},{5,7},{6,4},{7,5},{8,10},{9,11},{10,... | collective-permute-start | bytes 884744 | tf_op jit(solution)/shard_map/ppermute | solution.py:652
  214.1 23.3 %collective-permute-start.45 = (bf16[192,768]{1,0:T(8,128)(2,1)S(1)}, bf16[192,768]{1,0:T(8,128)(2,1)}, u32[]{:S(2)}, u32[]{:S(2)}) collective-permute-start(bf16[192,768]{1,0:T(8,128)(2,1)S(1)} %get-tuple-element.187.refs_3_), channel_id=1, source_target_pairs={{0,6},{1,7},{2,4},{3,5},{4,2},{5,3},{6,0},{7,1},{8,14},{9,15},{10,... | collective-permute-start | bytes 884744 | tf_op jit(solution)/shard_map/ppermute | solution.py:663
  230.0 9.9 %collective-permute-start.41 = (bf16[192,1024]{1,0:T(8,128)(2,1)}, bf16[192,1024]{1,0:T(8,128)(2,1)}, u32[]{:S(2)}, u32[]{:S(2)}) collective-permute-start(bf16[192,1024]{1,0:T(8,128)(2,1)} %slice.383), channel_id=1, source_target_pairs={{0,8},{4,12},{8,0},{12,4},{16,24},{20,28},{24,16},{28,20},{1,9},{5... | collective-permute-start | bytes 1179656 | tf_op jit(solution)/shard_map/ppermute | solution.py:652
  235.4 7.9 %collective-permute-start.47 = (bf16[256,896]{1,0:T(8,128)(2,1)S(1)}, bf16[256,896]{1,0:T(8,128)(2,1)S(1)}, u32[]{:S(2)}, u32[]{:S(2)}) collective-permute-start(bf16[256,896]{1,0:T(8,128)(2,1)S(1)} %slice.391), channel_id=1, source_target_pairs={{0,1},{1,0},{2,3},{3,2},{4,5},{5,4},{6,7},{7,6},{8,9},{9,8},{10,11... | collective-permute-start | bytes 1376264 | tf_op jit(solution)/shard_map/ppermute | solution.py:652
  236.4 13.7 %collective-permute-start.38 = (bf16[384,640]{1,0:T(8,128)(2,1)S(1)}, bf16[384,640]{1,0:T(8,128)(2,1)S(1)}, u32[]{:S(2)}, u32[]{:S(2)}) collective-permute-start(bf16[384,640]{1,0:T(8,128)(2,1)S(1)} %copy-done.16), channel_id=1, source_target_pairs={{0,4},{4,0},{8,12},{12,8},{16,20},{20,16},{24,28},{28,24},{1,5},{5... | collective-permute-start | bytes 1474568 | tf_op jit(solution)/shard_map/ppermute | solution.py:652
  237.3 29.3 %collective-permute-start.36 = (bf16[2,256,768]{2,1,0:T(8,128)(2,1)}, bf16[2,256,768]{2,1,0:T(8,128)(2,1)}, u32[]{:S(2)}, u32[]{:S(2)}) collective-permute-start(bf16[2,256,768]{2,1,0:T(8,128)(2,1)} %slice.312), channel_id=1, source_target_pairs={{0,1},{1,0},{2,3},{3,2},{4,5},{5,4},{6,7},{7,6},{8,9},{9,8},{10,11... | collective-permute-start | bytes 2359304 | tf_op jit(solution)/shard_map/ppermute | solution.py:652
  239.1 11.0 %copy-start.13 = (bf16[384,640]{1,0:T(8,128)(2,1)S(1)}, bf16[384,640]{1,0:T(8,128)(2,1)}, u32[]{:S(2)}) copy-start(bf16[384,640]{1,0:T(8,128)(2,1)} %copy-done.12) | copy-start | bytes 1474564
  239.1 14.7 %collective-permute-start.46 = (bf16[96,768]{1,0:T(8,128)(2,1)S(1)}, bf16[96,768]{1,0:T(8,128)(2,1)S(1)}, u32[]{:S(2)}, u32[]{:S(2)}) collective-permute-start(bf16[96,768]{1,0:T(8,128)(2,1)S(1)} %slice.388), channel_id=1, source_target_pairs={{0,16},{4,20},{8,24},{12,28},{16,0},{20,4},{24,8},{28,12},{1,17},{... | collective-permute-start | bytes 442376 | tf_op jit(solution)/shard_map/ppermute | solution.py:652
  241.0 16.8 %collective-permute-start.42 = (bf16[96,1024]{1,0:T(8,128)(2,1)S(1)}, bf16[96,1024]{1,0:T(8,128)(2,1)S(1)}, u32[]{:S(2)}, u32[]{:S(2)}) collective-permute-start(bf16[96,1024]{1,0:T(8,128)(2,1)S(1)} %slice.385), channel_id=1, source_target_pairs={{0,16},{4,20},{8,24},{12,28},{16,0},{20,4},{24,8},{28,12},{1,17},{... | collective-permute-start | bytes 589832 | tf_op jit(solution)/shard_map/ppermute | solution.py:652
  243.5 8.2 %collective-permute-start.48 = (bf16[128,896]{1,0:T(8,128)(2,1)S(1)}, bf16[128,896]{1,0:T(8,128)(2,1)S(1)}, u32[]{:S(2)}, u32[]{:S(2)}) collective-permute-start(bf16[128,896]{1,0:T(8,128)(2,1)S(1)} %slice.393), channel_id=1, source_target_pairs={{0,2},{1,3},{2,0},{3,1},{4,6},{5,7},{6,4},{7,5},{8,10},{9,11},{10,... | collective-permute-start | bytes 688136 | tf_op jit(solution)/shard_map/ppermute | solution.py:652
  251.0 12.4 %collective-permute-start.39 = (bf16[192,640]{1,0:T(8,128)(2,1)}, bf16[192,640]{1,0:T(8,128)(2,1)}, u32[]{:S(2)}, u32[]{:S(2)}) collective-permute-start(bf16[192,640]{1,0:T(8,128)(2,1)} %slice.376), channel_id=1, source_target_pairs={{0,8},{4,12},{8,0},{12,4},{16,24},{20,28},{24,16},{28,20},{1,9},{5... | collective-permute-start | bytes 737288 | tf_op jit(solution)/shard_map/ppermute | solution.py:652
  252.5 12.0 %collective-permute-start.49 = (bf16[64,896]{1,0:T(8,128)(2,1)}, bf16[64,896]{1,0:T(8,128)(2,1)}, u32[]{:S(2)}, u32[]{:S(2)}) collective-permute-start(bf16[64,896]{1,0:T(8,128)(2,1)} %slice.398), channel_id=1, source_target_pairs={{0,4},{4,0},{8,12},{12,8},{16,20},{20,16},{24,28},{28,24},{1,5},{5... | collective-permute-start | bytes 344072 | tf_op jit(solution)/shard_map/ppermute | solution.py:652
  264.4 8.4 %collective-permute-start.40 = (bf16[96,640]{1,0:T(8,128)(2,1)S(1)}, bf16[96,640]{1,0:T(8,128)(2,1)S(1)}, u32[]{:S(2)}, u32[]{:S(2)}) collective-permute-start(bf16[96,640]{1,0:T(8,128)(2,1)S(1)} %slice.378), channel_id=1, source_target_pairs={{0,16},{4,20},{8,24},{12,28},{16,0},{20,4},{24,8},{28,12},{1,17},{... | collective-permute-start | bytes 368648 | tf_op jit(solution)/shard_map/ppermute | solution.py:652
  265.4 6.8 %collective-permute-start.50 = (bf16[32,896]{1,0:T(8,128)(2,1)S(1)}, bf16[32,896]{1,0:T(8,128)(2,1)S(1)}, u32[]{:S(2)}, u32[]{:S(2)}) collective-permute-start(bf16[32,896]{1,0:T(8,128)(2,1)S(1)} %slice.400), channel_id=1, source_target_pairs={{0,8},{4,12},{8,0},{12,4},{16,24},{20,28},{24,16},{28,20},{1,9},{5... | collective-permute-start | bytes 172040 | tf_op jit(solution)/shard_map/ppermute | solution.py:652
  268.0 10.8 %collective-permute-start.37 = (bf16[1,256,768]{2,1,0:T(8,128)(2,1)S(1)}, bf16[1,256,768]{2,1,0:T(8,128)(2,1)S(1)}, u32[]{:S(2)}, u32[]{:S(2)}) collective-permute-start(bf16[1,256,768]{2,1,0:T(8,128)(2,1)S(1)} %slice.374), channel_id=1, source_target_pairs={{0,2},{1,3},{2,0},{3,1},{4,6},{5,7},{6,4},{7,5},{8,10},{9,11},{10,... | collective-permute-start | bytes 1179656 | tf_op jit(solution)/shard_map/ppermute | solution.py:652
  272.3 4.8 %collective-permute-start.51 = (bf16[16,896]{1,0:T(8,128)(2,1)S(1)}, bf16[16,896]{1,0:T(8,128)(2,1)S(1)}, u32[]{:S(2)}, u32[]{:S(2)}) collective-permute-start(bf16[16,896]{1,0:T(8,128)(2,1)S(1)} %slice.402), channel_id=1, source_target_pairs={{0,16},{4,20},{8,24},{12,28},{16,0},{20,4},{24,8},{28,12},{1,17},{... | collective-permute-start | bytes 86024 | tf_op jit(solution)/shard_map/ppermute | solution.py:652
  (54 other events, 243.6 us)

commit v2 on v1

--- a/solution.py
+++ b/solution.py
@@ -893,7 +893,7 @@
     grad_context = exchange(dict(zip(differences, grad_context)))
     grad_context = jnp.concatenate([grad_context[o] for o in differences], axis=0)
     up_got, down_got, _ = lax.optimization_barrier(
-        (swap(up_send, core), swap(down_send, core), grad_context)
+        (swap(up_send, core), swap(down_send, core), grad_context[:quarter])
     )
     lower, upper = slice(0, half), slice(half, D)
     up_stays, up_low, up_far, up_both = (

time: 282 us -> 281 us (level)
  starting transfers between devices: 49.1 us -> 52.1 us
  Pallas kernels: 99 us -> 96.1 us
    ppermute x48, starting transfers between devices: 42.5 us -> 47.4 us  [swap(): lax.ppermute(values, axis, [(i, i ^ bit) for i in range(lax.axis_size(axi...]
    unnamed x146 -> x143, local copies, waits for them, and re-layouts: 16.8 us -> 16.4 us
  transfers between devices with their start and end apart: 52 -> 52, of which waited for: 18 -> 19; matrix products, arithmetic and copies ran while one was open for 21% -> 21% of each run, Pallas kernels for 28% -> 27%
where the time goes in v2:
time: 281 us; the launch traced here: 279 us
  Pallas kernels  96.1 us (34%)
  waiting for transfers between devices  56.2 us (20%)
  starting transfers between devices  52.1 us (19%)
  other arithmetic  29.6 us (11%)
  local copies, waits for them, and re-layouts  24.4 us (9%)
  matrix products  18.7 us (7%)
    ppermute x48, waiting for transfers between devices, swap(): lax.ppermute(values, axis, [(i, i ^ bit) for i in range(lax.axis_size(axi...  53.1 us
    ppermute x48, starting transfers between devices, swap(): lax.ppermute(values, axis, [(i, i ^ bit) for i in range(lax.axis_size(axi...  47.4 us
    pallas_call x1, Pallas kernels, attention_forward(): pl.pallas_call(functools.partial(forward_kernel, owners=owners), out_shap...  37.9 us
    pallas_call x1, Pallas kernels, attention_backward(): pl.pallas_call(functools.partial(backward_kernel, owners=owners), out_sha...  31.1 us
    pallas_call x1, Pallas kernels, middle(): pl.pallas_call(middle_kernel, out_shape=(shape((rows, width), HALF), shap...  20.5 us
    dot_general x8, matrix products, dot(): return lax.dot_general(left, right, dims, preferred_element_type=FULL)  18.7 us
    unnamed x143, local copies, waits for them, and re-layouts  16.4 us
    convert_element_type x6, other arithmetic, add(): return sum((part.astype(FULL) for part in parts)).astype(HALF)  11.8 us
  transfers between devices with their start and end apart: 52, of which 19 were waited for; matrix products, arithmetic and copies ran while one was open for 21% of the time, Pallas kernels for 27%

profile of v2, /device:TPU:0, one launch (start us, length us, event | category | flops | bytes accessed | tf_op | source)
XLA Modules:
  0.0 279.2 jit_solution(13465522347496330662)
XLA Ops:
  0.7 1.0 convert.22
  1.9 4.1 %collective-permute-start.5 = (bf16[96,640]{1,0:T(8,128)(2,1)S(1)}, bf16[96,640]{1,0:T(8,128)(2,1)S(1)}, u32[]{:S(2)}, u32[]{:S(2)}) collective-permute-start(bf16[96,640]{1,0:T(8,128)(2,1)S(1)} %fusion.36), channel_id=1, source_target_pairs={{0,16},{4,20},{8,24},{12,28},{16,0},{20,4},{24,8},{28,12},{1,17},{... | collective-permute-start | bytes 368648 | tf_op jit(solution)/shard_map/ppermute | solution.py:652
  9.8 2.9 %collective-permute-start = (bf16[16,896]{1,0:T(8,128)(2,1)S(1)}, bf16[16,896]{1,0:T(8,128)(2,1)S(1)}, u32[]{:S(2)}, u32[]{:S(2)}) collective-permute-start(bf16[16,896]{1,0:T(8,128)(2,1)S(1)} %get-tuple-element.219), channel_id=1, source_target_pairs={{0,16},{4,20},{8,24},{12,28},{16,0},{20,4},{24,8},{28,12},{1,17},{... | collective-permute-start | bytes 86024 | tf_op jit(solution)/shard_map/ppermute | solution.py:652
  13.0 4.1 %fusion.5.inputs_ref = bf16[768,1024]{1,0:T(8,128)(2,1)} fusion(bf16[1024,768]{1,0:T(8,128)(2,1)} %param.26, s32[768]{0:T(1024)S(1)} %add.292), kind=kOutput, calls=%fused_computation.9 | convolution fusion | flops 1209335808 | bytes 3148800 | tf_op jit(solution)/shard_map/dot_general | solution.py:37
  17.1 1.9 constant_dynamic-slice_fusion
  19.2 2.4 collective-permute-done
  23.0 1.4 collective-permute-start.6
  24.3 1.9 collective-permute-done.1
  26.2 1.7 collective-permute-start.2
  29.4 2.5 collective-permute-done.6
  31.9 3.4 %collective-permute-start.10 = (bf16[96,768]{1,0:T(8,128)(2,1)S(1)}, bf16[96,768]{1,0:T(8,128)(2,1)S(1)}, u32[]{:S(2)}, u32[]{:S(2)}) collective-permute-start(bf16[96,768]{1,0:T(8,128)(2,1)S(1)} %convert_bitcast_fusion), channel_id=1, source_target_pairs={{0,16},{4,20},{8,24},{12,28},{16,0},{20,4},{24,8},{28,12},{1,17},{... | collective-permute-start | bytes 442376 | tf_op jit(solution)/shard_map/ppermute | solution.py:652
  35.4 1.6 collective-permute-start.3
  37.0 1.5 collective-permute-start.7
  38.5 2.3 collective-permute-done.10
  40.8 1.7 collective-permute-start.11
  42.5 1.5 collective-permute-start.12
  44.5 1.1 pad_maximum_fusion.7.refs_0_.refs_4_
  45.6 14.2 %collective-permute-done.11 = bf16[192,768]{1,0:T(8,128)(2,1)S(1)} collective-permute-done((bf16[192,768]{1,0:T(8,128)(2,1)S(1)}, bf16[192,768]{1,0:T(8,128)(2,1)S(1)}, u32[]{:S(2)}, u32[]{:S(2)}) %collective-permute-start.11) | collective-permute-done | bytes 294944 | tf_op jit(solution)/shard_map/ppermute | solution.py:652
  59.8 1.5 collective-permute-start.19
  61.8 1.4 collective-permute-start.21
  63.4 1.4 fusion.9.w_ref
  67.0 2.5 fusion.12
  69.5 4.5 %fusion.tab_ref = bf16[2048,384]{1,0:T(8,128)(2,1)} fusion(bf16[2048,512]{1,0:T(8,128)(2,1)} %constant.27.clone, bf16[512,384]{1,0:T(8,128)(2,1)} %fusion.12, s32[512]{0:T(512)S(1)} %add.302), kind=kOutput, calls=%fused_computation.2 | convolution fusion | flops 1007878144 | bytes 4065280 | tf_op jit(solution)/shard_map/dot_general | solution.py:37
  74.0 2.9 %fusion.10.qkv_ref = bf16[1024,576]{1,0:T(8,128)(2,1)S(1)} fusion(bf16[1024,768]{1,0:T(8,128)(2,1)} %param.26, bf16[768,576]{1,0:T(8,128)(2,1)S(1)} %fusion.9.w_ref, f32[576]{0:T(1024)S(1)} %pad_maximum_fusion.17), kind=kOutput, calls=%fused_computation.20 | convolution fusion | flops 907149312 | bytes 3639552 | tf_op jit(solution)/shard_map/dot_general | solution.py:37
  77.0 1.4 collective-permute-start.22
  78.4 37.9 %shard_map.401 = (bf16[1024,192]{1,0:T(8,128)(2,1)S(1)}, bf16[3,1024,1024]{2,1,0:T(8,128)(2,1)}) custom-call(s32[5]{0:T(128)S(1)} %pad_add_fusion.info, bf16[1024,576]{1,0:T(8,128)(2,1)S(1)} %fusion.10.qkv_ref, bf16[2048,384]{1,0:T(8,128)(2,1)S(1)} %copy-done.17, bf16[384,1024]{1,0:T(8,128)(2,1)} %pad_maximum_fusion.7.refs_0_.refs_4_, ...), custom_call_target="tpu_custom_call" | custom-call | flops 60000002048 | bytes 60000000 | tf_op jit(solution)/shard_map/pallas_call | solution.py:328
  118.3 4.5 %collective-permute-done.17.refs_2_ = bf16[256,192]{1,0:T(8,128)(2,1)S(1)} collective-permute-done((bf16[256,192]{1,0:T(8,128)(2,1)S(1)}, bf16[256,192]{1,0:T(8,128)(2,1)S(1)}, u32[]{:S(2)}, u32[]{:S(2)}) %collective-permute-start.17) | collective-permute-done | bytes 98336 | tf_op jit(solution)/shard_map/ppermute | solution.py:652
  122.8 1.9 collective-permute-done.18.refs_3_
  125.1 1.3 fusion.4.order_ref
  127.4 2.9 %fusion.11.refs_16_.normed_ref = bf16[768,512]{1,0:T(8,128)(2,1)} fusion(s32[768]{0:T(1024)S(1)} %add.292, f32[768]{0:T(1024)S(1)} %get-tuple-element.207, f32[768]{0:T(1024)S(1)} %get-tuple-element.206, bf16[512,896]{1,0:T(8,128)(2,1)} %copy-done.31), kind=kOutput, calls=%fused_computation.21 | convolution fusion | flops 606535680 | bytes 1582080 | tf_op jit(solution)/shard_map/dot_general | solution.py:37
  130.3 1.1 collective-permute-done.25.refs_11_
  132.2 20.5 %shard_map.402 = (bf16[256,768]{1,0:T(8,128)(2,1)}, f32[256,768]{1,0:T(8,128)S(1)}, f32[8,768]{1,0:T(8,128)S(1)}, f32[4,768]{1,0:T(4,128)S(1)}, bf16[256,192]{1,...) custom-call(s32[5]{0:T(128)S(1)} %pad_add_fusion.info, ...), custom_call_target="tpu_custom_call" | custom-call | flops 20000000000 | bytes 20000000 | tf_op jit(solution)/shard_map/pallas_call | solution.py:530
  157.5 2.2 collective-permute-done.27
  159.7 1.0 collective-permute-done.28
  160.7 1.5 collective-permute-done.29
  163.2 2.1 fusion.13.refs_3_
  166.1 3.6 %fusion.21 = (bf16[384,1024]{1,0:T(8,128)(2,1)S(1)}, bf16[384,1024]{1,0:T(8,128)(2,1)}, bf16[384,1024]{1,0:T(8,128)(2,1)S(1)}) fusion(bf16[2,768,1024]{2,1,0:T(8,128)(2,1)} %collective-permute-done.30, bf16[2,768,1024]{2,1,0:T(8,128)(2,1)S(1)} %copy-done.20), kind=kLoop, calls=%fused_computation.41 | loop fusion | flops 4718592 | bytes 7077888 | tf_op jit(solution)/shard_map/convert_element_type | solution.py:697
  169.7 1.5 collective-permute-start.32
  171.7 1.4 collective-permute-start.34
  173.2 31.1 %shard_map.403 = (bf16[1024,576]{1,0:T(8,128)(2,1)}, bf16[384,2048]{1,0:T(8,128)(2,1)}) custom-call(s32[5]{0:T(128)S(1)} %pad_add_fusion.info, bf16[1024,576]{1,0:T(8,128)(2,1)} %copy-done.18, bf16[2048,384]{1,0:T(8,128)(2,1)} %fusion.tab_ref, bf16[3,1024,1024]{2,1,0:T(8,128)(2,1)} %get-tuple-element.74.p_far, ...), custom_call_target="tpu_custom_call" | custom-call | flops 60000002048 | bytes 60000000 | tf_op jit(solution)/shard_map/pallas_call | solution.py:352
  204.3 3.1 %collective-permute-done.34 = bf16[384,1024]{1,0:T(8,128)(2,1)S(1)} collective-permute-done((bf16[384,1024]{1,0:T(8,128)(2,1)S(1)}, bf16[384,1024]{1,0:T(8,128)(2,1)S(1)}, u32[]{:S(2)}, u32[]{:S(2)}) %collective-permute-start.34) | collective-permute-done | bytes 786464 | tf_op jit(solution)/shard_map/ppermute | solution.py:663
  208.2 2.2 fusion.24
  210.4 1.6 collective-permute-start.43
  212.5 1.5 collective-permute-start.45
  214.0 2.2 fusion.8.refs_0_
  216.3 6.6 %shard_map.404 = (bf16[384,640]{1,0:T(8,128)(2,1)S(1)}, bf16[384,640]{1,0:T(8,128)(2,1)S(1)}, bf16[4,256,768]{2,1,0:T(8,128)(2,1)S(1)}, bf16[512,768]{1,0:T(8,128)(2,1)S(1)}, f32[16,768]{1,0:T(8,128)S(1)}) custom-call(s32[5]{0:T(128)S(1)} %pad_add_fusion.info, bf16[1024,576]{1,0:T(8,128)(2,1)S(1)} %copy-done.4, bf16[384,2048]{1,0:T(8,128)(2,1)S(1)} %copy-done.3, ...), custom_call_target="tpu_custom_call" | custom-call | flops 100000000 | bytes 100000 | tf_op jit(solution)/shard_map/pallas_call | solution.py:625
  222.9 1.2 copy-done
  227.6 1.3 collective-permute-start.41
  228.9 2.2 constant_dynamic-update-slice_fusion.14
  231.9 1.1 slice.391
  234.0 1.6 collective-permute-start.38
  235.8 1.6 add_convert_fusion.12
  237.4 1.7 collective-permute-start.46
  239.2 1.1 add_convert_fusion.9
  240.3 1.3 collective-permute-start.42
  242.3 5.4 %collective-permute-done.38 = bf16[384,640]{1,0:T(8,128)(2,1)S(1)} collective-permute-done((bf16[384,640]{1,0:T(8,128)(2,1)S(1)}, bf16[384,640]{1,0:T(8,128)(2,1)S(1)}, u32[]{:S(2)}, u32[]{:S(2)}) %collective-permute-start.38) | collective-permute-done | bytes 491552 | tf_op jit(solution)/shard_map/ppermute | solution.py:652
  250.0 1.5 collective-permute-start.49
  252.2 3.9 %collective-permute-done.42 = bf16[96,1024]{1,0:T(8,128)(2,1)S(1)} collective-permute-done((bf16[96,1024]{1,0:T(8,128)(2,1)S(1)}, bf16[96,1024]{1,0:T(8,128)(2,1)S(1)}, u32[]{:S(2)}, u32[]{:S(2)}) %collective-permute-start.42) | collective-permute-done | bytes 196640 | tf_op jit(solution)/shard_map/ppermute | solution.py:652
  259.5 2.1 multiply_add_fusion
  261.6 1.0 add_convert_fusion.13
  263.7 2.6 collective-permute-start.50
  266.3 1.3 add_convert_fusion.2
  268.1 3.1 %collective-permute-done.50 = bf16[32,896]{1,0:T(8,128)(2,1)S(1)} collective-permute-done((bf16[32,896]{1,0:T(8,128)(2,1)S(1)}, bf16[32,896]{1,0:T(8,128)(2,1)S(1)}, u32[]{:S(2)}, u32[]{:S(2)}) %collective-permute-start.50) | collective-permute-done | bytes 57376 | tf_op jit(solution)/shard_map/ppermute | solution.py:652
  272.7 3.5 %collective-permute-done.51 = bf16[16,896]{1,0:T(8,128)(2,1)S(1)} collective-permute-done((bf16[16,896]{1,0:T(8,128)(2,1)S(1)}, bf16[16,896]{1,0:T(8,128)(2,1)S(1)}, u32[]{:S(2)}, u32[]{:S(2)}) %collective-permute-start.51) | collective-permute-done | bytes 28704 | tf_op jit(solution)/shard_map/ppermute | solution.py:652
  (293 shorter events, 41.4 us)
Async XLA Ops:
  0.7 12.1 %copy-start.65 = (s32[8]{0:T(128)S(1)}, s32[8]{0:T(128)}, u32[]{:S(2)}) copy-start(s32[8]{0:T(128)} %constant.24.clone) | copy-start | bytes 100
  0.7 12.3 %copy-start.59 = (s32[32]{0:T(128)S(1)}, s32[32]{0:T(128)}, u32[]{:S(2)}) copy-start(s32[32]{0:T(128)} %constant.25.clone) | copy-start | bytes 388
  0.7 12.3 %copy-start.60 = (s32[32]{0:T(128)S(1)}, s32[32]{0:T(128)}, u32[]{:S(2)}) copy-start(s32[32]{0:T(128)} %constant.26.clone) | copy-start | bytes 388
  0.7 12.0 %copy-start.26 = (f32[768,96]{0,1:T(8,128)S(1)}, f32[768,96]{0,1:T(8,128)}, u32[]{:S(2)}) copy-start(f32[768,96]{0,1:T(8,128)} %param.38) | copy-start | bytes 884740
  1.9 21.1 %collective-permute-start.5 = (bf16[96,640]{1,0:T(8,128)(2,1)S(1)}, bf16[96,640]{1,0:T(8,128)(2,1)S(1)}, u32[]{:S(2)}, u32[]{:S(2)}) collective-permute-start(bf16[96,640]{1,0:T(8,128)(2,1)S(1)} %fusion.36), channel_id=1, source_target_pairs={{0,16},{4,20},{8,24},{12,28},{16,0},{20,4},{24,8},{28,12},{1,17},{... | collective-permute-start | bytes 368648 | tf_op jit(solution)/shard_map/ppermute | solution.py:652
  8.6 19.9 %collective-permute-start.8 = (bf16[96,1024]{1,0:T(8,128)(2,1)S(1)}, bf16[96,1024]{1,0:T(8,128)(2,1)S(1)}, u32[]{:S(2)}, u32[]{:S(2)}) collective-permute-start(bf16[96,1024]{1,0:T(8,128)(2,1)S(1)} %fusion.34), channel_id=1, source_target_pairs={{0,16},{4,20},{8,24},{12,28},{16,0},{20,4},{24,8},{28,12},{1,17},{... | collective-permute-start | bytes 589832 | tf_op jit(solution)/shard_map/ppermute | solution.py:652
  9.8 11.7 %collective-permute-start = (bf16[16,896]{1,0:T(8,128)(2,1)S(1)}, bf16[16,896]{1,0:T(8,128)(2,1)S(1)}, u32[]{:S(2)}, u32[]{:S(2)}) collective-permute-start(bf16[16,896]{1,0:T(8,128)(2,1)S(1)} %get-tuple-element.219), channel_id=1, source_target_pairs={{0,16},{4,20},{8,24},{12,28},{16,0},{20,4},{24,8},{28,12},{1,17},{... | collective-permute-start | bytes 86024 | tf_op jit(solution)/shard_map/ppermute | solution.py:652
  13.0 53.2 %copy-start.54 = (s32[32]{0:T(128)}, s32[32]{0:T(128)S(1)}, u32[]{:S(2)}) copy-start(s32[32]{0:T(128)S(1)} %get-tuple-element.181) | copy-start | bytes 388
  21.6 4.6 %collective-permute-start.1 = (bf16[32,896]{1,0:T(8,128)(2,1)S(1)}, bf16[32,896]{1,0:T(8,128)(2,1)S(1)}, u32[]{:S(2)}, u32[]{:S(2)}) collective-permute-start(bf16[32,896]{1,0:T(8,128)(2,1)S(1)} %pad_maximum_fusion.14), channel_id=1, source_target_pairs={{0,8},{4,12},{8,0},{12,4},{16,24},{20,28},{24,16},{28,20},{1,9},{5... | collective-permute-start | bytes 172040 | tf_op jit(solution)/shard_map/ppermute | solution.py:652
  23.0 8.9 %collective-permute-start.6 = (bf16[192,640]{1,0:T(8,128)(2,1)S(1)}, bf16[192,640]{1,0:T(8,128)(2,1)S(1)}, u32[]{:S(2)}, u32[]{:S(2)}) collective-permute-start(bf16[192,640]{1,0:T(8,128)(2,1)S(1)} %pad_maximum_fusion.11), channel_id=1, source_target_pairs={{0,8},{4,12},{8,0},{12,4},{16,24},{20,28},{24,16},{28,20},{1,9},{5... | collective-permute-start | bytes 737288 | tf_op jit(solution)/shard_map/ppermute | solution.py:652
  26.2 9.2 %collective-permute-start.2 = (bf16[64,896]{1,0:T(8,128)(2,1)S(1)}, bf16[64,896]{1,0:T(8,128)(2,1)S(1)}, u32[]{:S(2)}, u32[]{:S(2)}) collective-permute-start(bf16[64,896]{1,0:T(8,128)(2,1)S(1)} %pad_maximum_fusion.13), channel_id=1, source_target_pairs={{0,4},{4,0},{8,12},{12,8},{16,20},{20,16},{24,28},{28,24},{1,5},{5... | collective-permute-start | bytes 344072 | tf_op jit(solution)/shard_map/ppermute | solution.py:652
  28.5 15.8 %copy-start.58 = (bf16[256,896]{1,0:T(8,128)(2,1)S(1)}, bf16[256,896]{1,0:T(8,128)(2,1)}, u32[]{:S(2)}) copy-start(bf16[256,896]{1,0:T(8,128)(2,1)} %get-tuple-element.204) | copy-start | bytes 1376260
  28.5 15.9 %collective-permute-start.9 = (bf16[192,1024]{1,0:T(8,128)(2,1)S(1)}, bf16[192,1024]{1,0:T(8,128)(2,1)S(1)}, u32[]{:S(2)}, u32[]{:S(2)}) collective-permute-start(bf16[192,1024]{1,0:T(8,128)(2,1)S(1)} %pad_maximum_fusion.10), channel_id=1, source_target_pairs={{0,8},{4,12},{8,0},{12,4},{16,24},{20,28},{24,16},{28,20},{1,9},{5... | collective-permute-start | bytes 1179656 | tf_op jit(solution)/shard_map/ppermute | solution.py:652
  31.9 8.8 %collective-permute-start.10 = (bf16[96,768]{1,0:T(8,128)(2,1)S(1)}, bf16[96,768]{1,0:T(8,128)(2,1)S(1)}, u32[]{:S(2)}, u32[]{:S(2)}) collective-permute-start(bf16[96,768]{1,0:T(8,128)(2,1)S(1)} %convert_bitcast_fusion), channel_id=1, source_target_pairs={{0,16},{4,20},{8,24},{12,28},{16,0},{20,4},{24,8},{28,12},{1,17},{... | collective-permute-start | bytes 442376 | tf_op jit(solution)/shard_map/ppermute | solution.py:652
  35.4 8.6 %collective-permute-start.3 = (bf16[128,896]{1,0:T(8,128)(2,1)S(1)}, bf16[128,896]{1,0:T(8,128)(2,1)S(1)}, u32[]{:S(2)}, u32[]{:S(2)}) collective-permute-start(bf16[128,896]{1,0:T(8,128)(2,1)S(1)} %pad_maximum_fusion.12), channel_id=1, source_target_pairs={{0,2},{1,3},{2,0},{3,1},{4,6},{5,7},{6,4},{7,5},{8,10},{9,11},{10,... | collective-permute-start | bytes 688136 | tf_op jit(solution)/shard_map/ppermute | solution.py:652
  37.0 24.9 %collective-permute-start.7 = (bf16[384,640]{1,0:T(8,128)(2,1)S(1)}, bf16[384,640]{1,0:T(8,128)(2,1)S(1)}, u32[]{:S(2)}, u32[]{:S(2)}) collective-permute-start(bf16[384,640]{1,0:T(8,128)(2,1)S(1)} %pad_maximum_fusion.9), channel_id=1, source_target_pairs={{0,4},{4,0},{8,12},{12,8},{16,20},{20,16},{24,28},{28,24},{1,5},{5... | collective-permute-start | bytes 1474568 | tf_op jit(solution)/shard_map/ppermute | solution.py:652
  40.8 19.0 %collective-permute-start.11 = (bf16[192,768]{1,0:T(8,128)(2,1)S(1)}, bf16[192,768]{1,0:T(8,128)(2,1)S(1)}, u32[]{:S(2)}, u32[]{:S(2)}) collective-permute-start(bf16[192,768]{1,0:T(8,128)(2,1)S(1)} %constant_dynamic-update-slice_fusion.11), channel_id=1, source_target_pairs={{0,4},{4,0},{8,12},{12,8},{16,20},{20,16},{24,28},{28,24},{1,5},{5... | collective-permute-start | bytes 884744 | tf_op jit(solution)/shard_map/ppermute | solution.py:652
  42.5 17.3 %collective-permute-start.12 = (bf16[192,768]{1,0:T(8,128)(2,1)S(1)}, bf16[192,768]{1,0:T(8,128)(2,1)S(1)}, u32[]{:S(2)}, u32[]{:S(2)}) collective-permute-start(bf16[192,768]{1,0:T(8,128)(2,1)S(1)} %constant_dynamic-update-slice_fusion.11), channel_id=1, source_target_pairs={{0,2},{1,3},{2,0},{3,1},{4,6},{5,7},{6,4},{7,5},{8,10},{9,11},{10,... | collective-permute-start | bytes 884744 | tf_op jit(solution)/shard_map/ppermute | solution.py:652
  44.0 17.3 %collective-permute-start.13 = (bf16[192,768]{1,0:T(8,128)(2,1)S(1)}, bf16[192,768]{1,0:T(8,128)(2,1)S(1)}, u32[]{:S(2)}, u32[]{:S(2)}) collective-permute-start(bf16[192,768]{1,0:T(8,128)(2,1)S(1)} %constant_dynamic-update-slice_fusion.11), channel_id=1, source_target_pairs={{0,6},{1,7},{2,4},{3,5},{4,2},{5,3},{6,0},{7,1},{8,14},{9,15},{10,... | collective-permute-start | bytes 884744 | tf_op jit(solution)/shard_map/ppermute | solution.py:663
  44.4 18.8 %copy-start.29 = (bf16[512,896]{1,0:T(8,128)(2,1)}, bf16[512,896]{1,0:T(8,128)(2,1)S(1)}, u32[]{:S(2)}) copy-start(bf16[512,896]{1,0:T(8,128)(2,1)S(1)} %get-tuple-element.198) | copy-start | bytes 2752516
  44.5 20.4 %collective-permute-start.4 = (bf16[256,896]{1,0:T(8,128)(2,1)S(1)}, bf16[256,896]{1,0:T(8,128)(2,1)S(1)}, u32[]{:S(2)}, u32[]{:S(2)}) collective-permute-start(bf16[256,896]{1,0:T(8,128)(2,1)S(1)} %get-tuple-element.197), channel_id=1, source_target_pairs={{0,1},{1,0},{2,3},{3,2},{4,5},{5,4},{6,7},{7,6},{8,9},{9,8},{10,11... | collective-permute-start | bytes 1376264 | tf_op jit(solution)/shard_map/ppermute | solution.py:652
  59.8 17.2 %collective-permute-start.14 = (bf16[384,1024]{1,0:T(8,128)(2,1)}, bf16[384,1024]{1,0:T(8,128)(2,1)}, u32[]{:S(2)}, u32[]{:S(2)}) collective-permute-start(bf16[384,1024]{1,0:T(8,128)(2,1)} %pad_maximum_fusion.7.refs_0_.refs_4_), channel_id=1, source_target_pairs={{0,1},{1,0},{2,3},{3,2},{4,5},{5,4},{6,7},{7,6},{8,9},{9,8},{10,11... | collective-permute-start | bytes 2359304 | tf_op jit(solution)/shard_map/ppermute | solution.py:652
  59.8 56.7 %collective-permute-start.19 = (bf16[384,1024]{1,0:T(8,128)(2,1)}, bf16[384,1024]{1,0:T(8,128)(2,1)}, u32[]{:S(2)}, u32[]{:S(2)}) collective-permute-start(bf16[384,1024]{1,0:T(8,128)(2,1)} %pad_maximum_fusion.7.refs_0_.refs_4_), channel_id=1, source_target_pairs={{0,4},{4,0},{8,12},{12,8},{16,20},{20,16},{24,28},{28,24},{1,5},{5... | collective-permute-start | bytes 2359304 | tf_op jit(solution)/shard_map/ppermute | solution.py:652
  61.3 56.1 %collective-permute-start.20 = (bf16[384,1024]{1,0:T(8,128)(2,1)}, bf16[384,1024]{1,0:T(8,128)(2,1)}, u32[]{:S(2)}, u32[]{:S(2)}) collective-permute-start(bf16[384,1024]{1,0:T(8,128)(2,1)} %pad_maximum_fusion.7.refs_0_.refs_4_), channel_id=1, source_target_pairs={{0,2},{1,3},{2,0},{3,1},{4,6},{5,7},{6,4},{7,5},{8,10},{9,11},{10,... | collective-permute-start | bytes 2359304 | tf_op jit(solution)/shard_map/ppermute | solution.py:652
  61.8 56.5 %collective-permute-start.21 = (bf16[384,1024]{1,0:T(8,128)(2,1)}, bf16[384,1024]{1,0:T(8,128)(2,1)}, u32[]{:S(2)}, u32[]{:S(2)}) collective-permute-start(bf16[384,1024]{1,0:T(8,128)(2,1)} %pad_maximum_fusion.7.refs_0_.refs_4_), channel_id=1, source_target_pairs={{0,6},{1,7},{2,4},{3,5},{4,2},{5,3},{6,0},{7,1},{8,14},{9,15},{10,... | collective-permute-start | bytes 2359304 | tf_op jit(solution)/shard_map/ppermute | solution.py:663
  63.4 14.9 %copy-start.5 = (bf16[4,192,768]{2,1,0:T(8,128)(2,1)}, bf16[4,192,768]{2,1,0:T(8,128)(2,1)S(1)}, u32[]{:S(2)}) copy-start(bf16[4,192,768]{2,1,0:T(8,128)(2,1)S(1)} %pad_maximum_fusion.refs_1_.refs_12_) | copy-start | bytes 3538948
  64.9 51.4 %collective-permute-start.15 = (bf16[4,192,768]{2,1,0:T(8,128)(2,1)S(1)}, bf16[4,192,768]{2,1,0:T(8,128)(2,1)}, u32[]{:S(2)}, u32[]{:S(2)}) collective-permute-start(bf16[4,192,768]{2,1,0:T(8,128)(2,1)S(1)} %pad_maximum_fusion.refs_1_.refs_12_), channel_id=1, source_target_pairs={{0,1},{1,0},{2,3},{3,2},{4,5},{5,4},{6,7},{7,6},{8,9},{9,8},{10,11... | collective-permute-start | bytes 3538952 | tf_op jit(solution)/shard_map/ppermute | solution.py:652
  77.0 39.3 %copy-start.18 = (bf16[1024,576]{1,0:T(8,128)(2,1)}, bf16[1024,576]{1,0:T(8,128)(2,1)S(1)}, u32[]{:S(2)}) copy-start(bf16[1024,576]{1,0:T(8,128)(2,1)S(1)} %fusion.10.qkv_ref) | copy-start | bytes 3538948
  77.0 41.3 %collective-permute-start.22 = (bf16[4,192,768]{2,1,0:T(8,128)(2,1)S(1)}, bf16[4,192,768]{2,1,0:T(8,128)(2,1)}, u32[]{:S(2)}, u32[]{:S(2)}) collective-permute-start(bf16[4,192,768]{2,1,0:T(8,128)(2,1)S(1)} %pad_maximum_fusion.refs_1_.refs_12_), channel_id=1, source_target_pairs={{0,8},{4,12},{8,0},{12,4},{16,24},{20,28},{24,16},{28,20},{1,9},{5... | collective-permute-start | bytes 3538952 | tf_op jit(solution)/shard_map/ppermute | solution.py:652
  116.3 2.0 collective-permute-start.16
  116.5 6.3 %collective-permute-start.17 = (bf16[256,192]{1,0:T(8,128)(2,1)S(1)}, bf16[256,192]{1,0:T(8,128)(2,1)S(1)}, u32[]{:S(2)}, u32[]{:S(2)}) collective-permute-start(bf16[256,192]{1,0:T(8,128)(2,1)S(1)} %get-tuple-element.191), channel_id=1, source_target_pairs={{0,2},{1,3},{2,0},{3,1},{4,6},{5,7},{6,4},{7,5},{8,10},{9,11},{10,... | collective-permute-start | bytes 294920 | tf_op jit(solution)/shard_map/ppermute | solution.py:652
  117.4 7.3 %collective-permute-start.18 = (bf16[256,192]{1,0:T(8,128)(2,1)S(1)}, bf16[256,192]{1,0:T(8,128)(2,1)S(1)}, u32[]{:S(2)}, u32[]{:S(2)}) collective-permute-start(bf16[256,192]{1,0:T(8,128)(2,1)S(1)} %get-tuple-element.190), channel_id=1, source_target_pairs={{0,3},{1,2},{2,1},{3,0},{4,7},{5,6},{6,5},{7,4},{8,11},{9,10},{10,... | collective-permute-start | bytes 294920 | tf_op jit(solution)/shard_map/ppermute | solution.py:652
  124.7 6.7 %collective-permute-start.26 = (bf16[4,192,768]{2,1,0:T(8,128)(2,1)}, bf16[4,192,768]{2,1,0:T(8,128)(2,1)}, u32[]{:S(2)}, u32[]{:S(2)}) collective-permute-start(bf16[4,192,768]{2,1,0:T(8,128)(2,1)} %collective-permute-done.22.refs_13_), channel_id=1, source_target_pairs={{0,1},{1,0},{2,3},{3,2},{4,5},{5,4},{6,7},{7,6},{8,9},{9,8},{10,11... | collective-permute-start | bytes 3538952 | tf_op jit(solution)/shard_map/ppermute | solution.py:652
  126.5 3.7 %collective-permute-start.23 = (bf16[384,1024]{1,0:T(8,128)(2,1)}, bf16[384,1024]{1,0:T(8,128)(2,1)S(1)}, u32[]{:S(2)}, u32[]{:S(2)}) collective-permute-start(bf16[384,1024]{1,0:T(8,128)(2,1)} %collective-permute-done.19.refs_5_), channel_id=1, source_target_pairs={{0,1},{1,0},{2,3},{3,2},{4,5},{5,4},{6,7},{7,6},{8,9},{9,8},{10,11... | collective-permute-start | bytes 2359304 | tf_op jit(solution)/shard_map/ppermute | solution.py:652
  126.8 3.5 %collective-permute-start.24 = (bf16[384,1024]{1,0:T(8,128)(2,1)}, bf16[384,1024]{1,0:T(8,128)(2,1)S(1)}, u32[]{:S(2)}, u32[]{:S(2)}) collective-permute-start(bf16[384,1024]{1,0:T(8,128)(2,1)} %collective-permute-done.20.refs_6_), channel_id=1, source_target_pairs={{0,1},{1,0},{2,3},{3,2},{4,5},{5,4},{6,7},{7,6},{8,9},{9,8},{10,11... | collective-permute-start | bytes 2359304 | tf_op jit(solution)/shard_map/ppermute | solution.py:652
  127.1 4.2 %collective-permute-start.25 = (bf16[384,1024]{1,0:T(8,128)(2,1)}, bf16[384,1024]{1,0:T(8,128)(2,1)S(1)}, u32[]{:S(2)}, u32[]{:S(2)}) collective-permute-start(bf16[384,1024]{1,0:T(8,128)(2,1)} %collective-permute-done.21.refs_7_), channel_id=1, source_target_pairs={{0,1},{1,0},{2,3},{3,2},{4,5},{5,4},{6,7},{7,6},{8,9},{9,8},{10,11... | collective-permute-start | bytes 2359304 | tf_op jit(solution)/shard_map/ppermute | solution.py:652
  132.2 23.8 %copy-start.44 = (f32[192,96]{1,0:T(8,128)S(1)}, f32[192,96]{1,0:T(8,128)}, u32[]{:S(2)}) copy-start(f32[192,96]{1,0:T(8,128)} %param.33) | copy-start | bytes 221188
  132.2 24.5 %copy-start.45 = (f32[192,96]{1,0:T(8,128)S(1)}, f32[192,96]{1,0:T(8,128)}, u32[]{:S(2)}) copy-start(f32[192,96]{1,0:T(8,128)} %param.34) | copy-start | bytes 221188
  153.6 9.6 %collective-permute-start.30 = (bf16[2,768,1024]{2,1,0:T(8,128)(2,1)}, bf16[2,768,1024]{2,1,0:T(8,128)(2,1)}, u32[]{:S(2)}, u32[]{:S(2)}) collective-permute-start(bf16[2,768,1024]{2,1,0:T(8,128)(2,1)} %get-tuple-element.80), channel_id=1, source_target_pairs={{0,1},{1,0},{2,3},{3,2},{4,5},{5,4},{6,7},{7,6},{8,9},{9,8},{10,11... | collective-permute-start | bytes 9437192 | tf_op jit(solution)/shard_map/ppermute | solution.py:652
  153.9 9.3 %collective-permute-start.31 = (bf16[2,768,768]{2,1,0:T(8,128)(2,1)}, bf16[2,768,768]{2,1,0:T(8,128)(2,1)}, u32[]{:S(2)}, u32[]{:S(2)}) collective-permute-start(bf16[2,768,768]{2,1,0:T(8,128)(2,1)} %get-tuple-element.81), channel_id=1, source_target_pairs={{0,1},{1,0},{2,3},{3,2},{4,5},{5,4},{6,7},{7,6},{8,9},{9,8},{10,11... | collective-permute-start | bytes 7077896 | tf_op jit(solution)/shard_map/ppermute | solution.py:652
  154.2 5.5 %collective-permute-start.27 = (bf16[256,192]{1,0:T(8,128)(2,1)S(1)}, bf16[256,192]{1,0:T(8,128)(2,1)S(1)}, u32[]{:S(2)}, u32[]{:S(2)}) collective-permute-start(bf16[256,192]{1,0:T(8,128)(2,1)S(1)} %get-tuple-element.76), channel_id=1, source_target_pairs={{0,1},{1,0},{2,3},{3,2},{4,5},{5,4},{6,7},{7,6},{8,9},{9,8},{10,11... | collective-permute-start | bytes 294920 | tf_op jit(solution)/shard_map/ppermute | solution.py:652
  154.4 6.3 %collective-permute-start.28 = (bf16[256,192]{1,0:T(8,128)(2,1)S(1)}, bf16[256,192]{1,0:T(8,128)(2,1)S(1)}, u32[]{:S(2)}, u32[]{:S(2)}) collective-permute-start(bf16[256,192]{1,0:T(8,128)(2,1)S(1)} %get-tuple-element.77), channel_id=1, source_target_pairs={{0,2},{1,3},{2,0},{3,1},{4,6},{5,7},{6,4},{7,5},{8,10},{9,11},{10,... | collective-permute-start | bytes 294920 | tf_op jit(solution)/shard_map/ppermute | solution.py:652
  155.3 6.9 %collective-permute-start.29 = (bf16[256,192]{1,0:T(8,128)(2,1)S(1)}, bf16[256,192]{1,0:T(8,128)(2,1)S(1)}, u32[]{:S(2)}, u32[]{:S(2)}) collective-permute-start(bf16[256,192]{1,0:T(8,128)(2,1)S(1)} %get-tuple-element.78), channel_id=1, source_target_pairs={{0,3},{1,2},{2,1},{3,0},{4,7},{5,6},{6,5},{7,4},{8,11},{9,10},{10,... | collective-permute-start | bytes 294920 | tf_op jit(solution)/shard_map/ppermute | solution.py:652
  165.3 42.1 %collective-permute-start.35 = (bf16[2,2,192,768]{3,2,1,0:T(8,128)(2,1)S(1)}, bf16[2,2,192,768]{3,2,1,0:T(8,128)(2,1)S(1)}, u32[]{:S(2)}, u32[]{:S(2)}) collective-permute-start(bf16[2,2,192,768]{3,2,1,0:T(8,128)(2,1)S(1)} %fusion.13.refs_3_), channel_id=1, source_target_pairs={{0,8},{4,12},{8,0},{12,4},{16,24},{20,28},{24,16},{28,20},{1,9},{5... | collective-permute-start | bytes 3538952 | tf_op jit(solution)/shard_map/ppermute | solution.py:652
  169.7 34.6 %collective-permute-start.32 = (bf16[384,1024]{1,0:T(8,128)(2,1)S(1)}, bf16[384,1024]{1,0:T(8,128)(2,1)S(1)}, u32[]{:S(2)}, u32[]{:S(2)}) collective-permute-start(bf16[384,1024]{1,0:T(8,128)(2,1)S(1)} %get-tuple-element.186.refs_0_), channel_id=1, source_target_pairs={{0,4},{4,0},{8,12},{12,8},{16,20},{20,16},{24,28},{28,24},{1,5},{5... | collective-permute-start | bytes 2359304 | tf_op jit(solution)/shard_map/ppermute | solution.py:652
  171.2 33.1 %collective-permute-start.33 = (bf16[384,1024]{1,0:T(8,128)(2,1)}, bf16[384,1024]{1,0:T(8,128)(2,1)S(1)}, u32[]{:S(2)}, u32[]{:S(2)}) collective-permute-start(bf16[384,1024]{1,0:T(8,128)(2,1)} %get-tuple-element.185.refs_1_), channel_id=1, source_target_pairs={{0,2},{1,3},{2,0},{3,1},{4,6},{5,7},{6,4},{7,5},{8,10},{9,11},{10,... | collective-permute-start | bytes 2359304 | tf_op jit(solution)/shard_map/ppermute | solution.py:652
  171.7 35.6 %collective-permute-start.34 = (bf16[384,1024]{1,0:T(8,128)(2,1)S(1)}, bf16[384,1024]{1,0:T(8,128)(2,1)S(1)}, u32[]{:S(2)}, u32[]{:S(2)}) collective-permute-start(bf16[384,1024]{1,0:T(8,128)(2,1)S(1)} %get-tuple-element.184.refs_2_), channel_id=1, source_target_pairs={{0,6},{1,7},{2,4},{3,5},{4,2},{5,3},{6,0},{7,1},{8,14},{9,15},{10,... | collective-permute-start | bytes 2359304 | tf_op jit(solution)/shard_map/ppermute | solution.py:663
  210.4 23.5 %collective-permute-start.43 = (bf16[192,768]{1,0:T(8,128)(2,1)S(1)}, bf16[192,768]{1,0:T(8,128)(2,1)}, u32[]{:S(2)}, u32[]{:S(2)}) collective-permute-start(bf16[192,768]{1,0:T(8,128)(2,1)S(1)} %get-tuple-element.189.refs_1_), channel_id=1, source_target_pairs={{0,4},{4,0},{8,12},{12,8},{16,20},{20,16},{24,28},{28,24},{1,5},{5... | collective-permute-start | bytes 884744 | tf_op jit(solution)/shard_map/ppermute | solution.py:652
  212.0 23.5 %collective-permute-start.44 = (bf16[192,768]{1,0:T(8,128)(2,1)S(1)}, bf16[192,768]{1,0:T(8,128)(2,1)}, u32[]{:S(2)}, u32[]{:S(2)}) collective-permute-start(bf16[192,768]{1,0:T(8,128)(2,1)S(1)} %get-tuple-element.188.refs_2_), channel_id=1, source_target_pairs={{0,2},{1,3},{2,0},{3,1},{4,6},{5,7},{6,4},{7,5},{8,10},{9,11},{10,... | collective-permute-start | bytes 884744 | tf_op jit(solution)/shard_map/ppermute | solution.py:652
  212.5 23.2 %collective-permute-start.45 = (bf16[192,768]{1,0:T(8,128)(2,1)S(1)}, bf16[192,768]{1,0:T(8,128)(2,1)}, u32[]{:S(2)}, u32[]{:S(2)}) collective-permute-start(bf16[192,768]{1,0:T(8,128)(2,1)S(1)} %get-tuple-element.187.refs_3_), channel_id=1, source_target_pairs={{0,6},{1,7},{2,4},{3,5},{4,2},{5,3},{6,0},{7,1},{8,14},{9,15},{10,... | collective-permute-start | bytes 884744 | tf_op jit(solution)/shard_map/ppermute | solution.py:663
  216.2 10.4 %copy-start.55 = (s32[32]{0:T(128)S(1)}, s32[32]{0:T(128)}, u32[]{:S(2)}) copy-start(s32[32]{0:T(128)} %copy-done.54) | copy-start | bytes 388
  227.6 11.6 %collective-permute-start.41 = (bf16[192,1024]{1,0:T(8,128)(2,1)}, bf16[192,1024]{1,0:T(8,128)(2,1)}, u32[]{:S(2)}, u32[]{:S(2)}) collective-permute-start(bf16[192,1024]{1,0:T(8,128)(2,1)} %slice.383), channel_id=1, source_target_pairs={{0,8},{4,12},{8,0},{12,4},{16,24},{20,28},{24,16},{28,20},{1,9},{5... | collective-permute-start | bytes 1179656 | tf_op jit(solution)/shard_map/ppermute | solution.py:652
  233.0 8.7 %collective-permute-start.47 = (bf16[256,896]{1,0:T(8,128)(2,1)S(1)}, bf16[256,896]{1,0:T(8,128)(2,1)S(1)}, u32[]{:S(2)}, u32[]{:S(2)}) collective-permute-start(bf16[256,896]{1,0:T(8,128)(2,1)S(1)} %slice.391), channel_id=1, source_target_pairs={{0,1},{1,0},{2,3},{3,2},{4,5},{5,4},{6,7},{7,6},{8,9},{9,8},{10,11... | collective-permute-start | bytes 1376264 | tf_op jit(solution)/shard_map/ppermute | solution.py:652
  234.0 13.7 %collective-permute-start.38 = (bf16[384,640]{1,0:T(8,128)(2,1)S(1)}, bf16[384,640]{1,0:T(8,128)(2,1)S(1)}, u32[]{:S(2)}, u32[]{:S(2)}) collective-permute-start(bf16[384,640]{1,0:T(8,128)(2,1)S(1)} %copy-done.16), channel_id=1, source_target_pairs={{0,4},{4,0},{8,12},{12,8},{16,20},{20,16},{24,28},{28,24},{1,5},{5... | collective-permute-start | bytes 1474568 | tf_op jit(solution)/shard_map/ppermute | solution.py:652
  235.6 30.7 %collective-permute-start.36 = (bf16[2,256,768]{2,1,0:T(8,128)(2,1)}, bf16[2,256,768]{2,1,0:T(8,128)(2,1)}, u32[]{:S(2)}, u32[]{:S(2)}) collective-permute-start(bf16[2,256,768]{2,1,0:T(8,128)(2,1)} %slice.312), channel_id=1, source_target_pairs={{0,1},{1,0},{2,3},{3,2},{4,5},{5,4},{6,7},{7,6},{8,9},{9,8},{10,11... | collective-permute-start | bytes 2359304 | tf_op jit(solution)/shard_map/ppermute | solution.py:652
  237.4 14.8 %collective-permute-start.46 = (bf16[96,768]{1,0:T(8,128)(2,1)S(1)}, bf16[96,768]{1,0:T(8,128)(2,1)S(1)}, u32[]{:S(2)}, u32[]{:S(2)}) collective-permute-start(bf16[96,768]{1,0:T(8,128)(2,1)S(1)} %slice.388), channel_id=1, source_target_pairs={{0,16},{4,20},{8,24},{12,28},{16,0},{20,4},{24,8},{28,12},{1,17},{... | collective-permute-start | bytes 442376 | tf_op jit(solution)/shard_map/ppermute | solution.py:652
  240.3 15.8 %collective-permute-start.42 = (bf16[96,1024]{1,0:T(8,128)(2,1)S(1)}, bf16[96,1024]{1,0:T(8,128)(2,1)S(1)}, u32[]{:S(2)}, u32[]{:S(2)}) collective-permute-start(bf16[96,1024]{1,0:T(8,128)(2,1)S(1)} %slice.385), channel_id=1, source_target_pairs={{0,16},{4,20},{8,24},{12,28},{16,0},{20,4},{24,8},{28,12},{1,17},{... | collective-permute-start | bytes 589832 | tf_op jit(solution)/shard_map/ppermute | solution.py:652
  241.8 7.5 %collective-permute-start.48 = (bf16[128,896]{1,0:T(8,128)(2,1)S(1)}, bf16[128,896]{1,0:T(8,128)(2,1)S(1)}, u32[]{:S(2)}, u32[]{:S(2)}) collective-permute-start(bf16[128,896]{1,0:T(8,128)(2,1)S(1)} %slice.393), channel_id=1, source_target_pairs={{0,2},{1,3},{2,0},{3,1},{4,6},{5,7},{6,4},{7,5},{8,10},{9,11},{10,... | collective-permute-start | bytes 688136 | tf_op jit(solution)/shard_map/ppermute | solution.py:652
  248.5 13.1 %collective-permute-start.39 = (bf16[192,640]{1,0:T(8,128)(2,1)}, bf16[192,640]{1,0:T(8,128)(2,1)}, u32[]{:S(2)}, u32[]{:S(2)}) collective-permute-start(bf16[192,640]{1,0:T(8,128)(2,1)} %slice.376), channel_id=1, source_target_pairs={{0,8},{4,12},{8,0},{12,4},{16,24},{20,28},{24,16},{28,20},{1,9},{5... | collective-permute-start | bytes 737288 | tf_op jit(solution)/shard_map/ppermute | solution.py:652
  250.0 12.7 %collective-permute-start.49 = (bf16[64,896]{1,0:T(8,128)(2,1)}, bf16[64,896]{1,0:T(8,128)(2,1)}, u32[]{:S(2)}, u32[]{:S(2)}) collective-permute-start(bf16[64,896]{1,0:T(8,128)(2,1)} %slice.398), channel_id=1, source_target_pairs={{0,4},{4,0},{8,12},{12,8},{16,20},{20,16},{24,28},{28,24},{1,5},{5... | collective-permute-start | bytes 344072 | tf_op jit(solution)/shard_map/ppermute | solution.py:652
  262.6 8.8 %collective-permute-start.40 = (bf16[96,640]{1,0:T(8,128)(2,1)S(1)}, bf16[96,640]{1,0:T(8,128)(2,1)S(1)}, u32[]{:S(2)}, u32[]{:S(2)}) collective-permute-start(bf16[96,640]{1,0:T(8,128)(2,1)S(1)} %slice.378), channel_id=1, source_target_pairs={{0,16},{4,20},{8,24},{12,28},{16,0},{20,4},{24,8},{28,12},{1,17},{... | collective-permute-start | bytes 368648 | tf_op jit(solution)/shard_map/ppermute | solution.py:652
  263.7 7.6 %collective-permute-start.50 = (bf16[32,896]{1,0:T(8,128)(2,1)S(1)}, bf16[32,896]{1,0:T(8,128)(2,1)S(1)}, u32[]{:S(2)}, u32[]{:S(2)}) collective-permute-start(bf16[32,896]{1,0:T(8,128)(2,1)S(1)} %slice.400), channel_id=1, source_target_pairs={{0,8},{4,12},{8,0},{12,4},{16,24},{20,28},{24,16},{28,20},{1,9},{5... | collective-permute-start | bytes 172040 | tf_op jit(solution)/shard_map/ppermute | solution.py:652
  267.7 10.3 %collective-permute-start.37 = (bf16[1,256,768]{2,1,0:T(8,128)(2,1)S(1)}, bf16[1,256,768]{2,1,0:T(8,128)(2,1)S(1)}, u32[]{:S(2)}, u32[]{:S(2)}) collective-permute-start(bf16[1,256,768]{2,1,0:T(8,128)(2,1)S(1)} %slice.374), channel_id=1, source_target_pairs={{0,2},{1,3},{2,0},{3,1},{4,6},{5,7},{6,4},{7,5},{8,10},{9,11},{10,... | collective-permute-start | bytes 1179656 | tf_op jit(solution)/shard_map/ppermute | solution.py:652
  271.4 4.8 %collective-permute-start.51 = (bf16[16,896]{1,0:T(8,128)(2,1)S(1)}, bf16[16,896]{1,0:T(8,128)(2,1)S(1)}, u32[]{:S(2)}, u32[]{:S(2)}) collective-permute-start(bf16[16,896]{1,0:T(8,128)(2,1)S(1)} %slice.402), channel_id=1, source_target_pairs={{0,16},{4,20},{8,24},{12,28},{16,0},{20,4},{24,8},{28,12},{1,17},{... | collective-permute-start | bytes 86024 | tf_op jit(solution)/shard_map/ppermute | solution.py:652
  (54 other events, 246.1 us)
